TPU v7x, 32 devices: a whole 2x2x4 slice. The times are simulated.
32 devices in a mesh: rows: 16 (over z, x, core), cols: 2 (over y).
Axes of the slice: x: 2, y: 2, z: 4, core: 2. Of those that a mesh axis runs over, the one named last changes fastest.
Arguments:
- right_side: float32 [4, 2, 4096, 512], P(None, 'cols', 'rows'), may hold values from -6 to 6
- inverse_blocks: bfloat16 [4, 2, 4096, 8192], P(None, None, 'rows', 'cols'), may hold values from -0.09375 to 0.09375
- lower_blocks: bfloat16 [6, 2, 4096, 8192], P(None, None, 'rows', 'cols'), may hold values from -0.046875 to 0.046875
Outputs:
- solution: float32 [4, 2, 4096, 512], P(None, 'cols', 'rows')
All inputs are finite; a program needn't handle non-finite values.
Results may differ from a plain program's by a relative error of at most 0.014.
Values may be sent and summed in bfloat16 or wider, within the bound.
No kernel may reach another device: no remote copies, remote signals or barrier semaphores. Data moves between devices by JAX's collectives and lax.ppermute only.
A program may use at most 128 MiB of HBM per device.

v0:
```python
import jax
import jax.numpy as jnp
from jax import lax
from jax.sharding import PartitionSpec as P


def pair_index(target, source):
    return target * (target - 1) // 2 + source


def product(factor_block, rows_all):
    return jnp.einsum("abk,kn->abn", factor_block, rows_all, preferred_element_type=jnp.float32)


def fold_rows(factor_block, incoming):
    return jnp.einsum("abk,kn->abn", factor_block, incoming[0], preferred_element_type=jnp.float32)


def forward_solve(right_side, inverse_blocks, lower_blocks):
    panels = right_side.shape[0]
    groups = inverse_blocks.shape[1]
    local_rows = inverse_blocks.shape[2]
    columns = right_side.shape[3]
    gathered = []
    solutions = []
    for current in range(panels):
        if current == 0:
            residual = right_side[0].astype(jnp.bfloat16)
        else:
            partial_value = jnp.zeros((groups, local_rows, columns), jnp.float32)
            for source in range(current):
                partial_value = partial_value + product(
                    lower_blocks[pair_index(current, source)], gathered[source]
                )
            shares = lax.psum_scatter(partial_value, "cols", scatter_dimension=0, tiled=True)
            residual = (right_side[current] - shares).astype(jnp.bfloat16)
        products = fold_rows(
            inverse_blocks[current], lax.all_gather(residual, "rows", axis=1, tiled=True)
        )
        solved = lax.psum_scatter(products, "cols", scatter_dimension=0, tiled=True)
        solutions.append(solved)
        if current + 1 < panels:
            rows_all = lax.all_gather(solved.astype(jnp.bfloat16), "rows", axis=1, tiled=True)[0]
            gathered.append(rows_all)
    return jnp.stack(solutions)


def body(right_side, inverse_blocks, lower_blocks):
    return forward_solve(right_side, inverse_blocks, lower_blocks)


def solution(mesh):
    return jax.shard_map(
        body,
        mesh=mesh,
        in_specs=(
            P(None, "cols", "rows", None),
            P(None, None, "rows", "cols"),
            P(None, None, "rows", "cols"),
        ),
        out_specs=P(None, "cols", "rows", None),
        check_vma=False,
    )
```

profile of v0, /device:TPU:0, one launch (start us, length us, event | category | flops | bytes accessed | tf_op | source)
XLA Modules:
  0.0 586.1 jit_solution(14107384204727382122)
XLA Ops:
  6.5 1.8 slice.117
  8.3 0.0 all-gather.21.cloned.1.call-update
  8.3 0.0 reduce-scatter.8.cloned.1.call-start
  8.4 54.4 %all-gather.21.cloned.1.call-done = bf16[1,1,4096,512]{3,2,1,0:T(8,128)(2,1)} async-done(((bf16[1,1,256,512]{3,2,1,0:T(8,128)(2,1)}), bf16[1,1,4096,512]{3,2,1,0:T(8,128)(2,1)}) %all-gather.21.cloned.1.call-update) | async-done | bytes 4194320 | tf_op jit(solution)/shard_map/all_gather | solution.py:38
  62.8 6.8 %fusion.12 = f32[2,256,512]{2,1,0:T(8,128)} fusion(bf16[1,1,4096,512]{3,2,1,0:T(8,128)(2,1)} %all-gather.21.cloned.1.call-done, bf16[4,2,256,4096]{3,2,1,0:T(8,128)(2,1)} %param.4), kind=kOutput, calls=%fused_computation.12 | convolution fusion | flops 2147483648 | bytes 9437184 | tf_op jit(solution)/shard_map/abk,kn->abn/dot_general | solution.py:16
  69.6 0.0 reduce-scatter.8.cloned.1.call-update
  69.6 0.0 all-gather.9.cloned.1.call-start
  69.6 18.9 %reduce-scatter.8.cloned.1.call-done = f32[1,256,512]{2,1,0:T(8,128)} async-done(((f32[2,256,512]{2,1,0:T(8,128)}), f32[1,256,512]{2,1,0:T(8,128)}) %reduce-scatter.8.cloned.1.call-update) | async-done | bytes 524304 | tf_op jit(solution)/shard_map/reduce_scatter | solution.py:40
  88.6 1.8 convert_element_type.31
  90.3 0.0 all-gather.9.cloned.1.call-update
  90.4 0.0 reduce-scatter.10.cloned.1.call-start
  90.4 51.2 %all-gather.9.cloned.1.call-done = bf16[1,4096,512]{2,1,0:T(8,128)(2,1)} async-done(((bf16[1,256,512]{2,1,0:T(8,128)(2,1)}), bf16[1,4096,512]{2,1,0:T(8,128)(2,1)}) %all-gather.9.cloned.1.call-update) | async-done | bytes 4194320 | tf_op jit(solution)/shard_map/all_gather | solution.py:43
  141.6 6.8 %fusion.55 = f32[2,256,512]{1,2,0:T(8,128)} fusion(bf16[6,2,256,4096]{3,2,1,0:T(8,128)(2,1)} %param.5, bf16[1,4096,512]{2,1,0:T(8,128)(2,1)} %all-gather.9.cloned.1.call-done), kind=kOutput, calls=%fused_computation.44 | convolution fusion | flops 2147483648 | bytes 9437184 | tf_op jit(solution)/shard_map/abk,kn->abn/dot_general | solution.py:12
  148.4 0.0 reduce-scatter.10.cloned.1.call-update
  148.4 0.0 all-gather.11.cloned.1.call-start
  148.5 1.5 fusion.88
  149.9 0.2 copy.31
  150.1 17.2 %reduce-scatter.10.cloned.1.call-done = f32[1,256,512]{1,2,0:T(8,128)} async-done(((f32[2,256,512]{1,2,0:T(8,128)}), f32[1,256,512]{1,2,0:T(8,128)}) %reduce-scatter.10.cloned.1.call-update) | async-done | bytes 524304 | tf_op jit(solution)/shard_map/reduce_scatter | solution.py:35
  167.4 1.8 fusion.87
  169.2 0.0 all-gather.11.cloned.1.call-update
  169.2 0.0 reduce-scatter.12.cloned.1.call-start
  169.2 53.4 %all-gather.11.cloned.1.call-done = bf16[1,4096,512]{1,2,0:T(8,128)(2,1)} async-done(((bf16[1,256,512]{1,2,0:T(8,128)(2,1)}), bf16[1,4096,512]{1,2,0:T(8,128)(2,1)}) %all-gather.11.cloned.1.call-update) | async-done | bytes 4194320 | tf_op jit(solution)/shard_map/all_gather | solution.py:38
  222.6 6.8 %fusion.40 = f32[2,256,512]{2,1,0:T(8,128)} fusion(bf16[4,2,256,4096]{3,2,1,0:T(8,128)(2,1)} %param.4, bf16[1,4096,512]{1,2,0:T(8,128)(2,1)} %all-gather.11.cloned.1.call-done), kind=kOutput, calls=%fused_computation.41 | convolution fusion | flops 2147483648 | bytes 9437184 | tf_op jit(solution)/shard_map/abk,kn->abn/dot_general | solution.py:16
  229.4 0.0 reduce-scatter.12.cloned.1.call-update
  229.4 0.0 all-gather.13.cloned.1.call-start
  229.5 18.6 %reduce-scatter.12.cloned.1.call-done = f32[1,256,512]{2,1,0:T(8,128)} async-done(((f32[2,256,512]{2,1,0:T(8,128)}), f32[1,256,512]{2,1,0:T(8,128)}) %reduce-scatter.12.cloned.1.call-update) | async-done | bytes 524304 | tf_op jit(solution)/shard_map/reduce_scatter | solution.py:40
  248.1 1.8 convert_element_type.33
  249.9 0.0 all-gather.13.cloned.1.call-update
  249.9 0.0 reduce-scatter.14.cloned.1.call-start
  250.0 51.1 %all-gather.13.cloned.1.call-done = bf16[1,4096,512]{2,1,0:T(8,128)(2,1)} async-done(((bf16[1,256,512]{2,1,0:T(8,128)(2,1)}), bf16[1,4096,512]{2,1,0:T(8,128)(2,1)}) %all-gather.13.cloned.1.call-update) | async-done | bytes 4194320 | tf_op jit(solution)/shard_map/all_gather | solution.py:43
  301.1 6.0 %fusion.4 = f32[512,2,256]{2,0,1:T(8,128)S(1)} fusion(bf16[1,4096,512]{2,1,0:T(8,128)(2,1)} %all-gather.13.cloned.1.call-done, bf16[6,2,256,4096]{3,2,1,0:T(8,128)(2,1)} %param.5), kind=kOutput, calls=%fused_computation.4 | convolution fusion | flops 2147483648 | bytes 9437184 | tf_op jit(solution)/shard_map/abk,kn->abn/dot_general | solution.py:12
  307.1 0.0 copy-done.3
  307.1 5.6 fusion.65
  312.7 0.0 reduce-scatter.14.cloned.1.call-update
  312.7 0.2 all-gather.15.cloned.1.call-start
  312.9 0.2 copy.32
  313.1 18.5 %reduce-scatter.14.cloned.1.call-done = f32[1,256,512]{1,2,0:T(8,128)} async-done(((f32[2,256,512]{1,2,0:T(8,128)}), f32[1,256,512]{1,2,0:T(8,128)}) %reduce-scatter.14.cloned.1.call-update) | async-done | bytes 524304 | tf_op jit(solution)/shard_map/reduce_scatter | solution.py:35
  331.6 1.8 fusion.86
  333.4 0.0 all-gather.15.cloned.1.call-update
  333.5 0.0 reduce-scatter.16.cloned.1.call-start
  333.5 53.6 %all-gather.15.cloned.1.call-done = bf16[1,4096,512]{1,2,0:T(8,128)(2,1)} async-done(((bf16[1,256,512]{1,2,0:T(8,128)(2,1)}), bf16[1,4096,512]{1,2,0:T(8,128)(2,1)}) %all-gather.15.cloned.1.call-update) | async-done | bytes 4194320 | tf_op jit(solution)/shard_map/all_gather | solution.py:38
  387.1 6.8 %fusion.45 = f32[2,256,512]{2,1,0:T(8,128)} fusion(bf16[4,2,256,4096]{3,2,1,0:T(8,128)(2,1)} %param.4, bf16[1,4096,512]{1,2,0:T(8,128)(2,1)} %all-gather.15.cloned.1.call-done), kind=kOutput, calls=%fused_computation.42 | convolution fusion | flops 2147483648 | bytes 9437184 | tf_op jit(solution)/shard_map/abk,kn->abn/dot_general | solution.py:16
  393.9 0.0 reduce-scatter.16.cloned.1.call-update
  393.9 0.0 all-gather.17.cloned.1.call-start
  393.9 18.6 %reduce-scatter.16.cloned.1.call-done = f32[1,256,512]{2,1,0:T(8,128)} async-done(((f32[2,256,512]{2,1,0:T(8,128)}), f32[1,256,512]{2,1,0:T(8,128)}) %reduce-scatter.16.cloned.1.call-update) | async-done | bytes 524304 | tf_op jit(solution)/shard_map/reduce_scatter | solution.py:40
  412.5 1.8 convert_element_type.35
  414.3 0.0 all-gather.17.cloned.1.call-update
  414.3 0.0 reduce-scatter.18.cloned.1.call-start
  414.4 5.8 fusion.2
  420.2 45.3 %all-gather.17.cloned.1.call-done = bf16[1,4096,512]{2,1,0:T(8,128)(2,1)} async-done(((bf16[1,256,512]{2,1,0:T(8,128)(2,1)}), bf16[1,4096,512]{2,1,0:T(8,128)(2,1)}) %all-gather.17.cloned.1.call-update) | async-done | bytes 4194320 | tf_op jit(solution)/shard_map/all_gather | solution.py:43
  465.5 6.0 %fusion = f32[512,2,256]{2,0,1:T(8,128)S(1)} fusion(bf16[1,4096,512]{2,1,0:T(8,128)(2,1)} %all-gather.17.cloned.1.call-done, bf16[6,2,256,4096]{3,2,1,0:T(8,128)(2,1)} %param.5), kind=kOutput, calls=%fused_computation | convolution fusion | flops 2147483648 | bytes 9437184 | tf_op jit(solution)/shard_map/abk,kn->abn/dot_general | solution.py:12
  471.5 5.6 fusion.80
  477.1 0.0 reduce-scatter.18.cloned.1.call-update
  477.1 0.0 all-gather.19.cloned.1.call-start
  477.2 0.2 copy.33
  477.4 18.7 %reduce-scatter.18.cloned.1.call-done = f32[1,256,512]{1,2,0:T(8,128)} async-done(((f32[2,256,512]{1,2,0:T(8,128)}), f32[1,256,512]{1,2,0:T(8,128)}) %reduce-scatter.18.cloned.1.call-update) | async-done | bytes 524304 | tf_op jit(solution)/shard_map/reduce_scatter | solution.py:35
  496.1 1.8 fusion.85
  497.9 0.0 all-gather.19.cloned.1.call-update
  497.9 0.0 reduce-scatter.20.cloned.1.call-start
  498.0 53.5 %all-gather.19.cloned.1.call-done = bf16[1,4096,512]{1,2,0:T(8,128)(2,1)} async-done(((bf16[1,256,512]{1,2,0:T(8,128)(2,1)}), bf16[1,4096,512]{1,2,0:T(8,128)(2,1)}) %all-gather.19.cloned.1.call-update) | async-done | bytes 4194320 | tf_op jit(solution)/shard_map/all_gather | solution.py:38
  551.5 6.8 %fusion.50 = f32[2,256,512]{2,1,0:T(8,128)} fusion(bf16[4,2,256,4096]{3,2,1,0:T(8,128)(2,1)} %param.4, bf16[1,4096,512]{1,2,0:T(8,128)(2,1)} %all-gather.19.cloned.1.call-done), kind=kOutput, calls=%fused_computation.43 | convolution fusion | flops 2147483648 | bytes 9437184 | tf_op jit(solution)/shard_map/abk,kn->abn/dot_general | solution.py:16
  558.3 0.0 reduce-scatter.20.cloned.1.call-update
  558.3 18.7 %reduce-scatter.20.cloned.1.call-done = f32[1,256,512]{2,1,0:T(8,128)} async-done(((f32[2,256,512]{2,1,0:T(8,128)}), f32[1,256,512]{2,1,0:T(8,128)}) %reduce-scatter.20.cloned.1.call-update) | async-done | bytes 524304 | tf_op jit(solution)/shard_map/reduce_scatter | solution.py:40
  577.0 2.6 pad_maximum_fusion
  (10 shorter events, 0.0 us)
Async XLA Ops:
  6.5 56.3 %all-gather.21.cloned.1.call-start = ((), (), s32[]{:S(2)}) async-start(), calls=%async_computation.20 | async-start | bytes 4456448 | tf_op jit(solution)/shard_map/all_gather | solution.py:38
  8.3 80.2 %reduce-scatter.8.cloned.1.call-start = ((), (), s32[]{:S(2)}) async-start(), calls=%async_computation.7 | async-start | bytes 1572864 | tf_op jit(solution)/shard_map/reduce_scatter | solution.py:40
  69.6 72.0 %all-gather.9.cloned.1.call-start = ((), (), s32[]{:S(2)}) async-start(), calls=%async_computation.8 | async-start | bytes 4456448 | tf_op jit(solution)/shard_map/all_gather | solution.py:43
  90.4 77.0 %reduce-scatter.10.cloned.1.call-start = ((), (), s32[]{:S(2)}) async-start(), calls=%async_computation.9 | async-start | bytes 1572864 | tf_op jit(solution)/shard_map/reduce_scatter | solution.py:35
  148.4 74.2 %all-gather.11.cloned.1.call-start = ((), (), s32[]{:S(2)}) async-start(), calls=%async_computation.10 | async-start | bytes 4456448 | tf_op jit(solution)/shard_map/all_gather | solution.py:38
  169.2 78.9 %reduce-scatter.12.cloned.1.call-start = ((), (), s32[]{:S(2)}) async-start(), calls=%async_computation.11 | async-start | bytes 1572864 | tf_op jit(solution)/shard_map/reduce_scatter | solution.py:40
  229.4 71.6 %all-gather.13.cloned.1.call-start = ((), (), s32[]{:S(2)}) async-start(), calls=%async_computation.12 | async-start | bytes 4456448 | tf_op jit(solution)/shard_map/all_gather | solution.py:43
  249.9 81.7 %reduce-scatter.14.cloned.1.call-start = ((), (), s32[]{:S(2)}) async-start(), calls=%async_computation.13 | async-start | bytes 1572864 | tf_op jit(solution)/shard_map/reduce_scatter | solution.py:35
  301.1 6.0 %copy-start.3 = (bf16[1,4096,512]{2,1,0:T(8,128)(2,1)S(1)}, bf16[1,4096,512]{2,1,0:T(8,128)(2,1)}, u32[]{:S(2)}) copy-start(bf16[1,4096,512]{2,1,0:T(8,128)(2,1)} %all-gather.9.cloned.1.call-done) | copy-start | bytes 12582916
  312.7 74.4 %all-gather.15.cloned.1.call-start = ((), (), s32[]{:S(2)}) async-start(), calls=%async_computation.14 | async-start | bytes 4456448 | tf_op jit(solution)/shard_map/all_gather | solution.py:38
  333.5 79.1 %reduce-scatter.16.cloned.1.call-start = ((), (), s32[]{:S(2)}) async-start(), calls=%async_computation.15 | async-start | bytes 1572864 | tf_op jit(solution)/shard_map/reduce_scatter | solution.py:40
  393.9 71.6 %all-gather.17.cloned.1.call-start = ((), (), s32[]{:S(2)}) async-start(), calls=%async_computation.16 | async-start | bytes 4456448 | tf_op jit(solution)/shard_map/all_gather | solution.py:43
  414.3 81.7 %reduce-scatter.18.cloned.1.call-start = ((), (), s32[]{:S(2)}) async-start(), calls=%async_computation.17 | async-start | bytes 1572864 | tf_op jit(solution)/shard_map/reduce_scatter | solution.py:35
  465.5 6.0 %copy-start.4 = (bf16[1,4096,512]{2,1,0:T(8,128)(2,1)S(1)}, bf16[1,4096,512]{2,1,0:T(8,128)(2,1)}, u32[]{:S(2)}) copy-start(bf16[1,4096,512]{2,1,0:T(8,128)(2,1)} %all-gather.9.cloned.1.call-done) | copy-start | bytes 12582916
  477.1 74.4 %all-gather.19.cloned.1.call-start = ((), (), s32[]{:S(2)}) async-start(), calls=%async_computation.18 | async-start | bytes 4456448 | tf_op jit(solution)/shard_map/all_gather | solution.py:38
  497.9 79.1 %copy-start = (f32[1,256,512]{2,1,0:T(8,128)S(1)}, f32[1,256,512]{2,1,0:T(8,128)}, u32[]{:S(2)}) copy-start(f32[1,256,512]{2,1,0:T(8,128)} %reduce-scatter.8.cloned.1.call-done) | copy-start | bytes 1572868
  497.9 79.1 %copy-start.1 = (f32[1,256,512]{2,1,0:T(8,128)S(1)}, f32[1,256,512]{2,1,0:T(8,128)}, u32[]{:S(2)}) copy-start(f32[1,256,512]{2,1,0:T(8,128)} %reduce-scatter.12.cloned.1.call-done) | copy-start | bytes 1572868
  497.9 79.1 %copy-start.2 = (f32[1,256,512]{2,1,0:T(8,128)S(1)}, f32[1,256,512]{2,1,0:T(8,128)}, u32[]{:S(2)}) copy-start(f32[1,256,512]{2,1,0:T(8,128)} %reduce-scatter.16.cloned.1.call-done) | copy-start | bytes 1572868
  497.9 79.0 %reduce-scatter.20.cloned.1.call-start = ((), (), s32[]{:S(2)}) async-start(), calls=%async_computation.19 | async-start | bytes 1572864 | tf_op jit(solution)/shard_map/reduce_scatter | solution.py:40
Sparse Core Ops, SparseCore 0:
  9.5 53.2 all-gather.20
  69.7 18.7 reduce-scatter.7
  91.0 50.5 all-gather.8
  148.5 18.7 reduce-scatter.9
  169.4 53.2 all-gather.10
  229.6 18.4 reduce-scatter.11
  250.5 50.5 all-gather.12
  312.8 18.7 reduce-scatter.13
  333.8 53.2 all-gather.14
  394.0 18.4 reduce-scatter.15
  414.9 50.5 all-gather.16
  477.2 18.7 reduce-scatter.17
  498.2 53.2 all-gather.18
  558.4 18.4 reduce-scatter.19
where the time goes:
time: 587 us; the launch traced here: 586 us
  waiting for transfers between devices  492 us (84%)
  matrix products  62.9 us (11%)
  between operations  13.4 us (2%)
  other arithmetic  13.3 us (2%)
    all_gather x4, waiting for transfers between devices, forward_solve(): lax.all_gather(residual, 'rows', axis=1, tiled=True)  215 us
    all_gather x3, waiting for transfers between devices, forward_solve(): lax.all_gather(solved.astype(jnp.bfloat16), 'rows', axis=1, tiled=True)[0]  148 us
    reduce_scatter x4, waiting for transfers between devices, forward_solve(): solved = lax.psum_scatter(products, 'cols', scatter_dimension=0, tiled=True)  74.8 us
    reduce_scatter x3, waiting for transfers between devices, forward_solve(): lax.psum_scatter(partial_value, 'cols', scatter_dimension=0, tiled=True)  54.4 us
    dot_general x6, matrix products, product(): jnp.einsum('abk,kn->abn', factor_block, rows_all, preferred_element_type=...  35.8 us
    dot_general x4, matrix products, fold_rows(): jnp.einsum('abk,kn->abn', factor_block, incoming[0], preferred_element_ty...  27.1 us
  transfers between devices with their start and end apart: 14, of which 14 were waited for; matrix products, arithmetic and copies ran while one was open for 1% of the time, Pallas kernels for 0%

commit v1 on v0

v1 whole, which is shorter than its diff:
```python
import functools

import jax
import jax.numpy as jnp
from jax import lax
from jax.experimental import pallas as pl
from jax.experimental.pallas import tpu as pltpu
from jax.sharding import PartitionSpec as P


def pair_index(target, source):
    return target * (target - 1) // 2 + source


def swap(block, mask, rows):
    return lax.ppermute(block, "rows", [(i, i ^ mask) for i in range(rows)])


def gather_rows(block, rows):
    height = block.shape[0]
    half = height // 2
    if rows != 16:
        everything = lax.all_gather(block, "rows", axis=0, tiled=True)
        return [(everything, None)]
    join = lambda *parts: jnp.concatenate(parts, axis=0)
    far = swap(block, 8, rows)
    near = swap(block, 4, rows)
    side = swap(block, 2, rows)
    by_near = swap(join(far, side[:half]), 4, rows)
    by_side = swap(join(far, near[half:]), 2, rows)
    last_side = swap(by_near[:half], 2, rows)
    last_near = swap(by_side[half:height], 4, rows)
    stages = [
        (join(block, far, near, side), [(0, 0, height), (8, 0, height), (4, 0, height), (2, 0, height)]),
        (join(by_near, by_side), [(12, 0, height), (6, 0, half), (10, 0, height), (6, half, half)]),
        (join(last_side, last_near), [(14, 0, half), (14, half, half)]),
    ]
    pieces = []
    for array, parts in stages:
        pieces.append((array, parts))
        pieces.append((swap(array, 1, rows), [(mask + 1, start, count) for mask, start, count in parts]))
    return pieces


def product_kernel(parts, has_total, where_ref, factor_ref, *refs):
    piece_refs = refs[: len(parts)]
    total_ref = refs[len(parts)] if has_total else None
    out_refs = refs[len(parts) + has_total : -1]
    vector_ref = refs[-1]
    own_row, own_group = where_ref[0], where_ref[1]
    groups, height, _ = factor_ref.shape
    for piece_ref, inside in zip(piece_refs, parts, strict=True):
        if inside is None:
            vector_ref[...] = piece_ref[...]
            continue
        offset = 0
        for mask, start, count in inside:
            place = pl.multiple_of((own_row ^ mask) * height + start, count)
            vector_ref[pl.ds(place, count)] = piece_ref[offset : offset + count]
            offset += count
    vector = vector_ref[...]
    for turn in range(groups):
        group = lax.rem(own_group + 1 + turn, groups)
        result = jnp.dot(factor_ref[group], vector, preferred_element_type=jnp.float32)
        span = pl.ds(turn * height, height)
        if has_total:
            result = result + total_ref[span]
        if len(out_refs) == 1:
            out_refs[0][span] = result
        elif turn < groups - 1:
            out_refs[0][span] = result.astype(jnp.bfloat16)
        else:
            out_refs[1][...] = result


def product(where, factor, pieces, total, split):
    groups, height, width = factor.shape
    columns = pieces[0][0].shape[1]
    full = groups * height
    if split:
        out_shape = (
            jax.ShapeDtypeStruct((full - height, columns), jnp.bfloat16),
            jax.ShapeDtypeStruct((height, columns), jnp.float32),
        )
    else:
        out_shape = (jax.ShapeDtypeStruct((full, columns), jnp.float32),)
    vmem = pl.BlockSpec(memory_space=pltpu.VMEM)
    operands = [where, factor, *(array for array, _ in pieces)] + ([] if total is None else [total])
    return pl.pallas_call(
        functools.partial(product_kernel, [parts for _, parts in pieces], total is not None),
        out_shape=out_shape,
        in_specs=[pl.BlockSpec(memory_space=pltpu.SMEM)] + [vmem] * (len(operands) - 1),
        out_specs=tuple(vmem for _ in out_shape),
        scratch_shapes=[pltpu.VMEM((width, columns), jnp.bfloat16)],
        compiler_params=pltpu.CompilerParams(vmem_limit_bytes=20 * 1024 * 1024),
        cost_estimate=pl.CostEstimate(
            flops=2 * full * width * columns,
            bytes_accessed=2 * (full * width + width * columns) + 4 * full * columns,
            transcendentals=0,
        ),
    )(*operands)


def fold_cols(sends, keep, cols):
    height = keep.shape[0]
    total = keep
    for step in range(1, cols):
        share = sends[(step - 1) * height : step * height]
        came = lax.ppermute(share, "cols", [(i, (i + step) % cols) for i in range(cols)])
        total = total + came.astype(jnp.float32)
    return total


def forward_solve(rows, cols, right_side, inverse_blocks, lower_blocks):
    panels, _, height, columns = right_side.shape
    where = jnp.stack([lax.axis_index("rows"), lax.axis_index("cols")]).astype(jnp.int32)
    chunks = 2 if rows == 16 and cols == 2 else 1
    width = columns // chunks
    solved = [[None] * chunks for _ in range(panels)]
    totals = [{} for _ in range(chunks)]
    pieces = [None] * chunks
    for current in range(panels):
        inverse_blocks, lower_blocks, right_side = lax.optimization_barrier((inverse_blocks, lower_blocks, right_side))
        inverse = inverse_blocks[current]
        lowers = {later: lower_blocks[pair_index(later, current - 1)] for later in range(current, panels) if current > 0}
        for chunk in range(chunks):
            residual = right_side[current, 0, :, chunk * width : (chunk + 1) * width]
            if current > 0:
                factor = lowers[current]
                sends, keep = product(where, factor, pieces[chunk], totals[chunk].pop(current, None), True)
                residual = residual - fold_cols(sends, keep, cols)
                for later in range(current + 1, panels):
                    factor = lowers[later]
                    (totals[chunk][later],) = product(
                        where, factor, pieces[chunk], totals[chunk].get(later), False
                    )
            around = gather_rows(residual.astype(jnp.bfloat16), rows)
            sends, keep = product(where, inverse, around, None, True)
            answer = fold_cols(sends, keep, cols)
            solved[current][chunk] = answer
            if current + 1 < panels:
                pieces[chunk] = gather_rows(answer.astype(jnp.bfloat16), rows)
    return jnp.stack([jnp.concatenate(part, axis=1) for part in solved])[:, None]


def solution(mesh):
    return jax.shard_map(
        functools.partial(forward_solve, mesh.shape["rows"], mesh.shape["cols"]),
        mesh=mesh,
        in_specs=(
            P(None, "cols", "rows", None),
            P(None, None, "rows", "cols"),
            P(None, None, "rows", "cols"),
        ),
        out_specs=P(None, "cols", "rows", None),
        check_vma=False,
    )
```

time: 587 us -> 325 us (0.55)
  waiting for transfers between devices: 492 us -> 117 us
  starting transfers between devices: 0.73 us -> 127 us
  matrix products: 62.9 us -> 0 us
  Pallas kernels: 0 us -> 39.3 us
  local copies, waits for them, and re-layouts: 3.86 us -> 24.6 us
  between operations: 13.4 us -> 2.42 us
    all_gather x7 -> x0, waiting for transfers between devices: 362 us -> none  [the longest x4 215 us: forward_solve(): lax.all_gather(residual, 'rows', axis=1, tiled=True)]
    reduce_scatter x7 -> x0, waiting for transfers between devices: 129 us -> none  [the longest x4 74.8 us: forward_solve(): solved = lax.psum_scatter(products, 'cols', scatter_dimension=0, tiled=True)]
    ppermute x0 -> x154, starting transfers between devices: none -> 127 us  [the longest x140 112 us: swap(): return lax.ppermute(block, 'rows', [(i, i ^ mask) for i in range(rows)])]
    ppermute x0 -> x154, waiting for transfers between devices: none -> 117 us  [the longest x140 104 us: swap(): return lax.ppermute(block, 'rows', [(i, i ^ mask) for i in range(rows)])]
    dot_general x10 -> x0, matrix products: 62.9 us -> none  [the longest x6 35.8 us: product(): jnp.einsum('abk,kn->abn', factor_block, rows_all, preferred_element_type=...]
    pallas_call x0 -> x20, Pallas kernels: none -> 39.3 us  [product(): pl.pallas_call(functools.partial(product_kernel, [parts for _, parts in p...]
    squeeze x0 -> x7, local copies, waits for them, and re-layouts: none -> 23.6 us  [the longest x4 12 us: forward_solve(): inverse = inverse_blocks[current]]
    convert_element_type x6 -> x9, other arithmetic: 10.7 us -> 4.4 us  [the longest x6 3.02 us: forward_solve(): pieces[chunk] = gather_rows(answer.astype(jnp.bfloat16), rows)]
  transfers between devices with their start and end apart: 14 -> 154, of which waited for: 14 -> 72; matrix products, arithmetic and copies ran while one was open for 1% -> 9% of each run, Pallas kernels for 0% -> 12%
where the time goes in v1:
time: 325 us; the launch traced here: 319 us
  starting transfers between devices  127 us (39%)
  waiting for transfers between devices  117 us (36%)
  Pallas kernels  39.3 us (12%)
  local copies, waits for them, and re-layouts  24.6 us (8%)
  other arithmetic  8.85 us (3%)
    ppermute x140, starting transfers between devices, swap(): return lax.ppermute(block, 'rows', [(i, i ^ mask) for i in range(rows)])  112 us
    ppermute x140, waiting for transfers between devices, swap(): return lax.ppermute(block, 'rows', [(i, i ^ mask) for i in range(rows)])  104 us
    pallas_call x20, Pallas kernels, product(): pl.pallas_call(functools.partial(product_kernel, [parts for _, parts in p...  39.3 us
    ppermute x14, starting transfers between devices, fold_cols(): lax.ppermute(share, 'cols', [(i, (i + step) % cols) for i in range(cols)])  15.2 us
    ppermute x14, waiting for transfers between devices, fold_cols(): lax.ppermute(share, 'cols', [(i, (i + step) % cols) for i in range(cols)])  13.1 us
    squeeze x4, local copies, waits for them, and re-layouts, forward_solve(): inverse = inverse_blocks[current]  12 us
    squeeze x3, local copies, waits for them, and re-layouts, forward_solve(): lower_blocks[pair_index(later, current - 1)]  11.5 us
  transfers between devices with their start and end apart: 154, of which 72 were waited for; matrix products, arithmetic and copies ran while one was open for 9% of the time, Pallas kernels for 12%

profile of v1, /device:TPU:0, one launch (start us, length us, event | category | flops | bytes accessed | tf_op | source)
XLA Modules:
  0.0 319.0 jit_solution(4810544686532335817)
XLA Ops:
  1.8 3.0 collective-permute-start.13
  6.3 2.6 collective-permute-start.11
  9.9 4.7 %slice_bitcast_fusion.9.factor_ref = bf16[2,256,4096]{2,1,0:T(8,128)(2,1)} fusion(bf16[4,2,256,4096]{3,2,1,0:T(8,128)(2,1)} %param.4), kind=kLoop, calls=%fused_computation.9 | loop fusion | bytes 8388608 | tf_op jit(solution)/shard_map/squeeze | solution.py:124
  14.8 2.0 collective-permute-start.15
  18.4 3.2 %collective-permute-done = bf16[256,256]{1,0:T(8,128)(2,1)S(1)} collective-permute-done((bf16[256,256]{1,0:T(8,128)(2,1)S(1)}, bf16[256,256]{1,0:T(8,128)(2,1)S(1)}, u32[]{:S(2)}, u32[]{:S(2)}) %collective-permute-start) | collective-permute-done | bytes 131104 | tf_op jit(solution)/shard_map/ppermute | solution.py:16
  25.5 1.9 collective-permute-done.4
  35.9 2.6 collective-permute-done.8
  39.1 1.9 shard_map.38
  42.6 5.1 %slice_bitcast_fusion = (bf16[2,256,4096]{2,1,0:T(8,128)(2,1)S(1)}, bf16[2,256,4096]{2,1,0:T(8,128)(2,1)S(1)}, bf16[2,256,4096]{2,1,0:T(8,128)(2,1)S(1)}) fusion(bf16[6,2,256,4096]{3,2,1,0:T(8,128)(2,1)} %param.5), kind=kLoop, calls=%fused_computation | loop fusion | bytes 25165824 | tf_op jit(solution)/shard_map/squeeze | solution.py:125
  47.7 1.9 shard_map.37
  57.4 2.0 collective-permute-start.22
  63.5 2.6 collective-permute-done.23
  70.9 2.8 collective-permute-done.26
  76.0 2.0 collective-permute-done.52
  79.3 3.0 collective-permute-done.30
  82.9 4.0 %slice_bitcast_fusion.1 = (bf16[2,256,4096]{2,1,0:T(8,128)(2,1)S(1)}, bf16[2,256,4096]{2,1,0:T(8,128)(2,1)S(1)}) fusion(bf16[6,2,256,4096]{3,2,1,0:T(8,128)(2,1)} %param.5), kind=kLoop, calls=%fused_computation.1 | loop fusion | bytes 16777216 | tf_op jit(solution)/shard_map/squeeze | solution.py:125
  86.9 2.0 shard_map.41
  90.5 2.0 shard_map.39
  93.0 2.5 slice_bitcast_fusion.8.factor_ref
  95.5 2.2 collective-permute-done.32
  102.3 2.5 slice_bitcast_fusion.6.factor_ref
  106.6 1.8 collective-permute-start.33
  110.8 3.8 %collective-permute-done.34 = bf16[256,256]{1,0:T(8,128)(2,1)S(1)} collective-permute-done((bf16[256,256]{1,0:T(8,128)(2,1)S(1)}, bf16[256,256]{1,0:T(8,128)(2,1)S(1)}, u32[]{:S(2)}, u32[]{:S(2)}) %collective-permute-start.34) | collective-permute-done | bytes 131104 | tf_op jit(solution)/shard_map/ppermute | solution.py:16
  125.8 1.9 collective-permute-done.40
  127.7 2.0 collective-permute-done.41
  131.2 2.0 shard_map.42
  134.6 1.9 shard_map.46.refs_6_
  136.6 2.0 shard_map.40
  149.4 2.2 collective-permute-start.92
  151.9 3.0 collective-permute-done.67
  154.9 2.3 collective-permute-start.70
  160.6 2.1 collective-permute-done.70
  165.0 1.9 collective-permute-done.96
  168.6 2.7 collective-permute-done.74
  172.8 2.0 shard_map.43.refs_6_
  174.8 2.0 shard_map.47
  178.4 2.0 shard_map.44
  181.2 2.5 slice_bitcast_fusion.2.factor_ref
  183.7 2.4 collective-permute-done.76
  189.6 1.9 shard_map.53.refs_6_
  191.5 2.0 shard_map.49.refs_6_
  199.4 3.7 %collective-permute-done.78 = bf16[256,256]{1,0:T(8,128)(2,1)S(1)} collective-permute-done((bf16[256,256]{1,0:T(8,128)(2,1)S(1)}, bf16[256,256]{1,0:T(8,128)(2,1)S(1)}, u32[]{:S(2)}, u32[]{:S(2)}) %collective-permute-start.78) | collective-permute-done | bytes 131104 | tf_op jit(solution)/shard_map/ppermute | solution.py:16
  216.1 2.3 collective-permute-done.85
  219.9 2.0 shard_map.48
  222.8 2.0 shard_map.54.refs_6_
  224.8 2.0 shard_map.45
  229.7 1.8 collective-permute-start.132
  237.5 2.1 collective-permute-start.136
  240.1 2.8 collective-permute-done.111
  242.9 2.3 collective-permute-start.114
  248.7 2.0 collective-permute-done.114
  256.6 2.7 collective-permute-done.118
  260.7 2.0 shard_map.50.refs_6_
  262.7 2.2 shard_map.55
  265.9 2.0 shard_map.51
  269.1 2.5 slice_bitcast_fusion.3.factor_ref
  271.6 2.0 collective-permute-done.120
  281.0 3.3 %collective-permute-done.122 = bf16[256,256]{1,0:T(8,128)(2,1)S(1)} collective-permute-done((bf16[256,256]{1,0:T(8,128)(2,1)S(1)}, bf16[256,256]{1,0:T(8,128)(2,1)S(1)}, u32[]{:S(2)}, u32[]{:S(2)}) %collective-permute-start.122) | collective-permute-done | bytes 131104 | tf_op jit(solution)/shard_map/ppermute | solution.py:16
  286.7 2.3 collective-permute-done.144
  294.5 1.9 collective-permute-done.147
  302.1 2.8 collective-permute-done.151
  306.4 2.0 shard_map.52
  309.4 2.0 shard_map.56
  314.3 2.7 collective-permute-done.153
  (494 shorter events, 163.4 us)
Async XLA Ops:
  1.8 12.9 %collective-permute-start.13 = (bf16[256,256]{1,0:T(8,128)(2,1)S(1)}, bf16[256,256]{1,0:T(8,128)(2,1)S(1)}, u32[]{:S(2)}, u32[]{:S(2)}) collective-permute-start(bf16[256,256]{1,0:T(8,128)(2,1)S(1)} %get-tuple-element.107), channel_id=1, source_target_pairs={{0,4},{2,6},{4,0},{6,2},{8,12},{10,14},{12,8},{14,10},{16,20},{18,... | collective-permute-start | bytes 393224 | tf_op jit(solution)/shard_map/ppermute | solution.py:16
  4.8 9.9 %collective-permute-start.12 = (bf16[256,256]{1,0:T(8,128)(2,1)S(1)}, bf16[256,256]{1,0:T(8,128)(2,1)S(1)}, u32[]{:S(2)}, u32[]{:S(2)}) collective-permute-start(bf16[256,256]{1,0:T(8,128)(2,1)S(1)} %get-tuple-element.107), channel_id=1, source_target_pairs={{0,8},{2,10},{4,12},{6,14},{8,0},{10,2},{12,4},{14,6},{16,24},{18,... | collective-permute-start | bytes 393224 | tf_op jit(solution)/shard_map/ppermute | solution.py:16
  6.3 8.4 %collective-permute-start.11 = (bf16[256,256]{1,0:T(8,128)(2,1)S(1)}, bf16[256,256]{1,0:T(8,128)(2,1)S(1)}, u32[]{:S(2)}, u32[]{:S(2)}) collective-permute-start(bf16[256,256]{1,0:T(8,128)(2,1)S(1)} %get-tuple-element.107), channel_id=1, source_target_pairs={{0,16},{2,18},{4,20},{6,22},{8,24},{10,26},{12,28},{14,30},{16,0},... | collective-permute-start | bytes 393224 | tf_op jit(solution)/shard_map/ppermute | solution.py:16
  8.9 9.3 %collective-permute-start.2 = (bf16[256,256]{1,0:T(8,128)(2,1)S(1)}, bf16[256,256]{1,0:T(8,128)(2,1)S(1)}, u32[]{:S(2)}, u32[]{:S(2)}) collective-permute-start(bf16[256,256]{1,0:T(8,128)(2,1)S(1)} %get-tuple-element.106), channel_id=1, source_target_pairs={{0,4},{2,6},{4,0},{6,2},{8,12},{10,14},{12,8},{14,10},{16,20},{18,... | collective-permute-start | bytes 393224 | tf_op jit(solution)/shard_map/ppermute | solution.py:16
  9.5 8.9 %collective-permute-start.1 = (bf16[256,256]{1,0:T(8,128)(2,1)S(1)}, bf16[256,256]{1,0:T(8,128)(2,1)S(1)}, u32[]{:S(2)}, u32[]{:S(2)}) collective-permute-start(bf16[256,256]{1,0:T(8,128)(2,1)S(1)} %get-tuple-element.106), channel_id=1, source_target_pairs={{0,8},{2,10},{4,12},{6,14},{8,0},{10,2},{12,4},{14,6},{16,24},{18,... | collective-permute-start | bytes 393224 | tf_op jit(solution)/shard_map/ppermute | solution.py:16
  14.8 10.0 %collective-permute-start.15 = (bf16[384,256]{1,0:T(8,128)(2,1)S(1)}, bf16[384,256]{1,0:T(8,128)(2,1)S(1)}, u32[]{:S(2)}, u32[]{:S(2)}) collective-permute-start(bf16[384,256]{1,0:T(8,128)(2,1)S(1)} %get-tuple-element.135), channel_id=1, source_target_pairs={{0,8},{2,10},{4,12},{6,14},{8,0},{10,2},{12,4},{14,6},{16,24},{18,... | collective-permute-start | bytes 589832 | tf_op jit(solution)/shard_map/ppermute | solution.py:16
  18.3 20.8 %collective-permute-start.14 = (bf16[1024,256]{1,0:T(8,128)(2,1)S(1)}, bf16[1024,256]{1,0:T(8,128)(2,1)S(1)}, u32[]{:S(2)}, u32[]{:S(2)}) collective-permute-start(bf16[1024,256]{1,0:T(8,128)(2,1)S(1)} %pad_maximum_fusion.1.refs_0_), channel_id=1, source_target_pairs={{0,2},{2,0},{4,6},{6,4},{8,10},{10,8},{12,14},{14,12},{16,18},{18,... | collective-permute-start | bytes 1572872 | tf_op jit(solution)/shard_map/ppermute | solution.py:16
  24.8 22.9 %collective-permute-start.3 = (bf16[1024,256]{1,0:T(8,128)(2,1)S(1)}, bf16[1024,256]{1,0:T(8,128)(2,1)S(1)}, u32[]{:S(2)}, u32[]{:S(2)}) collective-permute-start(bf16[1024,256]{1,0:T(8,128)(2,1)S(1)} %pad_maximum_fusion.refs_0_), channel_id=1, source_target_pairs={{0,2},{2,0},{4,6},{6,4},{8,10},{10,8},{12,14},{14,12},{16,18},{18,... | collective-permute-start | bytes 1572872 | tf_op jit(solution)/shard_map/ppermute | solution.py:16
  24.9 14.1 %collective-permute-start.17 = (bf16[768,256]{1,0:T(8,128)(2,1)S(1)}, bf16[768,256]{1,0:T(8,128)(2,1)S(1)}, u32[]{:S(2)}, u32[]{:S(2)}) collective-permute-start(bf16[768,256]{1,0:T(8,128)(2,1)S(1)} %constant_dynamic-update-slice_fusion.4.refs_2_), channel_id=1, source_target_pairs={{0,2},{2,0},{4,6},{6,4},{8,10},{10,8},{12,14},{14,12},{16,18},{18,... | collective-permute-start | bytes 1179656 | tf_op jit(solution)/shard_map/ppermute | solution.py:16
  38.5 9.3 %collective-permute-start.6 = (bf16[768,256]{1,0:T(8,128)(2,1)S(1)}, bf16[768,256]{1,0:T(8,128)(2,1)S(1)}, u32[]{:S(2)}, u32[]{:S(2)}) collective-permute-start(bf16[768,256]{1,0:T(8,128)(2,1)S(1)} %constant_dynamic-update-slice_fusion.refs_2_), channel_id=1, source_target_pairs={{0,2},{2,0},{4,6},{6,4},{8,10},{10,8},{12,14},{14,12},{16,18},{18,... | collective-permute-start | bytes 1179656 | tf_op jit(solution)/shard_map/ppermute | solution.py:16
  38.5 9.2 %collective-permute-start.9 = (bf16[256,256]{1,0:T(8,128)(2,1)S(1)}, bf16[256,256]{1,0:T(8,128)(2,1)S(1)}, u32[]{:S(2)}, u32[]{:S(2)}) collective-permute-start(bf16[256,256]{1,0:T(8,128)(2,1)S(1)} %constant_dynamic-update-slice_fusion.2.refs_4_), channel_id=1, source_target_pairs={{0,2},{2,0},{4,6},{6,4},{8,10},{10,8},{12,14},{14,12},{16,18},{18,... | collective-permute-start | bytes 393224 | tf_op jit(solution)/shard_map/ppermute | solution.py:16
  41.0 9.2 %collective-permute-start.21 = (bf16[256,256]{1,0:T(8,128)(2,1)S(1)}, bf16[256,256]{1,0:T(8,128)(2,1)S(1)}, u32[]{:S(2)}, u32[]{:S(2)}) collective-permute-start(bf16[256,256]{1,0:T(8,128)(2,1)S(1)} %get-tuple-element.49), channel_id=1, source_target_pairs={{0,1},{1,0},{2,3},{3,2},{4,5},{5,4},{6,7},{7,6},{8,9},{9,8},{10,11... | collective-permute-start | bytes 393224 | tf_op jit(solution)/shard_map/ppermute | solution.py:109
  52.8 8.6 %collective-permute-start.44 = (bf16[256,256]{1,0:T(8,128)(2,1)S(1)}, bf16[256,256]{1,0:T(8,128)(2,1)S(1)}, u32[]{:S(2)}, u32[]{:S(2)}) collective-permute-start(bf16[256,256]{1,0:T(8,128)(2,1)S(1)} %get-tuple-element.93), channel_id=1, source_target_pairs={{0,16},{2,18},{4,20},{6,22},{8,24},{10,26},{12,28},{14,30},{16,0},... | collective-permute-start | bytes 393224 | tf_op jit(solution)/shard_map/ppermute | solution.py:16
  57.0 9.2 %collective-permute-start.23 = (bf16[256,256]{1,0:T(8,128)(2,1)S(1)}, bf16[256,256]{1,0:T(8,128)(2,1)S(1)}, u32[]{:S(2)}, u32[]{:S(2)}) collective-permute-start(bf16[256,256]{1,0:T(8,128)(2,1)S(1)} %get-tuple-element.87), channel_id=1, source_target_pairs={{0,8},{2,10},{4,12},{6,14},{8,0},{10,2},{12,4},{14,6},{16,24},{18,... | collective-permute-start | bytes 393224 | tf_op jit(solution)/shard_map/ppermute | solution.py:16
  57.4 8.7 %collective-permute-start.22 = (bf16[256,256]{1,0:T(8,128)(2,1)S(1)}, bf16[256,256]{1,0:T(8,128)(2,1)S(1)}, u32[]{:S(2)}, u32[]{:S(2)}) collective-permute-start(bf16[256,256]{1,0:T(8,128)(2,1)S(1)} %get-tuple-element.87), channel_id=1, source_target_pairs={{0,16},{2,18},{4,20},{6,22},{8,24},{10,26},{12,28},{14,30},{16,0},... | collective-permute-start | bytes 393224 | tf_op jit(solution)/shard_map/ppermute | solution.py:16
  61.4 9.0 %collective-permute-start.48 = (bf16[384,256]{1,0:T(8,128)(2,1)S(1)}, bf16[384,256]{1,0:T(8,128)(2,1)S(1)}, u32[]{:S(2)}, u32[]{:S(2)}) collective-permute-start(bf16[384,256]{1,0:T(8,128)(2,1)S(1)} %get-tuple-element.133), channel_id=1, source_target_pairs={{0,8},{2,10},{4,12},{6,14},{8,0},{10,2},{12,4},{14,6},{16,24},{18,... | collective-permute-start | bytes 589832 | tf_op jit(solution)/shard_map/ppermute | solution.py:16
  62.1 8.2 %collective-permute-start.49 = (bf16[384,256]{1,0:T(8,128)(2,1)S(1)}, bf16[384,256]{1,0:T(8,128)(2,1)S(1)}, u32[]{:S(2)}, u32[]{:S(2)}) collective-permute-start(bf16[384,256]{1,0:T(8,128)(2,1)S(1)} %get-tuple-element.132), channel_id=1, source_target_pairs={{0,4},{2,6},{4,0},{6,2},{8,12},{10,14},{12,8},{14,10},{16,20},{18,... | collective-permute-start | bytes 589832 | tf_op jit(solution)/shard_map/ppermute | solution.py:16
  63.4 23.4 %collective-permute-start.47 = (bf16[1024,256]{1,0:T(8,128)(2,1)S(1)}, bf16[1024,256]{1,0:T(8,128)(2,1)S(1)}, u32[]{:S(2)}, u32[]{:S(2)}) collective-permute-start(bf16[1024,256]{1,0:T(8,128)(2,1)S(1)} %pad_maximum_fusion.4.refs_0_), channel_id=1, source_target_pairs={{0,2},{2,0},{4,6},{6,4},{8,10},{10,8},{12,14},{14,12},{16,18},{18,... | collective-permute-start | bytes 1572872 | tf_op jit(solution)/shard_map/ppermute | solution.py:16
  70.3 20.1 %collective-permute-start.25 = (bf16[1024,256]{1,0:T(8,128)(2,1)S(1)}, bf16[1024,256]{1,0:T(8,128)(2,1)S(1)}, u32[]{:S(2)}, u32[]{:S(2)}) collective-permute-start(bf16[1024,256]{1,0:T(8,128)(2,1)S(1)} %pad_maximum_fusion.2.refs_0_), channel_id=1, source_target_pairs={{0,2},{2,0},{4,6},{6,4},{8,10},{10,8},{12,14},{14,12},{16,18},{18,... | collective-permute-start | bytes 1572872 | tf_op jit(solution)/shard_map/ppermute | solution.py:16
  74.6 12.2 %collective-permute-start.50 = (bf16[768,256]{1,0:T(8,128)(2,1)S(1)}, bf16[768,256]{1,0:T(8,128)(2,1)S(1)}, u32[]{:S(2)}, u32[]{:S(2)}) collective-permute-start(bf16[768,256]{1,0:T(8,128)(2,1)S(1)} %constant_dynamic-update-slice_fusion.16.refs_2_), channel_id=1, source_target_pairs={{0,2},{2,0},{4,6},{6,4},{8,10},{10,8},{12,14},{14,12},{16,18},{18,... | collective-permute-start | bytes 1179656 | tf_op jit(solution)/shard_map/ppermute | solution.py:16
  82.3 8.2 %collective-permute-start.28 = (bf16[768,256]{1,0:T(8,128)(2,1)S(1)}, bf16[768,256]{1,0:T(8,128)(2,1)S(1)}, u32[]{:S(2)}, u32[]{:S(2)}) collective-permute-start(bf16[768,256]{1,0:T(8,128)(2,1)S(1)} %constant_dynamic-update-slice_fusion.8.refs_2_), channel_id=1, source_target_pairs={{0,2},{2,0},{4,6},{6,4},{8,10},{10,8},{12,14},{14,12},{16,18},{18,... | collective-permute-start | bytes 1179656 | tf_op jit(solution)/shard_map/ppermute | solution.py:16
  99.6 8.8 %collective-permute-start.56 = (bf16[256,256]{1,0:T(8,128)(2,1)S(1)}, bf16[256,256]{1,0:T(8,128)(2,1)S(1)}, u32[]{:S(2)}, u32[]{:S(2)}) collective-permute-start(bf16[256,256]{1,0:T(8,128)(2,1)S(1)} %get-tuple-element.105), channel_id=1, source_target_pairs={{0,8},{2,10},{4,12},{6,14},{8,0},{10,2},{12,4},{14,6},{16,24},{18,... | collective-permute-start | bytes 393224 | tf_op jit(solution)/shard_map/ppermute | solution.py:16
  106.0 8.6 %collective-permute-start.34 = (bf16[256,256]{1,0:T(8,128)(2,1)S(1)}, bf16[256,256]{1,0:T(8,128)(2,1)S(1)}, u32[]{:S(2)}, u32[]{:S(2)}) collective-permute-start(bf16[256,256]{1,0:T(8,128)(2,1)S(1)} %get-tuple-element.104), channel_id=1, source_target_pairs={{0,8},{2,10},{4,12},{6,14},{8,0},{10,2},{12,4},{14,6},{16,24},{18,... | collective-permute-start | bytes 393224 | tf_op jit(solution)/shard_map/ppermute | solution.py:16
  108.5 10.3 %collective-permute-start.59 = (bf16[384,256]{1,0:T(8,128)(2,1)S(1)}, bf16[384,256]{1,0:T(8,128)(2,1)S(1)}, u32[]{:S(2)}, u32[]{:S(2)}) collective-permute-start(bf16[384,256]{1,0:T(8,128)(2,1)S(1)} %get-tuple-element.131), channel_id=1, source_target_pairs={{0,8},{2,10},{4,12},{6,14},{8,0},{10,2},{12,4},{14,6},{16,24},{18,... | collective-permute-start | bytes 589832 | tf_op jit(solution)/shard_map/ppermute | solution.py:16
  109.4 9.4 %collective-permute-start.60 = (bf16[384,256]{1,0:T(8,128)(2,1)S(1)}, bf16[384,256]{1,0:T(8,128)(2,1)S(1)}, u32[]{:S(2)}, u32[]{:S(2)}) collective-permute-start(bf16[384,256]{1,0:T(8,128)(2,1)S(1)} %get-tuple-element.130), channel_id=1, source_target_pairs={{0,4},{2,6},{4,0},{6,2},{8,12},{10,14},{12,8},{14,10},{16,20},{18,... | collective-permute-start | bytes 589832 | tf_op jit(solution)/shard_map/ppermute | solution.py:16
  110.8 20.4 %collective-permute-start.58 = (bf16[1024,256]{1,0:T(8,128)(2,1)S(1)}, bf16[1024,256]{1,0:T(8,128)(2,1)S(1)}, u32[]{:S(2)}, u32[]{:S(2)}) collective-permute-start(bf16[1024,256]{1,0:T(8,128)(2,1)S(1)} %pad_maximum_fusion.5.refs_0_), channel_id=1, source_target_pairs={{0,2},{2,0},{4,6},{6,4},{8,10},{10,8},{12,14},{14,12},{16,18},{18,... | collective-permute-start | bytes 1572872 | tf_op jit(solution)/shard_map/ppermute | solution.py:16
  118.8 17.8 %collective-permute-start.36 = (bf16[1024,256]{1,0:T(8,128)(2,1)S(1)}, bf16[1024,256]{1,0:T(8,128)(2,1)S(1)}, u32[]{:S(2)}, u32[]{:S(2)}) collective-permute-start(bf16[1024,256]{1,0:T(8,128)(2,1)S(1)} %pad_maximum_fusion.3.refs_0_), channel_id=1, source_target_pairs={{0,2},{2,0},{4,6},{6,4},{8,10},{10,8},{12,14},{14,12},{16,18},{18,... | collective-permute-start | bytes 1572872 | tf_op jit(solution)/shard_map/ppermute | solution.py:16
  121.6 9.6 %collective-permute-start.61 = (bf16[768,256]{1,0:T(8,128)(2,1)S(1)}, bf16[768,256]{1,0:T(8,128)(2,1)S(1)}, u32[]{:S(2)}, u32[]{:S(2)}) collective-permute-start(bf16[768,256]{1,0:T(8,128)(2,1)S(1)} %constant_dynamic-update-slice_fusion.20.refs_2_), channel_id=1, source_target_pairs={{0,2},{2,0},{4,6},{6,4},{8,10},{10,8},{12,14},{14,12},{16,18},{18,... | collective-permute-start | bytes 1179656 | tf_op jit(solution)/shard_map/ppermute | solution.py:16
  127.7 9.0 %collective-permute-start.39 = (bf16[768,256]{1,0:T(8,128)(2,1)S(1)}, bf16[768,256]{1,0:T(8,128)(2,1)S(1)}, u32[]{:S(2)}, u32[]{:S(2)}) collective-permute-start(bf16[768,256]{1,0:T(8,128)(2,1)S(1)} %constant_dynamic-update-slice_fusion.12.refs_2_), channel_id=1, source_target_pairs={{0,2},{2,0},{4,6},{6,4},{8,10},{10,8},{12,14},{14,12},{16,18},{18,... | collective-permute-start | bytes 1179656 | tf_op jit(solution)/shard_map/ppermute | solution.py:16
  145.8 9.1 %collective-permute-start.67 = (bf16[256,256]{1,0:T(8,128)(2,1)S(1)}, bf16[256,256]{1,0:T(8,128)(2,1)S(1)}, u32[]{:S(2)}, u32[]{:S(2)}) collective-permute-start(bf16[256,256]{1,0:T(8,128)(2,1)S(1)} %get-tuple-element.85), channel_id=1, source_target_pairs={{0,8},{2,10},{4,12},{6,14},{8,0},{10,2},{12,4},{14,6},{16,24},{18,... | collective-permute-start | bytes 393224 | tf_op jit(solution)/shard_map/ppermute | solution.py:16
  146.4 8.5 %collective-permute-start.66 = (bf16[256,256]{1,0:T(8,128)(2,1)S(1)}, bf16[256,256]{1,0:T(8,128)(2,1)S(1)}, u32[]{:S(2)}, u32[]{:S(2)}) collective-permute-start(bf16[256,256]{1,0:T(8,128)(2,1)S(1)} %get-tuple-element.85), channel_id=1, source_target_pairs={{0,16},{2,18},{4,20},{6,22},{8,24},{10,26},{12,28},{14,30},{16,0},... | collective-permute-start | bytes 393224 | tf_op jit(solution)/shard_map/ppermute | solution.py:16
  149.4 9.6 %collective-permute-start.92 = (bf16[384,256]{1,0:T(8,128)(2,1)S(1)}, bf16[384,256]{1,0:T(8,128)(2,1)S(1)}, u32[]{:S(2)}, u32[]{:S(2)}) collective-permute-start(bf16[384,256]{1,0:T(8,128)(2,1)S(1)} %get-tuple-element.129), channel_id=1, source_target_pairs={{0,8},{2,10},{4,12},{6,14},{8,0},{10,2},{12,4},{14,6},{16,24},{18,... | collective-permute-start | bytes 589832 | tf_op jit(solution)/shard_map/ppermute | solution.py:16
  151.8 22.9 %collective-permute-start.91 = (bf16[1024,256]{1,0:T(8,128)(2,1)S(1)}, bf16[1024,256]{1,0:T(8,128)(2,1)S(1)}, u32[]{:S(2)}, u32[]{:S(2)}) collective-permute-start(bf16[1024,256]{1,0:T(8,128)(2,1)S(1)} %pad_maximum_fusion.8.refs_0_), channel_id=1, source_target_pairs={{0,2},{2,0},{4,6},{6,4},{8,10},{10,8},{12,14},{14,12},{16,18},{18,... | collective-permute-start | bytes 1572872 | tf_op jit(solution)/shard_map/ppermute | solution.py:16
  159.1 19.1 %collective-permute-start.69 = (bf16[1024,256]{1,0:T(8,128)(2,1)S(1)}, bf16[1024,256]{1,0:T(8,128)(2,1)S(1)}, u32[]{:S(2)}, u32[]{:S(2)}) collective-permute-start(bf16[1024,256]{1,0:T(8,128)(2,1)S(1)} %pad_maximum_fusion.6.refs_0_), channel_id=1, source_target_pairs={{0,2},{2,0},{4,6},{6,4},{8,10},{10,8},{12,14},{14,12},{16,18},{18,... | collective-permute-start | bytes 1572872 | tf_op jit(solution)/shard_map/ppermute | solution.py:16
  163.5 11.2 %collective-permute-start.94 = (bf16[768,256]{1,0:T(8,128)(2,1)S(1)}, bf16[768,256]{1,0:T(8,128)(2,1)S(1)}, u32[]{:S(2)}, u32[]{:S(2)}) collective-permute-start(bf16[768,256]{1,0:T(8,128)(2,1)S(1)} %constant_dynamic-update-slice_fusion.32.refs_2_), channel_id=1, source_target_pairs={{0,2},{2,0},{4,6},{6,4},{8,10},{10,8},{12,14},{14,12},{16,18},{18,... | collective-permute-start | bytes 1179656 | tf_op jit(solution)/shard_map/ppermute | solution.py:16
  168.6 9.6 %collective-permute-start.72 = (bf16[768,256]{1,0:T(8,128)(2,1)S(1)}, bf16[768,256]{1,0:T(8,128)(2,1)S(1)}, u32[]{:S(2)}, u32[]{:S(2)}) collective-permute-start(bf16[768,256]{1,0:T(8,128)(2,1)S(1)} %constant_dynamic-update-slice_fusion.24.refs_2_), channel_id=1, source_target_pairs={{0,2},{2,0},{4,6},{6,4},{8,10},{10,8},{12,14},{14,12},{16,18},{18,... | collective-permute-start | bytes 1179656 | tf_op jit(solution)/shard_map/ppermute | solution.py:16
  186.1 9.2 %collective-permute-start.101 = (bf16[256,256]{1,0:T(8,128)(2,1)S(1)}, bf16[256,256]{1,0:T(8,128)(2,1)S(1)}, u32[]{:S(2)}, u32[]{:S(2)}) collective-permute-start(bf16[256,256]{1,0:T(8,128)(2,1)S(1)} %get-tuple-element.103), channel_id=1, source_target_pairs={{0,4},{2,6},{4,0},{6,2},{8,12},{10,14},{12,8},{14,10},{16,20},{18,... | collective-permute-start | bytes 393224 | tf_op jit(solution)/shard_map/ppermute | solution.py:16
  187.4 9.8 %collective-permute-start.100 = (bf16[256,256]{1,0:T(8,128)(2,1)S(1)}, bf16[256,256]{1,0:T(8,128)(2,1)S(1)}, u32[]{:S(2)}, u32[]{:S(2)}) collective-permute-start(bf16[256,256]{1,0:T(8,128)(2,1)S(1)} %get-tuple-element.103), channel_id=1, source_target_pairs={{0,8},{2,10},{4,12},{6,14},{8,0},{10,2},{12,4},{14,6},{16,24},{18,... | collective-permute-start | bytes 393224 | tf_op jit(solution)/shard_map/ppermute | solution.py:16
  187.9 9.3 %collective-permute-start.99 = (bf16[256,256]{1,0:T(8,128)(2,1)S(1)}, bf16[256,256]{1,0:T(8,128)(2,1)S(1)}, u32[]{:S(2)}, u32[]{:S(2)}) collective-permute-start(bf16[256,256]{1,0:T(8,128)(2,1)S(1)} %get-tuple-element.103), channel_id=1, source_target_pairs={{0,16},{2,18},{4,20},{6,22},{8,24},{10,26},{12,28},{14,30},{16,0},... | collective-permute-start | bytes 393224 | tf_op jit(solution)/shard_map/ppermute | solution.py:16
  194.5 8.5 %collective-permute-start.78 = (bf16[256,256]{1,0:T(8,128)(2,1)S(1)}, bf16[256,256]{1,0:T(8,128)(2,1)S(1)}, u32[]{:S(2)}, u32[]{:S(2)}) collective-permute-start(bf16[256,256]{1,0:T(8,128)(2,1)S(1)} %get-tuple-element.102), channel_id=1, source_target_pairs={{0,8},{2,10},{4,12},{6,14},{8,0},{10,2},{12,4},{14,6},{16,24},{18,... | collective-permute-start | bytes 393224 | tf_op jit(solution)/shard_map/ppermute | solution.py:16
  197.2 10.0 %collective-permute-start.103 = (bf16[384,256]{1,0:T(8,128)(2,1)S(1)}, bf16[384,256]{1,0:T(8,128)(2,1)S(1)}, u32[]{:S(2)}, u32[]{:S(2)}) collective-permute-start(bf16[384,256]{1,0:T(8,128)(2,1)S(1)} %get-tuple-element.127), channel_id=1, source_target_pairs={{0,8},{2,10},{4,12},{6,14},{8,0},{10,2},{12,4},{14,6},{16,24},{18,... | collective-permute-start | bytes 589832 | tf_op jit(solution)/shard_map/ppermute | solution.py:16
  197.9 9.4 %collective-permute-start.104 = (bf16[384,256]{1,0:T(8,128)(2,1)S(1)}, bf16[384,256]{1,0:T(8,128)(2,1)S(1)}, u32[]{:S(2)}, u32[]{:S(2)}) collective-permute-start(bf16[384,256]{1,0:T(8,128)(2,1)S(1)} %get-tuple-element.126), channel_id=1, source_target_pairs={{0,4},{2,6},{4,0},{6,2},{8,12},{10,14},{12,8},{14,10},{16,20},{18,... | collective-permute-start | bytes 589832 | tf_op jit(solution)/shard_map/ppermute | solution.py:16
  199.3 20.6 %collective-permute-start.102 = (bf16[1024,256]{1,0:T(8,128)(2,1)S(1)}, bf16[1024,256]{1,0:T(8,128)(2,1)S(1)}, u32[]{:S(2)}, u32[]{:S(2)}) collective-permute-start(bf16[1024,256]{1,0:T(8,128)(2,1)S(1)} %pad_maximum_fusion.9.refs_0_), channel_id=1, source_target_pairs={{0,2},{2,0},{4,6},{6,4},{8,10},{10,8},{12,14},{14,12},{16,18},{18,... | collective-permute-start | bytes 1572872 | tf_op jit(solution)/shard_map/ppermute | solution.py:16
  207.2 17.5 %collective-permute-start.80 = (bf16[1024,256]{1,0:T(8,128)(2,1)S(1)}, bf16[1024,256]{1,0:T(8,128)(2,1)S(1)}, u32[]{:S(2)}, u32[]{:S(2)}) collective-permute-start(bf16[1024,256]{1,0:T(8,128)(2,1)S(1)} %pad_maximum_fusion.7.refs_0_), channel_id=1, source_target_pairs={{0,2},{2,0},{4,6},{6,4},{8,10},{10,8},{12,14},{14,12},{16,18},{18,... | collective-permute-start | bytes 1572872 | tf_op jit(solution)/shard_map/ppermute | solution.py:16
  210.3 9.6 %collective-permute-start.105 = (bf16[768,256]{1,0:T(8,128)(2,1)S(1)}, bf16[768,256]{1,0:T(8,128)(2,1)S(1)}, u32[]{:S(2)}, u32[]{:S(2)}) collective-permute-start(bf16[768,256]{1,0:T(8,128)(2,1)S(1)} %constant_dynamic-update-slice_fusion.36.refs_2_), channel_id=1, source_target_pairs={{0,2},{2,0},{4,6},{6,4},{8,10},{10,8},{12,14},{14,12},{16,18},{18,... | collective-permute-start | bytes 1179656 | tf_op jit(solution)/shard_map/ppermute | solution.py:16
  216.1 8.7 %collective-permute-start.83 = (bf16[768,256]{1,0:T(8,128)(2,1)S(1)}, bf16[768,256]{1,0:T(8,128)(2,1)S(1)}, u32[]{:S(2)}, u32[]{:S(2)}) collective-permute-start(bf16[768,256]{1,0:T(8,128)(2,1)S(1)} %constant_dynamic-update-slice_fusion.28.refs_2_), channel_id=1, source_target_pairs={{0,2},{2,0},{4,6},{6,4},{8,10},{10,8},{12,14},{14,12},{16,18},{18,... | collective-permute-start | bytes 1179656 | tf_op jit(solution)/shard_map/ppermute | solution.py:16
  228.9 8.5 %collective-permute-start.133 = (bf16[256,256]{1,0:T(8,128)(2,1)S(1)}, bf16[256,256]{1,0:T(8,128)(2,1)S(1)}, u32[]{:S(2)}, u32[]{:S(2)}) collective-permute-start(bf16[256,256]{1,0:T(8,128)(2,1)S(1)} %get-tuple-element.89), channel_id=1, source_target_pairs={{0,8},{2,10},{4,12},{6,14},{8,0},{10,2},{12,4},{14,6},{16,24},{18,... | collective-permute-start | bytes 393224 | tf_op jit(solution)/shard_map/ppermute | solution.py:16
  233.2 9.7 %collective-permute-start.111 = (bf16[256,256]{1,0:T(8,128)(2,1)S(1)}, bf16[256,256]{1,0:T(8,128)(2,1)S(1)}, u32[]{:S(2)}, u32[]{:S(2)}) collective-permute-start(bf16[256,256]{1,0:T(8,128)(2,1)S(1)} %get-tuple-element.83), channel_id=1, source_target_pairs={{0,8},{2,10},{4,12},{6,14},{8,0},{10,2},{12,4},{14,6},{16,24},{18,... | collective-permute-start | bytes 393224 | tf_op jit(solution)/shard_map/ppermute | solution.py:16
  234.3 8.5 %collective-permute-start.110 = (bf16[256,256]{1,0:T(8,128)(2,1)S(1)}, bf16[256,256]{1,0:T(8,128)(2,1)S(1)}, u32[]{:S(2)}, u32[]{:S(2)}) collective-permute-start(bf16[256,256]{1,0:T(8,128)(2,1)S(1)} %get-tuple-element.83), channel_id=1, source_target_pairs={{0,16},{2,18},{4,20},{6,22},{8,24},{10,26},{12,28},{14,30},{16,0},... | collective-permute-start | bytes 393224 | tf_op jit(solution)/shard_map/ppermute | solution.py:16
  237.5 9.6 %collective-permute-start.136 = (bf16[384,256]{1,0:T(8,128)(2,1)S(1)}, bf16[384,256]{1,0:T(8,128)(2,1)S(1)}, u32[]{:S(2)}, u32[]{:S(2)}) collective-permute-start(bf16[384,256]{1,0:T(8,128)(2,1)S(1)} %get-tuple-element.125), channel_id=1, source_target_pairs={{0,8},{2,10},{4,12},{6,14},{8,0},{10,2},{12,4},{14,6},{16,24},{18,... | collective-permute-start | bytes 589832 | tf_op jit(solution)/shard_map/ppermute | solution.py:16
  240.0 22.7 %collective-permute-start.135 = (bf16[1024,256]{1,0:T(8,128)(2,1)S(1)}, bf16[1024,256]{1,0:T(8,128)(2,1)S(1)}, u32[]{:S(2)}, u32[]{:S(2)}) collective-permute-start(bf16[1024,256]{1,0:T(8,128)(2,1)S(1)} %pad_maximum_fusion.12.refs_0_), channel_id=1, source_target_pairs={{0,2},{2,0},{4,6},{6,4},{8,10},{10,8},{12,14},{14,12},{16,18},{18,... | collective-permute-start | bytes 1572872 | tf_op jit(solution)/shard_map/ppermute | solution.py:16
  247.1 18.8 %collective-permute-start.113 = (bf16[1024,256]{1,0:T(8,128)(2,1)S(1)}, bf16[1024,256]{1,0:T(8,128)(2,1)S(1)}, u32[]{:S(2)}, u32[]{:S(2)}) collective-permute-start(bf16[1024,256]{1,0:T(8,128)(2,1)S(1)} %pad_maximum_fusion.10.refs_0_), channel_id=1, source_target_pairs={{0,2},{2,0},{4,6},{6,4},{8,10},{10,8},{12,14},{14,12},{16,18},{18,... | collective-permute-start | bytes 1572872 | tf_op jit(solution)/shard_map/ppermute | solution.py:16
  251.5 11.2 %collective-permute-start.138 = (bf16[768,256]{1,0:T(8,128)(2,1)S(1)}, bf16[768,256]{1,0:T(8,128)(2,1)S(1)}, u32[]{:S(2)}, u32[]{:S(2)}) collective-permute-start(bf16[768,256]{1,0:T(8,128)(2,1)S(1)} %constant_dynamic-update-slice_fusion.48.refs_2_), channel_id=1, source_target_pairs={{0,2},{2,0},{4,6},{6,4},{8,10},{10,8},{12,14},{14,12},{16,18},{18,... | collective-permute-start | bytes 1179656 | tf_op jit(solution)/shard_map/ppermute | solution.py:16
  256.6 9.3 %collective-permute-start.116 = (bf16[768,256]{1,0:T(8,128)(2,1)S(1)}, bf16[768,256]{1,0:T(8,128)(2,1)S(1)}, u32[]{:S(2)}, u32[]{:S(2)}) collective-permute-start(bf16[768,256]{1,0:T(8,128)(2,1)S(1)} %constant_dynamic-update-slice_fusion.40.refs_2_), channel_id=1, source_target_pairs={{0,2},{2,0},{4,6},{6,4},{8,10},{10,8},{12,14},{14,12},{16,18},{18,... | collective-permute-start | bytes 1179656 | tf_op jit(solution)/shard_map/ppermute | solution.py:16
  275.0 9.2 %collective-permute-start.122 = (bf16[256,256]{1,0:T(8,128)(2,1)S(1)}, bf16[256,256]{1,0:T(8,128)(2,1)S(1)}, u32[]{:S(2)}, u32[]{:S(2)}) collective-permute-start(bf16[256,256]{1,0:T(8,128)(2,1)S(1)} %get-tuple-element.100), channel_id=1, source_target_pairs={{0,8},{2,10},{4,12},{6,14},{8,0},{10,2},{12,4},{14,6},{16,24},{18,... | collective-permute-start | bytes 393224 | tf_op jit(solution)/shard_map/ppermute | solution.py:16
  275.4 9.0 %collective-permute-start.121 = (bf16[256,256]{1,0:T(8,128)(2,1)S(1)}, bf16[256,256]{1,0:T(8,128)(2,1)S(1)}, u32[]{:S(2)}, u32[]{:S(2)}) collective-permute-start(bf16[256,256]{1,0:T(8,128)(2,1)S(1)} %get-tuple-element.100), channel_id=1, source_target_pairs={{0,16},{2,18},{4,20},{6,22},{8,24},{10,26},{12,28},{14,30},{16,0},... | collective-permute-start | bytes 393224 | tf_op jit(solution)/shard_map/ppermute | solution.py:16
  277.2 9.4 %collective-permute-start.145 = (bf16[256,256]{1,0:T(8,128)(2,1)S(1)}, bf16[256,256]{1,0:T(8,128)(2,1)S(1)}, u32[]{:S(2)}, u32[]{:S(2)}) collective-permute-start(bf16[256,256]{1,0:T(8,128)(2,1)S(1)} %get-tuple-element.101), channel_id=1, source_target_pairs={{0,4},{2,6},{4,0},{6,2},{8,12},{10,14},{12,8},{14,10},{16,20},{18,... | collective-permute-start | bytes 393224 | tf_op jit(solution)/shard_map/ppermute | solution.py:16
  278.5 10.5 %collective-permute-start.144 = (bf16[256,256]{1,0:T(8,128)(2,1)S(1)}, bf16[256,256]{1,0:T(8,128)(2,1)S(1)}, u32[]{:S(2)}, u32[]{:S(2)}) collective-permute-start(bf16[256,256]{1,0:T(8,128)(2,1)S(1)} %get-tuple-element.101), channel_id=1, source_target_pairs={{0,8},{2,10},{4,12},{6,14},{8,0},{10,2},{12,4},{14,6},{16,24},{18,... | collective-permute-start | bytes 393224 | tf_op jit(solution)/shard_map/ppermute | solution.py:16
  279.3 9.7 %collective-permute-start.143 = (bf16[256,256]{1,0:T(8,128)(2,1)S(1)}, bf16[256,256]{1,0:T(8,128)(2,1)S(1)}, u32[]{:S(2)}, u32[]{:S(2)}) collective-permute-start(bf16[256,256]{1,0:T(8,128)(2,1)S(1)} %get-tuple-element.101), channel_id=1, source_target_pairs={{0,16},{2,18},{4,20},{6,22},{8,24},{10,26},{12,28},{14,30},{16,0},... | collective-permute-start | bytes 393224 | tf_op jit(solution)/shard_map/ppermute | solution.py:16
  284.4 8.8 %collective-permute-start.125 = (bf16[384,256]{1,0:T(8,128)(2,1)S(1)}, bf16[384,256]{1,0:T(8,128)(2,1)S(1)}, u32[]{:S(2)}, u32[]{:S(2)}) collective-permute-start(bf16[384,256]{1,0:T(8,128)(2,1)S(1)} %get-tuple-element.109), channel_id=1, source_target_pairs={{0,8},{2,10},{4,12},{6,14},{8,0},{10,2},{12,4},{14,6},{16,24},{18,... | collective-permute-start | bytes 589832 | tf_op jit(solution)/shard_map/ppermute | solution.py:16
  285.1 8.2 %collective-permute-start.126 = (bf16[384,256]{1,0:T(8,128)(2,1)S(1)}, bf16[384,256]{1,0:T(8,128)(2,1)S(1)}, u32[]{:S(2)}, u32[]{:S(2)}) collective-permute-start(bf16[384,256]{1,0:T(8,128)(2,1)S(1)} %get-tuple-element.108), channel_id=1, source_target_pairs={{0,4},{2,6},{4,0},{6,2},{8,12},{10,14},{12,8},{14,10},{16,20},{18,... | collective-permute-start | bytes 589832 | tf_op jit(solution)/shard_map/ppermute | solution.py:16
  286.7 19.8 %collective-permute-start.124 = (bf16[1024,256]{1,0:T(8,128)(2,1)S(1)}, bf16[1024,256]{1,0:T(8,128)(2,1)S(1)}, u32[]{:S(2)}, u32[]{:S(2)}) collective-permute-start(bf16[1024,256]{1,0:T(8,128)(2,1)S(1)} %pad_maximum_fusion.11.refs_0_), channel_id=1, source_target_pairs={{0,2},{2,0},{4,6},{6,4},{8,10},{10,8},{12,14},{14,12},{16,18},{18,... | collective-permute-start | bytes 1572872 | tf_op jit(solution)/shard_map/ppermute | solution.py:16
  293.3 16.1 %collective-permute-start.146 = (bf16[1024,256]{1,0:T(8,128)(2,1)S(1)}, bf16[1024,256]{1,0:T(8,128)(2,1)S(1)}, u32[]{:S(2)}, u32[]{:S(2)}) collective-permute-start(bf16[1024,256]{1,0:T(8,128)(2,1)S(1)} %pad_maximum_fusion.13.refs_0_), channel_id=1, source_target_pairs={{0,2},{2,0},{4,6},{6,4},{8,10},{10,8},{12,14},{14,12},{16,18},{18,... | collective-permute-start | bytes 1572872 | tf_op jit(solution)/shard_map/ppermute | solution.py:16
  296.8 9.6 %collective-permute-start.127 = (bf16[768,256]{1,0:T(8,128)(2,1)S(1)}, bf16[768,256]{1,0:T(8,128)(2,1)S(1)}, u32[]{:S(2)}, u32[]{:S(2)}) collective-permute-start(bf16[768,256]{1,0:T(8,128)(2,1)S(1)} %constant_dynamic-update-slice_fusion.44.refs_2_), channel_id=1, source_target_pairs={{0,2},{2,0},{4,6},{6,4},{8,10},{10,8},{12,14},{14,12},{16,18},{18,... | collective-permute-start | bytes 1179656 | tf_op jit(solution)/shard_map/ppermute | solution.py:16
  (122 other events, 953.5 us)

commit v2 on v0

v2 whole, which is shorter than its diff:
```python
import functools

import jax
import jax.numpy as jnp
from jax import lax
from jax.experimental import pallas as pl
from jax.experimental.pallas import tpu as pltpu
from jax.sharding import PartitionSpec as P

VMEM = pl.BlockSpec(memory_space=pltpu.VMEM)
ANY = pl.BlockSpec(memory_space=pl.ANY)
MIB = 1024 * 1024


def pair_index(target, source):
    return target * (target - 1) // 2 + source


def swap(block, rows, even, odd=None):
    odd = even if odd is None else odd
    return lax.ppermute(block, "rows", [(i, i ^ (odd if i % 2 else even)) for i in range(rows)])


def local_call(kernel, out_shape, operands, after, limit, cost=None):
    return pl.pallas_call(
        kernel,
        out_shape=out_shape,
        in_specs=[VMEM] * len(operands) + [ANY] * len(after),
        out_specs=tuple(VMEM for _ in out_shape),
        compiler_params=pltpu.CompilerParams(vmem_limit_bytes=limit * MIB),
        cost_estimate=pl.CostEstimate(flops=cost or 0, bytes_accessed=1024, transcendentals=0),
    )(*operands, *after)


def pack_kernel(sources, layout, *refs):
    for out_ref, spans in zip(refs[len(refs) - len(layout) :], layout):
        at = 0
        for source, start, count in spans:
            out_ref[at : at + count] = refs[source][start : start + count]
            at += count


def pack(sources, layout, after):
    columns, dtype = sources[0].shape[1], sources[0].dtype
    shapes = tuple(jax.ShapeDtypeStruct((sum(span[2] for span in spans), columns), dtype) for spans in layout)
    return local_call(functools.partial(pack_kernel, len(sources), layout), shapes, sources, after, 6)


class Gather:
    def __init__(self, block, rows):
        self.block, self.rows = block, rows
        self.height = block.shape[0]
        self.half = self.height // 2
        self.pieces = []
        self.split = rows == 16
        if self.split:
            self.far, self.near, self.side = (swap(block, rows, mask) for mask in (8, 4, 2))
        else:
            self.pieces.append((lax.all_gather(block, "rows", axis=0, tiled=True), None))

    def add(self, array, parts):
        self.pieces.append((array, parts))
        self.pieces.append((swap(array, self.rows, 1), [(mask + 1, start, count) for mask, start, count in parts]))

    def second(self, after):
        height, half = self.height, self.half
        self.for_near, self.for_side = pack(
            [self.far, self.near, self.side],
            [[(0, 0, height), (2, 0, half)], [(0, 0, height), (1, half, half)]],
            after,
        )
        self.by_near = swap(self.for_near, self.rows, 4)
        self.by_side = swap(self.for_side, self.rows, 2)

    def joining(self):
        return [self.block, self.far, self.near, self.side, self.by_near, self.by_side] if self.split else []

    def third(self, joined, other):
        height, half = self.height, self.half
        self.add(
            joined,
            [(mask, 0, height) for mask in (0, 8, 4, 2)]
            + [(12, 0, height), (6, 0, half), (10, 0, height), (6, half, half)],
        )
        self.last = swap(other, self.rows, 2, 4)

    def fourth(self):
        height = self.height
        (self.tail,) = pack([self.last], [[(0, 0, height)]], [])
        self.add(self.tail, [(14, 0, height)])


def product_kernel(parts, has_total, factor_ref, *refs):
    own_row, own_group = lax.axis_index("rows"), lax.axis_index("cols")
    groups, height, _ = factor_ref.shape
    send_ref, keep_ref, vector_ref = refs[-3:]
    for piece_ref, spans in zip(refs, parts):
        if spans is None:
            vector_ref[...] = piece_ref[...]
            continue
        at = 0
        for mask, start, count in spans:
            place = pl.multiple_of((own_row ^ mask) * height + start, count)
            vector_ref[pl.ds(place, count)] = piece_ref[at : at + count]
            at += count
    vector = vector_ref[...]
    for turn in range(groups):
        group = lax.rem(own_group + 1 + turn, groups)
        span = pl.ds(turn * height, height)
        result = jnp.dot(factor_ref[group], vector, preferred_element_type=jnp.float32)
        if has_total:
            result = result + refs[len(parts)][span]
        if turn < groups - 1:
            send_ref[span] = result.astype(send_ref.dtype)
        else:
            keep_ref[...] = result


def total_kernel(has_total, factor_ref, vector_ref, *refs):
    own_group = lax.axis_index("cols")
    groups, height, _ = factor_ref.shape
    vector = vector_ref[...]
    for turn in range(groups):
        group = lax.rem(own_group + 1 + turn, groups)
        span = pl.ds(turn * height, height)
        result = jnp.dot(factor_ref[group], vector, preferred_element_type=jnp.float32)
        refs[-1][span] = result + refs[0][span] if has_total else result


def product(factor, pieces, total, after):
    groups, height, width = factor.shape
    columns = pieces[0][0].shape[1]
    given = [] if total is None else [total]
    return local_call(
        functools.partial(product_kernel, [spans for _, spans in pieces], len(given)),
        (
            jax.ShapeDtypeStruct(((groups - 1) * height, columns), jnp.bfloat16),
            jax.ShapeDtypeStruct((height, columns), jnp.float32),
            jax.ShapeDtypeStruct((width, columns), jnp.bfloat16),
        ),
        [factor, *(array for array, _ in pieces), *given],
        after,
        14,
    )


def add_product(factor, vector, total):
    groups, height, width = factor.shape
    columns = vector.shape[1]
    given = [] if total is None else [total]
    return local_call(
        functools.partial(total_kernel, len(given)),
        (jax.ShapeDtypeStruct((groups * height, columns), jnp.float32),),
        [factor, vector, *given],
        [],
        14,
        2 * groups * height * width * columns,
    )[0]


def fold_kernel(shares, has_right, joins, keep_ref, *refs):
    total = keep_ref[...]
    for share_ref in refs[:shares]:
        total = total + share_ref[...].astype(jnp.float32)
    outs = list(refs[shares + has_right + joins :])
    if has_right:
        outs.pop(0)[...] = (refs[shares][...] - total).astype(jnp.bfloat16)
    else:
        outs.pop(0)[...] = total.astype(jnp.bfloat16)
        outs.pop(0)[...] = total
    if joins:
        joined_ref, other_ref = outs
        sources = refs[shares + has_right :][:joins]
        at = 0
        for source_ref in sources:
            count = source_ref.shape[0]
            joined_ref[at : at + count] = source_ref[...]
            at += count
        is_odd = lax.rem(lax.axis_index("rows"), 2) == 1
        height = other_ref.shape[0]
        other_ref[...] = jnp.where(is_odd, sources[5][:height], sources[4][:height])


def fold(keep, shares, right, joining):
    rounded = jax.ShapeDtypeStruct(keep.shape, jnp.bfloat16)
    given = [] if right is None else [right]
    out_shape = [rounded]
    if right is None:
        out_shape.append(jax.ShapeDtypeStruct(keep.shape, jnp.float32))
    if joining:
        rows, columns = sum(array.shape[0] for array in joining), keep.shape[1]
        out_shape.append(jax.ShapeDtypeStruct((rows, columns), jnp.bfloat16))
        out_shape.append(jax.ShapeDtypeStruct(keep.shape, jnp.bfloat16))
    kernel = functools.partial(fold_kernel, len(shares), len(given), len(joining))
    return list(local_call(kernel, tuple(out_shape), [keep, *shares, *given, *joining], [], 8))


def start_third(joining):
    height = joining[0].shape[0]
    is_odd = lax.rem(lax.axis_index("rows"), 2) == 1
    (joined,) = pack(joining, [[(i, 0, array.shape[0]) for i, array in enumerate(joining)]], [])
    return joined, jnp.where(is_odd, joining[5][:height], joining[4][:height])


def forward_solve(rows, cols, right_side, inverse_blocks, lower_blocks):
    panels, _, height, columns = right_side.shape
    chunks = 2 if rows == 16 and cols == 2 else 1
    width = columns // chunks
    steps = 2 * panels - 1
    solved = [[None] * chunks for _ in range(panels)]
    totals = [{} for _ in range(chunks)]
    factors = {}

    def right(current, chunk):
        return right_side[current, 0, :, chunk * width : (chunk + 1) * width]

    def load(step, after):
        current = step // 2
        blocks = inverse_blocks if step % 2 == 0 else lower_blocks
        if after is not None:
            blocks, _ = lax.optimization_barrier((blocks, after))
        if step % 2 == 0:
            loaded = {current: blocks[current]}
        else:
            loaded = {later: blocks[pair_index(later, current)] for later in range(current + 1, panels)}
        factors[step] = loaded
        return list(loaded.values())

    def multiply(step, chunk, gather, after):
        current, solving = step // 2, step % 2 == 0
        first = current if solving else current + 1
        total = None if solving else totals[chunk].pop(first, None)
        sends, keep, vector = product(factors[step][first], gather.pieces, total, after)
        made = []
        if not solving:
            for later in range(current + 2, panels):
                old = totals[chunk].get(later)
                totals[chunk][later] = add_product(factors[step][later], vector, old)
                made.append(totals[chunk][later])
        return sends, keep, made

    def finish(step, chunk, sends, keep, following):
        current, solving = step // 2, step % 2 == 0
        shares = []
        for turn in range(1, cols):
            share = sends[(turn - 1) * height : turn * height]
            shares.append(lax.ppermute(share, "cols", [(i, (i + turn) % cols) for i in range(cols)]))
        joining = following.joining() if following else []
        made = fold(keep, shares, None if solving else right(current + 1, chunk), joining)
        vectors[chunk] = made.pop(0)
        if solving:
            solved[current][chunk] = made.pop(0)
        if joining:
            following.third(*made)

    vectors = [right(0, chunk).astype(jnp.bfloat16) for chunk in range(chunks)]
    load(0, None)
    if chunks == 1:
        for step in range(steps):
            if step + 1 < steps:
                load(step + 1, vectors[0])
            sends, keep, _ = multiply(step, 0, Gather(vectors[0], rows), [])
            finish(step, 0, sends, keep, None)
    else:
        made = []
        gather = Gather(vectors[0], rows)
        gather.second([])
        gather.third(*start_third(gather.joining()))
        for step in range(steps):
            for chunk in range(chunks):
                other = 1 - chunk
                following = None
                gather.fourth()
                if step + chunk < steps:
                    following = Gather(vectors[other], rows)
                    loaded = load(step + 1, vectors[other]) if chunk == 0 and step + 1 < steps else []
                    following.second([gather.tail, *made, *loaded])
                sends, keep, made = multiply(step, chunk, gather, [following.for_near] if following else [])
                finish(step, chunk, sends, keep, following)
                gather = following
    return jnp.stack([jnp.concatenate(part, axis=1) for part in solved])[:, None]


def solution(mesh):
    return jax.shard_map(
        functools.partial(forward_solve, mesh.shape["rows"], mesh.shape["cols"]),
        mesh=mesh,
        in_specs=(
            P(None, "cols", "rows", None),
            P(None, None, "rows", "cols"),
            P(None, None, "rows", "cols"),
        ),
        out_specs=P(None, "cols", "rows", None),
        check_vma=False,
    )
```

time: 587 us -> 287 us (0.49)
  waiting for transfers between devices: 492 us -> 100 us
  starting transfers between devices: 0.73 us -> 126 us
  matrix products: 62.9 us -> 0 us
  Pallas kernels: 0 us -> 33.1 us
  local copies, waits for them, and re-layouts: 3.86 us -> 22.2 us
  between operations: 13.4 us -> 0.71 us
  other arithmetic: 13.3 us -> 3.47 us
    all_gather x7 -> x0, waiting for transfers between devices: 362 us -> none  [the longest x4 215 us: forward_solve(): lax.all_gather(residual, 'rows', axis=1, tiled=True)]
    reduce_scatter x7 -> x0, waiting for transfers between devices: 129 us -> none  [the longest x4 74.8 us: forward_solve(): solved = lax.psum_scatter(products, 'cols', scatter_dimension=0, tiled=True)]
    ppermute x0 -> x126, starting transfers between devices: none -> 126 us  [the longest x112 105 us: swap(): lax.ppermute(block, 'rows', [(i, i ^ (odd if i % 2 else even)) for i in r...]
    ppermute x0 -> x126, waiting for transfers between devices: none -> 100 us  [the longest x112 77.1 us: swap(): lax.ppermute(block, 'rows', [(i, i ^ (odd if i % 2 else even)) for i in r...]
    dot_general x10 -> x0, matrix products: 62.9 us -> none  [the longest x6 35.8 us: product(): jnp.einsum('abk,kn->abn', factor_block, rows_all, preferred_element_type=...]
    pallas_call x0 -> x63, Pallas kernels: none -> 33.1 us  [local_call(): pl.pallas_call(kernel, out_shape=out_shape, in_specs=[VMEM] * len(operand...]
    squeeze x0 -> x8, local copies, waits for them, and re-layouts: none -> 22.2 us  [the longest x3 12 us: load(): blocks[pair_index(later, current)]]
    convert_element_type x6 -> x0, other arithmetic: 10.7 us -> none  [the longest x3 5.39 us: forward_solve(): residual = (right_side[current] - shares).astype(jnp.bfloat16)]
  transfers between devices with their start and end apart: 14 -> 126, of which waited for: 14 -> 68; matrix products, arithmetic and copies ran while one was open for 1% -> 8% of each run, Pallas kernels for 0% -> 10%
where the time goes in v2:
time: 287 us; the launch traced here: 286 us
  starting transfers between devices  126 us (44%)
  waiting for transfers between devices  100 us (35%)
  Pallas kernels  33.1 us (12%)
  local copies, waits for them, and re-layouts  22.2 us (8%)
  other arithmetic  3.47 us (1%)
    ppermute x112, starting transfers between devices, swap(): lax.ppermute(block, 'rows', [(i, i ^ (odd if i % 2 else even)) for i in r...  105 us
    ppermute x112, waiting for transfers between devices, swap(): lax.ppermute(block, 'rows', [(i, i ^ (odd if i % 2 else even)) for i in r...  77.1 us
    pallas_call x63, Pallas kernels, local_call(): pl.pallas_call(kernel, out_shape=out_shape, in_specs=[VMEM] * len(operand...  33.1 us
    ppermute x14, waiting for transfers between devices, finish(): lax.ppermute(share, 'cols', [(i, (i + turn) % cols) for i in range(cols)])  23.4 us
    ppermute x14, starting transfers between devices, finish(): lax.ppermute(share, 'cols', [(i, (i + turn) % cols) for i in range(cols)])  21.8 us
    squeeze x3, local copies, waits for them, and re-layouts, load(): blocks[pair_index(later, current)]  12 us
    squeeze x4, local copies, waits for them, and re-layouts, load(): loaded = {current: blocks[current]}  10.1 us
  transfers between devices with their start and end apart: 126, of which 68 were waited for; matrix products, arithmetic and copies ran while one was open for 8% of the time, Pallas kernels for 10%

profile of v2, /device:TPU:0, one launch (start us, length us, event | category | flops | bytes accessed | tf_op | source)
XLA Modules:
  0.0 286.4 jit_solution(10527411831763862012)
XLA Ops:
  0.0 1.7 convert.4
  1.8 4.1 %collective-permute-start = (bf16[256,256]{1,0:T(8,128)(2,1)S(1)}, bf16[256,256]{1,0:T(8,128)(2,1)S(1)}, u32[]{:S(2)}, u32[]{:S(2)}) collective-permute-start(bf16[256,256]{1,0:T(8,128)(2,1)S(1)} %get-tuple-element.241.refs_0_), channel_id=1, source_target_pairs={{0,16},{2,18},{4,20},{6,22},{8,24},{10,26},{12,28},{14,30},{16,0},... | collective-permute-start | bytes 393224 | tf_op jit(solution)/shard_map/ppermute | solution.py:21
  5.9 1.6 collective-permute-start.1
  8.9 3.3 %collective-permute-done.refs_0_.refs_1_ = bf16[256,256]{1,0:T(8,128)(2,1)S(1)} collective-permute-done((bf16[256,256]{1,0:T(8,128)(2,1)S(1)}, bf16[256,256]{1,0:T(8,128)(2,1)S(1)}, u32[]{:S(2)}, u32[]{:S(2)}) %collective-permute-start) | collective-permute-done | bytes 131104 | tf_op jit(solution)/shard_map/ppermute | solution.py:21
  15.5 2.4 collective-permute-start.8
  19.7 3.9 %collective-permute-start.6 = (bf16[256,256]{1,0:T(8,128)(2,1)S(1)}, bf16[256,256]{1,0:T(8,128)(2,1)S(1)}, u32[]{:S(2)}, u32[]{:S(2)}) collective-permute-start(bf16[256,256]{1,0:T(8,128)(2,1)S(1)} %slice_select_fusion), channel_id=1, source_target_pairs={{0,4},{2,10},{4,0},{6,14},{8,12},{10,2},{12,8},{14,6},{16,20},{18,... | collective-permute-start | bytes 393224 | tf_op jit(solution)/shard_map/ppermute | solution.py:21
  23.6 5.5 %slice_bitcast_fusion.6 = (bf16[2,256,4096]{2,1,0:T(8,128)(2,1)S(1)}, bf16[2,256,4096]{2,1,0:T(8,128)(2,1)S(1)}, bf16[2,256,4096]{2,1,0:T(8,128)(2,1)S(1)}) fusion(bf16[6,2,256,4096]{3,2,1,0:T(8,128)(2,1)} %param.5), kind=kLoop, calls=%fused_computation.6 | loop fusion | bytes 25165824 | tf_op jit(solution)/shard_map/squeeze | solution.py:225
  30.0 2.5 slice_bitcast_fusion.9.factor_ref
  32.5 1.6 shard_map.41
  36.8 2.7 collective-permute-done.11.refs_0_
  39.8 1.8 collective-permute-start.15
  41.5 4.7 %collective-permute-start.17 = (bf16[256,256]{1,0:T(8,128)(2,1)S(1)}, bf16[256,256]{1,0:T(8,128)(2,1)S(1)}, u32[]{:S(2)}, u32[]{:S(2)}) collective-permute-start(bf16[256,256]{1,0:T(8,128)(2,1)S(1)} %get-tuple-element.127.refs_1_), channel_id=1, source_target_pairs={{0,16},{2,18},{4,20},{6,22},{8,24},{10,26},{12,28},{14,30},{16,0},... | collective-permute-start | bytes 393224 | tf_op jit(solution)/shard_map/ppermute | solution.py:21
  47.6 3.5 %collective-permute-done.17.refs_0_.refs_2_ = bf16[256,256]{1,0:T(8,128)(2,1)S(1)} collective-permute-done((bf16[256,256]{1,0:T(8,128)(2,1)S(1)}, bf16[256,256]{1,0:T(8,128)(2,1)S(1)}, u32[]{:S(2)}, u32[]{:S(2)}) %collective-permute-start.17) | collective-permute-done | bytes 131104 | tf_op jit(solution)/shard_map/ppermute | solution.py:21
  51.8 1.8 collective-permute-start.21
  55.0 1.6 shard_map.45
  59.5 2.1 collective-permute-done.20.refs_0_
  62.4 2.3 collective-permute-start.26
  67.4 2.7 slice_bitcast_fusion.5.refs_4_.factor_ref
  74.4 1.6 collective-permute-start.29
  80.7 1.5 collective-permute-start.35
  87.3 2.3 collective-permute-done.35.refs_0_.refs_3_
  93.3 1.6 collective-permute-start.38
  94.9 1.8 collective-permute-done.39.refs_6_
  96.8 1.6 collective-permute-done.38.refs_0_
  101.9 2.4 collective-permute-start.44
  106.3 4.0 %slice_bitcast_fusion.3 = (bf16[2,256,4096]{2,1,0:T(8,128)(2,1)S(1)}, bf16[2,256,4096]{2,1,0:T(8,128)(2,1)S(1)}) fusion(bf16[6,2,256,4096]{3,2,1,0:T(8,128)(2,1)} %param.5), kind=kLoop, calls=%fused_computation.3 | loop fusion | bytes 16777216 | tf_op jit(solution)/shard_map/squeeze | solution.py:225
  113.1 1.6 shard_map.61
  114.7 1.5 collective-permute-start.47
  125.0 5.1 %collective-permute-done.53.refs_0_.refs_2_ = bf16[256,256]{1,0:T(8,128)(2,1)S(1)} collective-permute-done((bf16[256,256]{1,0:T(8,128)(2,1)S(1)}, bf16[256,256]{1,0:T(8,128)(2,1)S(1)}, u32[]{:S(2)}, u32[]{:S(2)}) %collective-permute-start.53) | collective-permute-done | bytes 131104 | tf_op jit(solution)/shard_map/ppermute | solution.py:21
  131.5 1.6 shard_map.65
  133.2 1.5 collective-permute-start.56
  134.7 2.0 collective-permute-done.57.refs_5_
  138.3 1.6 collective-permute-start.60
  142.8 1.7 collective-permute-done.60.refs_0_
  144.6 2.5 slice_bitcast_fusion.2.refs_4_.factor_ref
  151.1 1.6 collective-permute-start.65
  152.7 1.8 collective-permute-done.66.refs_6_
  157.3 1.6 collective-permute-start.71
  163.8 3.0 %collective-permute-done.71.refs_0_.refs_3_ = bf16[256,256]{1,0:T(8,128)(2,1)S(1)} collective-permute-done((bf16[256,256]{1,0:T(8,128)(2,1)S(1)}, bf16[256,256]{1,0:T(8,128)(2,1)S(1)}, u32[]{:S(2)}, u32[]{:S(2)}) %collective-permute-start.71) | collective-permute-done | bytes 131104 | tf_op jit(solution)/shard_map/ppermute | solution.py:21
  170.0 1.6 collective-permute-start.74
  177.5 2.2 collective-permute-start.80
  181.8 2.5 slice_bitcast_fusion.1.refs_5_.factor_ref
  187.4 1.6 shard_map.79
  192.5 1.6 collective-permute-done.83.refs_0_
  199.4 5.2 %collective-permute-done.89.refs_0_.refs_2_ = bf16[256,256]{1,0:T(8,128)(2,1)S(1)} collective-permute-done((bf16[256,256]{1,0:T(8,128)(2,1)S(1)}, bf16[256,256]{1,0:T(8,128)(2,1)S(1)}, u32[]{:S(2)}, u32[]{:S(2)}) %collective-permute-start.89) | collective-permute-done | bytes 131104 | tf_op jit(solution)/shard_map/ppermute | solution.py:21
  206.7 1.9 shard_map.83
  208.6 1.6 collective-permute-start.92
  211.4 2.1 collective-permute-done.92.refs_0_
  214.5 1.8 collective-permute-start.98
  218.2 1.7 collective-permute-done.96.refs_0_
  220.0 2.5 slice_bitcast_fusion.refs_4_.factor_ref
  224.4 1.6 shard_map.87
  226.1 1.6 collective-permute-start.101
  227.7 2.2 collective-permute-done.102.refs_6_
  236.7 5.2 %collective-permute-done.107.refs_0_.refs_3_ = bf16[256,256]{1,0:T(8,128)(2,1)S(1)} collective-permute-done((bf16[256,256]{1,0:T(8,128)(2,1)S(1)}, bf16[256,256]{1,0:T(8,128)(2,1)S(1)}, u32[]{:S(2)}, u32[]{:S(2)}) %collective-permute-start.107) | collective-permute-done | bytes 131104 | tf_op jit(solution)/shard_map/ppermute | solution.py:21
  244.1 1.6 shard_map.91
  245.7 1.6 collective-permute-start.110
  248.8 1.8 collective-permute-done.110.refs_0_
  256.0 5.4 %collective-permute-done.116.refs_0_.refs_2_ = bf16[256,256]{1,0:T(8,128)(2,1)S(1)} collective-permute-done((bf16[256,256]{1,0:T(8,128)(2,1)S(1)}, bf16[256,256]{1,0:T(8,128)(2,1)S(1)}, u32[]{:S(2)}, u32[]{:S(2)}) %collective-permute-start.116) | collective-permute-done | bytes 131104 | tf_op jit(solution)/shard_map/ppermute | solution.py:21
  263.2 1.6 shard_map.95
  266.3 1.6 collective-permute-done.120.refs_5_
  271.7 3.8 %collective-permute-done.123.refs_0_ = bf16[256,256]{1,0:T(8,128)(2,1)S(1)} collective-permute-done((bf16[256,256]{1,0:T(8,128)(2,1)S(1)}, bf16[256,256]{1,0:T(8,128)(2,1)S(1)}, u32[]{:S(2)}, u32[]{:S(2)}) %collective-permute-start.123) | collective-permute-done | bytes 131104 | tf_op jit(solution)/shard_map/ppermute | solution.py:21
  276.9 1.6 shard_map.98
  280.3 3.9 %collective-permute-done.125.refs_0_ = bf16[256,256]{1,0:T(8,128)(2,1)S(1)} collective-permute-done((bf16[256,256]{1,0:T(8,128)(2,1)S(1)}, bf16[256,256]{1,0:T(8,128)(2,1)S(1)}, u32[]{:S(2)}, u32[]{:S(2)}) %collective-permute-start.125) | collective-permute-done | bytes 131104 | tf_op jit(solution)/shard_map/ppermute | solution.py:247
  (269 shorter events, 132.1 us)
Async XLA Ops:
  1.8 10.5 %collective-permute-start = (bf16[256,256]{1,0:T(8,128)(2,1)S(1)}, bf16[256,256]{1,0:T(8,128)(2,1)S(1)}, u32[]{:S(2)}, u32[]{:S(2)}) collective-permute-start(bf16[256,256]{1,0:T(8,128)(2,1)S(1)} %get-tuple-element.241.refs_0_), channel_id=1, source_target_pairs={{0,16},{2,18},{4,20},{6,22},{8,24},{10,26},{12,28},{14,30},{16,0},... | collective-permute-start | bytes 393224 | tf_op jit(solution)/shard_map/ppermute | solution.py:21
  5.9 6.6 %collective-permute-start.1 = (bf16[256,256]{1,0:T(8,128)(2,1)S(1)}, bf16[256,256]{1,0:T(8,128)(2,1)S(1)}, u32[]{:S(2)}, u32[]{:S(2)}) collective-permute-start(bf16[256,256]{1,0:T(8,128)(2,1)S(1)} %get-tuple-element.241.refs_0_), channel_id=1, source_target_pairs={{0,8},{2,10},{4,12},{6,14},{8,0},{10,2},{12,4},{14,6},{16,24},{18,... | collective-permute-start | bytes 393224 | tf_op jit(solution)/shard_map/ppermute | solution.py:21
  15.5 14.3 %collective-permute-start.8 = (bf16[256,256]{1,0:T(8,128)(2,1)S(1)}, bf16[256,256]{1,0:T(8,128)(2,1)S(1)}, u32[]{:S(2)}, u32[]{:S(2)}) collective-permute-start(bf16[256,256]{1,0:T(8,128)(2,1)S(1)} %get-tuple-element.240.refs_1_), channel_id=1, source_target_pairs={{0,16},{2,18},{4,20},{6,22},{8,24},{10,26},{12,28},{14,30},{16,0},... | collective-permute-start | bytes 393224 | tf_op jit(solution)/shard_map/ppermute | solution.py:21
  17.9 11.9 %collective-permute-start.9 = (bf16[256,256]{1,0:T(8,128)(2,1)S(1)}, bf16[256,256]{1,0:T(8,128)(2,1)S(1)}, u32[]{:S(2)}, u32[]{:S(2)}) collective-permute-start(bf16[256,256]{1,0:T(8,128)(2,1)S(1)} %get-tuple-element.240.refs_1_), channel_id=1, source_target_pairs={{0,8},{2,10},{4,12},{6,14},{8,0},{10,2},{12,4},{14,6},{16,24},{18,... | collective-permute-start | bytes 393224 | tf_op jit(solution)/shard_map/ppermute | solution.py:21
  17.9 11.9 %collective-permute-start.10 = (bf16[256,256]{1,0:T(8,128)(2,1)S(1)}, bf16[256,256]{1,0:T(8,128)(2,1)S(1)}, u32[]{:S(2)}, u32[]{:S(2)}) collective-permute-start(bf16[256,256]{1,0:T(8,128)(2,1)S(1)} %get-tuple-element.240.refs_1_), channel_id=1, source_target_pairs={{0,4},{2,6},{4,0},{6,2},{8,12},{10,14},{12,8},{14,10},{16,20},{18,... | collective-permute-start | bytes 393224 | tf_op jit(solution)/shard_map/ppermute | solution.py:21
  19.7 9.5 %collective-permute-start.6 = (bf16[256,256]{1,0:T(8,128)(2,1)S(1)}, bf16[256,256]{1,0:T(8,128)(2,1)S(1)}, u32[]{:S(2)}, u32[]{:S(2)}) collective-permute-start(bf16[256,256]{1,0:T(8,128)(2,1)S(1)} %slice_select_fusion), channel_id=1, source_target_pairs={{0,4},{2,10},{4,0},{6,14},{8,12},{10,2},{12,8},{14,6},{16,20},{18,... | collective-permute-start | bytes 393224 | tf_op jit(solution)/shard_map/ppermute | solution.py:21
  29.8 6.9 %collective-permute-start.12 = (bf16[384,256]{1,0:T(8,128)(2,1)S(1)}, bf16[384,256]{1,0:T(8,128)(2,1)S(1)}, u32[]{:S(2)}, u32[]{:S(2)}) collective-permute-start(bf16[384,256]{1,0:T(8,128)(2,1)S(1)} %get-tuple-element.120.refs_4_), channel_id=1, source_target_pairs={{0,8},{2,10},{4,12},{6,14},{8,0},{10,2},{12,4},{14,6},{16,24},{18,... | collective-permute-start | bytes 589832 | tf_op jit(solution)/shard_map/ppermute | solution.py:21
  29.9 6.9 %collective-permute-start.13 = (bf16[384,256]{1,0:T(8,128)(2,1)S(1)}, bf16[384,256]{1,0:T(8,128)(2,1)S(1)}, u32[]{:S(2)}, u32[]{:S(2)}) collective-permute-start(bf16[384,256]{1,0:T(8,128)(2,1)S(1)} %get-tuple-element.123), channel_id=1, source_target_pairs={{0,4},{2,6},{4,0},{6,2},{8,12},{10,14},{12,8},{14,10},{16,20},{18,... | collective-permute-start | bytes 589832 | tf_op jit(solution)/shard_map/ppermute | solution.py:21
  39.7 15.3 %collective-permute-start.14 = (bf16[1792,256]{1,0:T(8,128)(2,1)S(1)}, bf16[1792,256]{1,0:T(8,128)(2,1)S(1)}, u32[]{:S(2)}, u32[]{:S(2)}) collective-permute-start(bf16[1792,256]{1,0:T(8,128)(2,1)S(1)} %get-tuple-element.125.refs_0_), channel_id=1, source_target_pairs={{0,2},{2,0},{4,6},{6,4},{8,10},{10,8},{12,14},{14,12},{16,18},{18,... | collective-permute-start | bytes 2752520 | tf_op jit(solution)/shard_map/ppermute | solution.py:21
  39.8 7.3 %collective-permute-start.15 = (bf16[256,256]{1,0:T(8,128)(2,1)S(1)}, bf16[256,256]{1,0:T(8,128)(2,1)S(1)}, u32[]{:S(2)}, u32[]{:S(2)}) collective-permute-start(bf16[256,256]{1,0:T(8,128)(2,1)S(1)} %get-tuple-element.126), channel_id=1, source_target_pairs={{0,4},{2,10},{4,0},{6,14},{8,12},{10,2},{12,8},{14,6},{16,20},{18,... | collective-permute-start | bytes 393224 | tf_op jit(solution)/shard_map/ppermute | solution.py:21
  41.5 9.6 %collective-permute-start.17 = (bf16[256,256]{1,0:T(8,128)(2,1)S(1)}, bf16[256,256]{1,0:T(8,128)(2,1)S(1)}, u32[]{:S(2)}, u32[]{:S(2)}) collective-permute-start(bf16[256,256]{1,0:T(8,128)(2,1)S(1)} %get-tuple-element.127.refs_1_), channel_id=1, source_target_pairs={{0,16},{2,18},{4,20},{6,22},{8,24},{10,26},{12,28},{14,30},{16,0},... | collective-permute-start | bytes 393224 | tf_op jit(solution)/shard_map/ppermute | solution.py:21
  47.0 8.0 %collective-permute-start.16 = (bf16[256,256]{1,0:T(8,128)(2,1)S(1)}, bf16[256,256]{1,0:T(8,128)(2,1)S(1)}, u32[]{:S(2)}, u32[]{:S(2)}) collective-permute-start(bf16[256,256]{1,0:T(8,128)(2,1)S(1)} %shard_map.43.refs_3_.refs_2_), channel_id=1, source_target_pairs={{0,2},{2,0},{4,6},{6,4},{8,10},{10,8},{12,14},{14,12},{16,18},{18,... | collective-permute-start | bytes 393224 | tf_op jit(solution)/shard_map/ppermute | solution.py:21
  62.4 7.9 %collective-permute-start.26 = (bf16[256,256]{1,0:T(8,128)(2,1)S(1)}, bf16[256,256]{1,0:T(8,128)(2,1)S(1)}, u32[]{:S(2)}, u32[]{:S(2)}) collective-permute-start(bf16[256,256]{1,0:T(8,128)(2,1)S(1)} %get-tuple-element.133.refs_2_), channel_id=1, source_target_pairs={{0,16},{2,18},{4,20},{6,22},{8,24},{10,26},{12,28},{14,30},{16,0},... | collective-permute-start | bytes 393224 | tf_op jit(solution)/shard_map/ppermute | solution.py:21
  66.2 6.7 %collective-permute-start.23 = (bf16[1792,256]{1,0:T(8,128)(2,1)S(1)}, bf16[1792,256]{1,0:T(8,128)(2,1)S(1)}, u32[]{:S(2)}, u32[]{:S(2)}) collective-permute-start(bf16[1792,256]{1,0:T(8,128)(2,1)S(1)} %get-tuple-element.135.refs_0_), channel_id=1, source_target_pairs={{0,2},{2,0},{4,6},{6,4},{8,10},{10,8},{12,14},{14,12},{16,18},{18,... | collective-permute-start | bytes 2752520 | tf_op jit(solution)/shard_map/ppermute | solution.py:21
  70.8 6.7 %collective-permute-start.30 = (bf16[384,256]{1,0:T(8,128)(2,1)S(1)}, bf16[384,256]{1,0:T(8,128)(2,1)S(1)}, u32[]{:S(2)}, u32[]{:S(2)}) collective-permute-start(bf16[384,256]{1,0:T(8,128)(2,1)S(1)} %get-tuple-element.137.refs_4_), channel_id=1, source_target_pairs={{0,8},{2,10},{4,12},{6,14},{8,0},{10,2},{12,4},{14,6},{16,24},{18,... | collective-permute-start | bytes 589832 | tf_op jit(solution)/shard_map/ppermute | solution.py:21
  71.8 6.8 %collective-permute-start.31 = (bf16[384,256]{1,0:T(8,128)(2,1)S(1)}, bf16[384,256]{1,0:T(8,128)(2,1)S(1)}, u32[]{:S(2)}, u32[]{:S(2)}) collective-permute-start(bf16[384,256]{1,0:T(8,128)(2,1)S(1)} %get-tuple-element.140), channel_id=1, source_target_pairs={{0,4},{2,6},{4,0},{6,2},{8,12},{10,14},{12,8},{14,10},{16,20},{18,... | collective-permute-start | bytes 589832 | tf_op jit(solution)/shard_map/ppermute | solution.py:21
  79.5 12.4 %collective-permute-start.32 = (bf16[1792,256]{1,0:T(8,128)(2,1)S(1)}, bf16[1792,256]{1,0:T(8,128)(2,1)S(1)}, u32[]{:S(2)}, u32[]{:S(2)}) collective-permute-start(bf16[1792,256]{1,0:T(8,128)(2,1)S(1)} %get-tuple-element.141.refs_0_), channel_id=1, source_target_pairs={{0,2},{2,0},{4,6},{6,4},{8,10},{10,8},{12,14},{14,12},{16,18},{18,... | collective-permute-start | bytes 2752520 | tf_op jit(solution)/shard_map/ppermute | solution.py:21
  80.7 8.9 %collective-permute-start.35 = (bf16[256,256]{1,0:T(8,128)(2,1)S(1)}, bf16[256,256]{1,0:T(8,128)(2,1)S(1)}, u32[]{:S(2)}, u32[]{:S(2)}) collective-permute-start(bf16[256,256]{1,0:T(8,128)(2,1)S(1)} %get-tuple-element.143.refs_2_), channel_id=1, source_target_pairs={{0,16},{2,18},{4,20},{6,22},{8,24},{10,26},{12,28},{14,30},{16,0},... | collective-permute-start | bytes 393224 | tf_op jit(solution)/shard_map/ppermute | solution.py:21
  82.2 7.5 %collective-permute-start.36 = (bf16[256,256]{1,0:T(8,128)(2,1)S(1)}, bf16[256,256]{1,0:T(8,128)(2,1)S(1)}, u32[]{:S(2)}, u32[]{:S(2)}) collective-permute-start(bf16[256,256]{1,0:T(8,128)(2,1)S(1)} %get-tuple-element.143.refs_2_), channel_id=1, source_target_pairs={{0,8},{2,10},{4,12},{6,14},{8,0},{10,2},{12,4},{14,6},{16,24},{18,... | collective-permute-start | bytes 393224 | tf_op jit(solution)/shard_map/ppermute | solution.py:21
  89.7 7.0 %collective-permute-start.39 = (bf16[384,256]{1,0:T(8,128)(2,1)S(1)}, bf16[384,256]{1,0:T(8,128)(2,1)S(1)}, u32[]{:S(2)}, u32[]{:S(2)}) collective-permute-start(bf16[384,256]{1,0:T(8,128)(2,1)S(1)} %get-tuple-element.145.refs_4_), channel_id=1, source_target_pairs={{0,8},{2,10},{4,12},{6,14},{8,0},{10,2},{12,4},{14,6},{16,24},{18,... | collective-permute-start | bytes 589832 | tf_op jit(solution)/shard_map/ppermute | solution.py:21
  98.5 7.2 %collective-permute-start.42 = (bf16[256,256]{1,0:T(8,128)(2,1)S(1)}, bf16[256,256]{1,0:T(8,128)(2,1)S(1)}, u32[]{:S(2)}, u32[]{:S(2)}) collective-permute-start(bf16[256,256]{1,0:T(8,128)(2,1)S(1)} %get-tuple-element.150), channel_id=1, source_target_pairs={{0,4},{2,10},{4,0},{6,14},{8,12},{10,2},{12,8},{14,6},{16,20},{18,... | collective-permute-start | bytes 393224 | tf_op jit(solution)/shard_map/ppermute | solution.py:21
  101.9 8.4 %collective-permute-start.44 = (bf16[256,256]{1,0:T(8,128)(2,1)S(1)}, bf16[256,256]{1,0:T(8,128)(2,1)S(1)}, u32[]{:S(2)}, u32[]{:S(2)}) collective-permute-start(bf16[256,256]{1,0:T(8,128)(2,1)S(1)} %get-tuple-element.151.refs_1_), channel_id=1, source_target_pairs={{0,16},{2,18},{4,20},{6,22},{8,24},{10,26},{12,28},{14,30},{16,0},... | collective-permute-start | bytes 393224 | tf_op jit(solution)/shard_map/ppermute | solution.py:21
  105.7 7.4 %collective-permute-start.41 = (bf16[1792,256]{1,0:T(8,128)(2,1)S(1)}, bf16[1792,256]{1,0:T(8,128)(2,1)S(1)}, u32[]{:S(2)}, u32[]{:S(2)}) collective-permute-start(bf16[1792,256]{1,0:T(8,128)(2,1)S(1)} %get-tuple-element.149.refs_0_), channel_id=1, source_target_pairs={{0,2},{2,0},{4,6},{6,4},{8,10},{10,8},{12,14},{14,12},{16,18},{18,... | collective-permute-start | bytes 2752520 | tf_op jit(solution)/shard_map/ppermute | solution.py:21
  105.7 7.4 %collective-permute-start.43 = (bf16[256,256]{1,0:T(8,128)(2,1)S(1)}, bf16[256,256]{1,0:T(8,128)(2,1)S(1)}, u32[]{:S(2)}, u32[]{:S(2)}) collective-permute-start(bf16[256,256]{1,0:T(8,128)(2,1)S(1)} %shard_map.57.refs_3_.refs_2_), channel_id=1, source_target_pairs={{0,2},{2,0},{4,6},{6,4},{8,10},{10,8},{12,14},{14,12},{16,18},{18,... | collective-permute-start | bytes 393224 | tf_op jit(solution)/shard_map/ppermute | solution.py:21
  110.4 6.9 %collective-permute-start.48 = (bf16[384,256]{1,0:T(8,128)(2,1)S(1)}, bf16[384,256]{1,0:T(8,128)(2,1)S(1)}, u32[]{:S(2)}, u32[]{:S(2)}) collective-permute-start(bf16[384,256]{1,0:T(8,128)(2,1)S(1)} %get-tuple-element.154.refs_4_), channel_id=1, source_target_pairs={{0,8},{2,10},{4,12},{6,14},{8,0},{10,2},{12,4},{14,6},{16,24},{18,... | collective-permute-start | bytes 589832 | tf_op jit(solution)/shard_map/ppermute | solution.py:21
  111.6 6.5 %collective-permute-start.49 = (bf16[384,256]{1,0:T(8,128)(2,1)S(1)}, bf16[384,256]{1,0:T(8,128)(2,1)S(1)}, u32[]{:S(2)}, u32[]{:S(2)}) collective-permute-start(bf16[384,256]{1,0:T(8,128)(2,1)S(1)} %get-tuple-element.157), channel_id=1, source_target_pairs={{0,4},{2,6},{4,0},{6,2},{8,12},{10,14},{12,8},{14,10},{16,20},{18,... | collective-permute-start | bytes 589832 | tf_op jit(solution)/shard_map/ppermute | solution.py:21
  119.8 11.8 %collective-permute-start.50 = (bf16[1792,256]{1,0:T(8,128)(2,1)S(1)}, bf16[1792,256]{1,0:T(8,128)(2,1)S(1)}, u32[]{:S(2)}, u32[]{:S(2)}) collective-permute-start(bf16[1792,256]{1,0:T(8,128)(2,1)S(1)} %get-tuple-element.159.refs_0_), channel_id=1, source_target_pairs={{0,2},{2,0},{4,6},{6,4},{8,10},{10,8},{12,14},{14,12},{16,18},{18,... | collective-permute-start | bytes 2752520 | tf_op jit(solution)/shard_map/ppermute | solution.py:21
  120.5 9.6 %collective-permute-start.53 = (bf16[256,256]{1,0:T(8,128)(2,1)S(1)}, bf16[256,256]{1,0:T(8,128)(2,1)S(1)}, u32[]{:S(2)}, u32[]{:S(2)}) collective-permute-start(bf16[256,256]{1,0:T(8,128)(2,1)S(1)} %get-tuple-element.161.refs_1_), channel_id=1, source_target_pairs={{0,16},{2,18},{4,20},{6,22},{8,24},{10,26},{12,28},{14,30},{16,0},... | collective-permute-start | bytes 393224 | tf_op jit(solution)/shard_map/ppermute | solution.py:21
  121.7 8.4 %collective-permute-start.54 = (bf16[256,256]{1,0:T(8,128)(2,1)S(1)}, bf16[256,256]{1,0:T(8,128)(2,1)S(1)}, u32[]{:S(2)}, u32[]{:S(2)}) collective-permute-start(bf16[256,256]{1,0:T(8,128)(2,1)S(1)} %get-tuple-element.161.refs_1_), channel_id=1, source_target_pairs={{0,8},{2,10},{4,12},{6,14},{8,0},{10,2},{12,4},{14,6},{16,24},{18,... | collective-permute-start | bytes 393224 | tf_op jit(solution)/shard_map/ppermute | solution.py:21
  122.9 7.2 %collective-permute-start.55 = (bf16[256,256]{1,0:T(8,128)(2,1)S(1)}, bf16[256,256]{1,0:T(8,128)(2,1)S(1)}, u32[]{:S(2)}, u32[]{:S(2)}) collective-permute-start(bf16[256,256]{1,0:T(8,128)(2,1)S(1)} %get-tuple-element.161.refs_1_), channel_id=1, source_target_pairs={{0,4},{2,6},{4,0},{6,2},{8,12},{10,14},{12,8},{14,10},{16,20},{18,... | collective-permute-start | bytes 393224 | tf_op jit(solution)/shard_map/ppermute | solution.py:21
  125.0 6.6 %collective-permute-start.52 = (bf16[256,256]{1,0:T(8,128)(2,1)S(1)}, bf16[256,256]{1,0:T(8,128)(2,1)S(1)}, u32[]{:S(2)}, u32[]{:S(2)}) collective-permute-start(bf16[256,256]{1,0:T(8,128)(2,1)S(1)} %shard_map.63.refs_3_.refs_2_), channel_id=1, source_target_pairs={{0,2},{2,0},{4,6},{6,4},{8,10},{10,8},{12,14},{14,12},{16,18},{18,... | collective-permute-start | bytes 393224 | tf_op jit(solution)/shard_map/ppermute | solution.py:21
  130.1 6.6 %collective-permute-start.57 = (bf16[384,256]{1,0:T(8,128)(2,1)S(1)}, bf16[384,256]{1,0:T(8,128)(2,1)S(1)}, u32[]{:S(2)}, u32[]{:S(2)}) collective-permute-start(bf16[384,256]{1,0:T(8,128)(2,1)S(1)} %get-tuple-element.162.refs_4_), channel_id=1, source_target_pairs={{0,8},{2,10},{4,12},{6,14},{8,0},{10,2},{12,4},{14,6},{16,24},{18,... | collective-permute-start | bytes 589832 | tf_op jit(solution)/shard_map/ppermute | solution.py:21
  131.0 6.5 %collective-permute-start.58 = (bf16[384,256]{1,0:T(8,128)(2,1)S(1)}, bf16[384,256]{1,0:T(8,128)(2,1)S(1)}, u32[]{:S(2)}, u32[]{:S(2)}) collective-permute-start(bf16[384,256]{1,0:T(8,128)(2,1)S(1)} %get-tuple-element.165), channel_id=1, source_target_pairs={{0,4},{2,6},{4,0},{6,2},{8,12},{10,14},{12,8},{14,10},{16,20},{18,... | collective-permute-start | bytes 589832 | tf_op jit(solution)/shard_map/ppermute | solution.py:21
  139.9 7.3 %collective-permute-start.62 = (bf16[256,256]{1,0:T(8,128)(2,1)S(1)}, bf16[256,256]{1,0:T(8,128)(2,1)S(1)}, u32[]{:S(2)}, u32[]{:S(2)}) collective-permute-start(bf16[256,256]{1,0:T(8,128)(2,1)S(1)} %get-tuple-element.167.refs_2_), channel_id=1, source_target_pairs={{0,16},{2,18},{4,20},{6,22},{8,24},{10,26},{12,28},{14,30},{16,0},... | collective-permute-start | bytes 393224 | tf_op jit(solution)/shard_map/ppermute | solution.py:21
  142.8 6.9 %collective-permute-start.59 = (bf16[1792,256]{1,0:T(8,128)(2,1)S(1)}, bf16[1792,256]{1,0:T(8,128)(2,1)S(1)}, u32[]{:S(2)}, u32[]{:S(2)}) collective-permute-start(bf16[1792,256]{1,0:T(8,128)(2,1)S(1)} %get-tuple-element.169.refs_0_), channel_id=1, source_target_pairs={{0,2},{2,0},{4,6},{6,4},{8,10},{10,8},{12,14},{14,12},{16,18},{18,... | collective-permute-start | bytes 2752520 | tf_op jit(solution)/shard_map/ppermute | solution.py:21
  147.2 7.3 %collective-permute-start.66 = (bf16[384,256]{1,0:T(8,128)(2,1)S(1)}, bf16[384,256]{1,0:T(8,128)(2,1)S(1)}, u32[]{:S(2)}, u32[]{:S(2)}) collective-permute-start(bf16[384,256]{1,0:T(8,128)(2,1)S(1)} %get-tuple-element.171.refs_5_), channel_id=1, source_target_pairs={{0,8},{2,10},{4,12},{6,14},{8,0},{10,2},{12,4},{14,6},{16,24},{18,... | collective-permute-start | bytes 589832 | tf_op jit(solution)/shard_map/ppermute | solution.py:21
  148.3 7.0 %collective-permute-start.67 = (bf16[384,256]{1,0:T(8,128)(2,1)S(1)}, bf16[384,256]{1,0:T(8,128)(2,1)S(1)}, u32[]{:S(2)}, u32[]{:S(2)}) collective-permute-start(bf16[384,256]{1,0:T(8,128)(2,1)S(1)} %get-tuple-element.174), channel_id=1, source_target_pairs={{0,4},{2,6},{4,0},{6,2},{8,12},{10,14},{12,8},{14,10},{16,20},{18,... | collective-permute-start | bytes 589832 | tf_op jit(solution)/shard_map/ppermute | solution.py:21
  156.6 11.9 %collective-permute-start.68 = (bf16[1792,256]{1,0:T(8,128)(2,1)S(1)}, bf16[1792,256]{1,0:T(8,128)(2,1)S(1)}, u32[]{:S(2)}, u32[]{:S(2)}) collective-permute-start(bf16[1792,256]{1,0:T(8,128)(2,1)S(1)} %get-tuple-element.175.refs_0_), channel_id=1, source_target_pairs={{0,2},{2,0},{4,6},{6,4},{8,10},{10,8},{12,14},{14,12},{16,18},{18,... | collective-permute-start | bytes 2752520 | tf_op jit(solution)/shard_map/ppermute | solution.py:21
  157.3 9.5 %collective-permute-start.71 = (bf16[256,256]{1,0:T(8,128)(2,1)S(1)}, bf16[256,256]{1,0:T(8,128)(2,1)S(1)}, u32[]{:S(2)}, u32[]{:S(2)}) collective-permute-start(bf16[256,256]{1,0:T(8,128)(2,1)S(1)} %get-tuple-element.177.refs_2_), channel_id=1, source_target_pairs={{0,16},{2,18},{4,20},{6,22},{8,24},{10,26},{12,28},{14,30},{16,0},... | collective-permute-start | bytes 393224 | tf_op jit(solution)/shard_map/ppermute | solution.py:21
  159.0 7.9 %collective-permute-start.72 = (bf16[256,256]{1,0:T(8,128)(2,1)S(1)}, bf16[256,256]{1,0:T(8,128)(2,1)S(1)}, u32[]{:S(2)}, u32[]{:S(2)}) collective-permute-start(bf16[256,256]{1,0:T(8,128)(2,1)S(1)} %get-tuple-element.177.refs_2_), channel_id=1, source_target_pairs={{0,8},{2,10},{4,12},{6,14},{8,0},{10,2},{12,4},{14,6},{16,24},{18,... | collective-permute-start | bytes 393224 | tf_op jit(solution)/shard_map/ppermute | solution.py:21
  160.0 6.8 %collective-permute-start.73 = (bf16[256,256]{1,0:T(8,128)(2,1)S(1)}, bf16[256,256]{1,0:T(8,128)(2,1)S(1)}, u32[]{:S(2)}, u32[]{:S(2)}) collective-permute-start(bf16[256,256]{1,0:T(8,128)(2,1)S(1)} %get-tuple-element.177.refs_2_), channel_id=1, source_target_pairs={{0,4},{2,6},{4,0},{6,2},{8,12},{10,14},{12,8},{14,10},{16,20},{18,... | collective-permute-start | bytes 393224 | tf_op jit(solution)/shard_map/ppermute | solution.py:21
  161.7 6.8 %collective-permute-start.70 = (bf16[256,256]{1,0:T(8,128)(2,1)S(1)}, bf16[256,256]{1,0:T(8,128)(2,1)S(1)}, u32[]{:S(2)}, u32[]{:S(2)}) collective-permute-start(bf16[256,256]{1,0:T(8,128)(2,1)S(1)} %shard_map.71.refs_3_.refs_2_), channel_id=1, source_target_pairs={{0,2},{2,0},{4,6},{6,4},{8,10},{10,8},{12,14},{14,12},{16,18},{18,... | collective-permute-start | bytes 393224 | tf_op jit(solution)/shard_map/ppermute | solution.py:21
  177.5 7.4 %collective-permute-start.80 = (bf16[256,256]{1,0:T(8,128)(2,1)S(1)}, bf16[256,256]{1,0:T(8,128)(2,1)S(1)}, u32[]{:S(2)}, u32[]{:S(2)}) collective-permute-start(bf16[256,256]{1,0:T(8,128)(2,1)S(1)} %get-tuple-element.185.refs_1_), channel_id=1, source_target_pairs={{0,16},{2,18},{4,20},{6,22},{8,24},{10,26},{12,28},{14,30},{16,0},... | collective-permute-start | bytes 393224 | tf_op jit(solution)/shard_map/ppermute | solution.py:21
  194.2 12.5 %collective-permute-start.86 = (bf16[1792,256]{1,0:T(8,128)(2,1)S(1)}, bf16[1792,256]{1,0:T(8,128)(2,1)S(1)}, u32[]{:S(2)}, u32[]{:S(2)}) collective-permute-start(bf16[1792,256]{1,0:T(8,128)(2,1)S(1)} %get-tuple-element.193.refs_0_), channel_id=1, source_target_pairs={{0,2},{2,0},{4,6},{6,4},{8,10},{10,8},{12,14},{14,12},{16,18},{18,... | collective-permute-start | bytes 2752520 | tf_op jit(solution)/shard_map/ppermute | solution.py:21
  195.7 8.9 %collective-permute-start.89 = (bf16[256,256]{1,0:T(8,128)(2,1)S(1)}, bf16[256,256]{1,0:T(8,128)(2,1)S(1)}, u32[]{:S(2)}, u32[]{:S(2)}) collective-permute-start(bf16[256,256]{1,0:T(8,128)(2,1)S(1)} %get-tuple-element.195.refs_1_), channel_id=1, source_target_pairs={{0,16},{2,18},{4,20},{6,22},{8,24},{10,26},{12,28},{14,30},{16,0},... | collective-permute-start | bytes 393224 | tf_op jit(solution)/shard_map/ppermute | solution.py:21
  196.8 7.8 %collective-permute-start.90 = (bf16[256,256]{1,0:T(8,128)(2,1)S(1)}, bf16[256,256]{1,0:T(8,128)(2,1)S(1)}, u32[]{:S(2)}, u32[]{:S(2)}) collective-permute-start(bf16[256,256]{1,0:T(8,128)(2,1)S(1)} %get-tuple-element.195.refs_1_), channel_id=1, source_target_pairs={{0,8},{2,10},{4,12},{6,14},{8,0},{10,2},{12,4},{14,6},{16,24},{18,... | collective-permute-start | bytes 393224 | tf_op jit(solution)/shard_map/ppermute | solution.py:21
  197.9 6.7 %collective-permute-start.91 = (bf16[256,256]{1,0:T(8,128)(2,1)S(1)}, bf16[256,256]{1,0:T(8,128)(2,1)S(1)}, u32[]{:S(2)}, u32[]{:S(2)}) collective-permute-start(bf16[256,256]{1,0:T(8,128)(2,1)S(1)} %get-tuple-element.195.refs_1_), channel_id=1, source_target_pairs={{0,4},{2,6},{4,0},{6,2},{8,12},{10,14},{12,8},{14,10},{16,20},{18,... | collective-permute-start | bytes 393224 | tf_op jit(solution)/shard_map/ppermute | solution.py:21
  199.3 7.4 %collective-permute-start.88 = (bf16[256,256]{1,0:T(8,128)(2,1)S(1)}, bf16[256,256]{1,0:T(8,128)(2,1)S(1)}, u32[]{:S(2)}, u32[]{:S(2)}) collective-permute-start(bf16[256,256]{1,0:T(8,128)(2,1)S(1)} %shard_map.81.refs_3_.refs_2_), channel_id=1, source_target_pairs={{0,2},{2,0},{4,6},{6,4},{8,10},{10,8},{12,14},{14,12},{16,18},{18,... | collective-permute-start | bytes 393224 | tf_op jit(solution)/shard_map/ppermute | solution.py:21
  214.5 7.9 %collective-permute-start.98 = (bf16[256,256]{1,0:T(8,128)(2,1)S(1)}, bf16[256,256]{1,0:T(8,128)(2,1)S(1)}, u32[]{:S(2)}, u32[]{:S(2)}) collective-permute-start(bf16[256,256]{1,0:T(8,128)(2,1)S(1)} %get-tuple-element.201.refs_2_), channel_id=1, source_target_pairs={{0,16},{2,18},{4,20},{6,22},{8,24},{10,26},{12,28},{14,30},{16,0},... | collective-permute-start | bytes 393224 | tf_op jit(solution)/shard_map/ppermute | solution.py:21
  222.5 7.4 %collective-permute-start.102 = (bf16[384,256]{1,0:T(8,128)(2,1)S(1)}, bf16[384,256]{1,0:T(8,128)(2,1)S(1)}, u32[]{:S(2)}, u32[]{:S(2)}) collective-permute-start(bf16[384,256]{1,0:T(8,128)(2,1)S(1)} %get-tuple-element.205.refs_5_), channel_id=1, source_target_pairs={{0,8},{2,10},{4,12},{6,14},{8,0},{10,2},{12,4},{14,6},{16,24},{18,... | collective-permute-start | bytes 589832 | tf_op jit(solution)/shard_map/ppermute | solution.py:21
  223.6 7.0 %collective-permute-start.103 = (bf16[384,256]{1,0:T(8,128)(2,1)S(1)}, bf16[384,256]{1,0:T(8,128)(2,1)S(1)}, u32[]{:S(2)}, u32[]{:S(2)}) collective-permute-start(bf16[384,256]{1,0:T(8,128)(2,1)S(1)} %get-tuple-element.208), channel_id=1, source_target_pairs={{0,4},{2,6},{4,0},{6,2},{8,12},{10,14},{12,8},{14,10},{16,20},{18,... | collective-permute-start | bytes 589832 | tf_op jit(solution)/shard_map/ppermute | solution.py:21
  231.5 12.5 %collective-permute-start.104 = (bf16[1792,256]{1,0:T(8,128)(2,1)S(1)}, bf16[1792,256]{1,0:T(8,128)(2,1)S(1)}, u32[]{:S(2)}, u32[]{:S(2)}) collective-permute-start(bf16[1792,256]{1,0:T(8,128)(2,1)S(1)} %get-tuple-element.209.refs_0_), channel_id=1, source_target_pairs={{0,2},{2,0},{4,6},{6,4},{8,10},{10,8},{12,14},{14,12},{16,18},{18,... | collective-permute-start | bytes 2752520 | tf_op jit(solution)/shard_map/ppermute | solution.py:21
  232.9 9.1 %collective-permute-start.107 = (bf16[256,256]{1,0:T(8,128)(2,1)S(1)}, bf16[256,256]{1,0:T(8,128)(2,1)S(1)}, u32[]{:S(2)}, u32[]{:S(2)}) collective-permute-start(bf16[256,256]{1,0:T(8,128)(2,1)S(1)} %get-tuple-element.211.refs_2_), channel_id=1, source_target_pairs={{0,16},{2,18},{4,20},{6,22},{8,24},{10,26},{12,28},{14,30},{16,0},... | collective-permute-start | bytes 393224 | tf_op jit(solution)/shard_map/ppermute | solution.py:21
  234.2 7.8 %collective-permute-start.108 = (bf16[256,256]{1,0:T(8,128)(2,1)S(1)}, bf16[256,256]{1,0:T(8,128)(2,1)S(1)}, u32[]{:S(2)}, u32[]{:S(2)}) collective-permute-start(bf16[256,256]{1,0:T(8,128)(2,1)S(1)} %get-tuple-element.211.refs_2_), channel_id=1, source_target_pairs={{0,8},{2,10},{4,12},{6,14},{8,0},{10,2},{12,4},{14,6},{16,24},{18,... | collective-permute-start | bytes 393224 | tf_op jit(solution)/shard_map/ppermute | solution.py:21
  235.2 6.8 %collective-permute-start.109 = (bf16[256,256]{1,0:T(8,128)(2,1)S(1)}, bf16[256,256]{1,0:T(8,128)(2,1)S(1)}, u32[]{:S(2)}, u32[]{:S(2)}) collective-permute-start(bf16[256,256]{1,0:T(8,128)(2,1)S(1)} %get-tuple-element.211.refs_2_), channel_id=1, source_target_pairs={{0,4},{2,6},{4,0},{6,2},{8,12},{10,14},{12,8},{14,10},{16,20},{18,... | collective-permute-start | bytes 393224 | tf_op jit(solution)/shard_map/ppermute | solution.py:21
  236.7 7.4 %collective-permute-start.106 = (bf16[256,256]{1,0:T(8,128)(2,1)S(1)}, bf16[256,256]{1,0:T(8,128)(2,1)S(1)}, u32[]{:S(2)}, u32[]{:S(2)}) collective-permute-start(bf16[256,256]{1,0:T(8,128)(2,1)S(1)} %shard_map.89.refs_3_.refs_2_), channel_id=1, source_target_pairs={{0,2},{2,0},{4,6},{6,4},{8,10},{10,8},{12,14},{14,12},{16,18},{18,... | collective-permute-start | bytes 393224 | tf_op jit(solution)/shard_map/ppermute | solution.py:21
  242.0 6.4 %collective-permute-start.111 = (bf16[384,256]{1,0:T(8,128)(2,1)S(1)}, bf16[384,256]{1,0:T(8,128)(2,1)S(1)}, u32[]{:S(2)}, u32[]{:S(2)}) collective-permute-start(bf16[384,256]{1,0:T(8,128)(2,1)S(1)} %get-tuple-element.212.refs_5_), channel_id=1, source_target_pairs={{0,8},{2,10},{4,12},{6,14},{8,0},{10,2},{12,4},{14,6},{16,24},{18,... | collective-permute-start | bytes 589832 | tf_op jit(solution)/shard_map/ppermute | solution.py:21
  250.8 12.4 %collective-permute-start.113 = (bf16[1792,256]{1,0:T(8,128)(2,1)S(1)}, bf16[1792,256]{1,0:T(8,128)(2,1)S(1)}, u32[]{:S(2)}, u32[]{:S(2)}) collective-permute-start(bf16[1792,256]{1,0:T(8,128)(2,1)S(1)} %get-tuple-element.216.refs_0_), channel_id=1, source_target_pairs={{0,2},{2,0},{4,6},{6,4},{8,10},{10,8},{12,14},{14,12},{16,18},{18,... | collective-permute-start | bytes 2752520 | tf_op jit(solution)/shard_map/ppermute | solution.py:21
  251.8 9.6 %collective-permute-start.116 = (bf16[256,256]{1,0:T(8,128)(2,1)S(1)}, bf16[256,256]{1,0:T(8,128)(2,1)S(1)}, u32[]{:S(2)}, u32[]{:S(2)}) collective-permute-start(bf16[256,256]{1,0:T(8,128)(2,1)S(1)} %get-tuple-element.218.refs_1_), channel_id=1, source_target_pairs={{0,16},{2,18},{4,20},{6,22},{8,24},{10,26},{12,28},{14,30},{16,0},... | collective-permute-start | bytes 393224 | tf_op jit(solution)/shard_map/ppermute | solution.py:21
  253.2 8.2 %collective-permute-start.117 = (bf16[256,256]{1,0:T(8,128)(2,1)S(1)}, bf16[256,256]{1,0:T(8,128)(2,1)S(1)}, u32[]{:S(2)}, u32[]{:S(2)}) collective-permute-start(bf16[256,256]{1,0:T(8,128)(2,1)S(1)} %get-tuple-element.218.refs_1_), channel_id=1, source_target_pairs={{0,8},{2,10},{4,12},{6,14},{8,0},{10,2},{12,4},{14,6},{16,24},{18,... | collective-permute-start | bytes 393224 | tf_op jit(solution)/shard_map/ppermute | solution.py:21
  254.0 7.3 %collective-permute-start.118 = (bf16[256,256]{1,0:T(8,128)(2,1)S(1)}, bf16[256,256]{1,0:T(8,128)(2,1)S(1)}, u32[]{:S(2)}, u32[]{:S(2)}) collective-permute-start(bf16[256,256]{1,0:T(8,128)(2,1)S(1)} %get-tuple-element.218.refs_1_), channel_id=1, source_target_pairs={{0,4},{2,6},{4,0},{6,2},{8,12},{10,14},{12,8},{14,10},{16,20},{18,... | collective-permute-start | bytes 393224 | tf_op jit(solution)/shard_map/ppermute | solution.py:21
  255.9 7.3 %collective-permute-start.115 = (bf16[256,256]{1,0:T(8,128)(2,1)S(1)}, bf16[256,256]{1,0:T(8,128)(2,1)S(1)}, u32[]{:S(2)}, u32[]{:S(2)}) collective-permute-start(bf16[256,256]{1,0:T(8,128)(2,1)S(1)} %shard_map.93.refs_3_.refs_2_), channel_id=1, source_target_pairs={{0,2},{2,0},{4,6},{6,4},{8,10},{10,8},{12,14},{14,12},{16,18},{18,... | collective-permute-start | bytes 393224 | tf_op jit(solution)/shard_map/ppermute | solution.py:21
  261.4 6.6 %collective-permute-start.120 = (bf16[384,256]{1,0:T(8,128)(2,1)S(1)}, bf16[384,256]{1,0:T(8,128)(2,1)S(1)}, u32[]{:S(2)}, u32[]{:S(2)}) collective-permute-start(bf16[384,256]{1,0:T(8,128)(2,1)S(1)} %get-tuple-element.219.refs_4_), channel_id=1, source_target_pairs={{0,8},{2,10},{4,12},{6,14},{8,0},{10,2},{12,4},{14,6},{16,24},{18,... | collective-permute-start | bytes 589832 | tf_op jit(solution)/shard_map/ppermute | solution.py:21
  270.5 6.4 %collective-permute-start.122 = (bf16[1792,256]{1,0:T(8,128)(2,1)S(1)}, bf16[1792,256]{1,0:T(8,128)(2,1)S(1)}, u32[]{:S(2)}, u32[]{:S(2)}) collective-permute-start(bf16[1792,256]{1,0:T(8,128)(2,1)S(1)} %get-tuple-element.224.refs_0_), channel_id=1, source_target_pairs={{0,2},{2,0},{4,6},{6,4},{8,10},{10,8},{12,14},{14,12},{16,18},{18,... | collective-permute-start | bytes 2752520 | tf_op jit(solution)/shard_map/ppermute | solution.py:21
  (63 other events, 341.2 us)

commit v3 on v2

--- a/solution.py
+++ b/solution.py
@@ -93,7 +93,7 @@
 def product_kernel(parts, has_total, factor_ref, *refs):
     own_row, own_group = lax.axis_index("rows"), lax.axis_index("cols")
     groups, height, _ = factor_ref.shape
-    send_ref, keep_ref, vector_ref = refs[-3:]
+    send_ref, vector_ref = refs[-2:]
     for piece_ref, spans in zip(refs, parts):
         if spans is None:
             vector_ref[...] = piece_ref[...]
@@ -104,27 +104,33 @@
             vector_ref[pl.ds(place, count)] = piece_ref[at : at + count]
             at += count
     vector = vector_ref[...]
-    for turn in range(groups):
+    for turn in range(groups - 1):
         group = lax.rem(own_group + 1 + turn, groups)
         span = pl.ds(turn * height, height)
         result = jnp.dot(factor_ref[group], vector, preferred_element_type=jnp.float32)
         if has_total:
             result = result + refs[len(parts)][span]
-        if turn < groups - 1:
-            send_ref[span] = result.astype(send_ref.dtype)
-        else:
-            keep_ref[...] = result
+        send_ref[span] = result.astype(send_ref.dtype)
+
+
+def own_kernel(has_total, factor_ref, vector_ref, *refs):
+    groups, height, _ = factor_ref.shape
+    result = jnp.dot(factor_ref[lax.axis_index("cols")], vector_ref[...], preferred_element_type=jnp.float32)
+    refs[-1][...] = result + refs[0][pl.ds((groups - 1) * height, height)] if has_total else result
 
 
 def total_kernel(has_total, factor_ref, vector_ref, *refs):
     own_group = lax.axis_index("cols")
     groups, height, _ = factor_ref.shape
-    vector = vector_ref[...]
-    for turn in range(groups):
+
+    def one(turn, carry):
         group = lax.rem(own_group + 1 + turn, groups)
-        span = pl.ds(turn * height, height)
-        result = jnp.dot(factor_ref[group], vector, preferred_element_type=jnp.float32)
+        span = pl.ds(pl.multiple_of(turn * height, height), height)
+        result = jnp.dot(factor_ref[group], vector_ref[...], preferred_element_type=jnp.float32)
         refs[-1][span] = result + refs[0][span] if has_total else result
+        return carry
+
+    lax.fori_loop(0, groups, one, 0)
 
 
 def product(factor, pieces, total, after):
@@ -135,13 +141,26 @@
         functools.partial(product_kernel, [spans for _, spans in pieces], len(given)),
         (
             jax.ShapeDtypeStruct(((groups - 1) * height, columns), jnp.bfloat16),
-            jax.ShapeDtypeStruct((height, columns), jnp.float32),
             jax.ShapeDtypeStruct((width, columns), jnp.bfloat16),
         ),
         [factor, *(array for array, _ in pieces), *given],
         after,
         14,
     )
+
+
+def own_product(factor, vector, total):
+    given = [] if total is None else [total]
+    _, height, width = factor.shape
+    columns = vector.shape[1]
+    return local_call(
+        functools.partial(own_kernel, len(given)),
+        (jax.ShapeDtypeStruct((height, columns), jnp.float32),),
+        [factor, vector, *given],
+        [],
+        14,
+        2 * height * width * columns,
+    )[0]
 
 
 def add_product(factor, vector, total):
@@ -230,7 +249,8 @@
         current, solving = step // 2, step % 2 == 0
         first = current if solving else current + 1
         total = None if solving else totals[chunk].pop(first, None)
-        sends, keep, vector = product(factors[step][first], gather.pieces, total, after)
+        sends, vector = product(factors[step][first], gather.pieces, total, after)
+        keep = own_product(factors[step][first], vector, total)
         made = []
         if not solving:
             for later in range(current + 2, panels):

time: 287 us -> 278 us (0.969)
  waiting for transfers between devices: 100 us -> 89.3 us
    ppermute x14, waiting for transfers between devices: 23.4 us -> 14.4 us  [finish(): lax.ppermute(share, 'cols', [(i, (i + turn) % cols) for i in range(cols)])]
    pallas_call x63 -> x77, Pallas kernels: 33.1 us -> 35 us  [local_call(): pl.pallas_call(kernel, out_shape=out_shape, in_specs=[VMEM] * len(operand...]
  transfers between devices with their start and end apart: 126 -> 126, of which waited for: 68 -> 67; matrix products, arithmetic and copies ran while one was open for 8% -> 8% of each run, Pallas kernels for 10% -> 11%
where the time goes in v3:
time: 278 us
  starting transfers between devices  127 us (46%)
  waiting for transfers between devices  89.3 us (32%)
  Pallas kernels  35 us (13%)
  local copies, waits for them, and re-layouts  21.9 us (8%)
  other arithmetic  3.47 us (1%)
    ppermute x112, starting transfers between devices, swap(): lax.ppermute(block, 'rows', [(i, i ^ (odd if i % 2 else even)) for i in r...  105 us
    ppermute x112, waiting for transfers between devices, swap(): lax.ppermute(block, 'rows', [(i, i ^ (odd if i % 2 else even)) for i in r...  74.8 us
    pallas_call x77, Pallas kernels, local_call(): pl.pallas_call(kernel, out_shape=out_shape, in_specs=[VMEM] * len(operand...  35 us
    ppermute x14, starting transfers between devices, finish(): lax.ppermute(share, 'cols', [(i, (i + turn) % cols) for i in range(cols)])  22.2 us
    ppermute x14, waiting for transfers between devices, finish(): lax.ppermute(share, 'cols', [(i, (i + turn) % cols) for i in range(cols)])  14.4 us
    squeeze x3, local copies, waits for them, and re-layouts, load(): blocks[pair_index(later, current)]  11.7 us
    squeeze x4, local copies, waits for them, and re-layouts, load(): loaded = {current: blocks[current]}  10.1 us
  transfers between devices with their start and end apart: 126, of which 67 were waited for; matrix products, arithmetic and copies ran while one was open for 8% of the time, Pallas kernels for 11%

profile of v3, /device:TPU:0, one launch (start us, length us, event | category | flops | bytes accessed | tf_op | source)
XLA Modules:
  0.0 278.0 jit_solution(12143156892949848255)
XLA Ops:
  0.0 1.7 convert.4
  1.8 4.1 %collective-permute-start = (bf16[256,256]{1,0:T(8,128)(2,1)S(1)}, bf16[256,256]{1,0:T(8,128)(2,1)S(1)}, u32[]{:S(2)}, u32[]{:S(2)}) collective-permute-start(bf16[256,256]{1,0:T(8,128)(2,1)S(1)} %get-tuple-element.233.refs_0_), channel_id=1, source_target_pairs={{0,16},{2,18},{4,20},{6,22},{8,24},{10,26},{12,28},{14,30},{16,0},... | collective-permute-start | bytes 393224 | tf_op jit(solution)/shard_map/ppermute | solution.py:21
  5.9 1.6 collective-permute-start.1
  7.4 1.5 collective-permute-start.2
  8.9 3.3 %collective-permute-done.refs_0_.refs_1_ = bf16[256,256]{1,0:T(8,128)(2,1)S(1)} collective-permute-done((bf16[256,256]{1,0:T(8,128)(2,1)S(1)}, bf16[256,256]{1,0:T(8,128)(2,1)S(1)}, u32[]{:S(2)}, u32[]{:S(2)}) %collective-permute-start) | collective-permute-done | bytes 131104 | tf_op jit(solution)/shard_map/ppermute | solution.py:21
  12.5 1.5 collective-permute-start.3
  14.0 1.5 collective-permute-start.4
  15.5 2.4 collective-permute-start.8
  19.7 3.9 %collective-permute-start.6 = (bf16[256,256]{1,0:T(8,128)(2,1)S(1)}, bf16[256,256]{1,0:T(8,128)(2,1)S(1)}, u32[]{:S(2)}, u32[]{:S(2)}) collective-permute-start(bf16[256,256]{1,0:T(8,128)(2,1)S(1)} %slice_select_fusion), channel_id=1, source_target_pairs={{0,4},{2,10},{4,0},{6,14},{8,12},{10,2},{12,8},{14,6},{16,20},{18,... | collective-permute-start | bytes 393224 | tf_op jit(solution)/shard_map/ppermute | solution.py:21
  23.6 5.5 %slice_bitcast_fusion.6 = (bf16[2,256,4096]{2,1,0:T(8,128)(2,1)S(1)}, bf16[2,256,4096]{2,1,0:T(8,128)(2,1)S(1)}, bf16[2,256,4096]{2,1,0:T(8,128)(2,1)S(1)}) fusion(bf16[6,2,256,4096]{3,2,1,0:T(8,128)(2,1)} %param.5), kind=kLoop, calls=%fused_computation.6 | loop fusion | bytes 25165824 | tf_op jit(solution)/shard_map/squeeze | solution.py:244
  30.0 2.5 slice_bitcast_fusion.9.factor_ref
  33.4 1.6 collective-permute-start.11
  36.8 2.1 collective-permute-done.11.refs_0_
  39.1 1.8 collective-permute-start.15
  40.9 4.7 %collective-permute-start.17 = (bf16[256,256]{1,0:T(8,128)(2,1)S(1)}, bf16[256,256]{1,0:T(8,128)(2,1)S(1)}, u32[]{:S(2)}, u32[]{:S(2)}) collective-permute-start(bf16[256,256]{1,0:T(8,128)(2,1)S(1)} %get-tuple-element.123.refs_1_), channel_id=1, source_target_pairs={{0,16},{2,18},{4,20},{6,22},{8,24},{10,26},{12,28},{14,30},{16,0},... | collective-permute-start | bytes 393224 | tf_op jit(solution)/shard_map/ppermute | solution.py:21
  47.0 3.5 %collective-permute-done.17.refs_0_.refs_2_ = bf16[256,256]{1,0:T(8,128)(2,1)S(1)} collective-permute-done((bf16[256,256]{1,0:T(8,128)(2,1)S(1)}, bf16[256,256]{1,0:T(8,128)(2,1)S(1)}, u32[]{:S(2)}, u32[]{:S(2)}) %collective-permute-start.17) | collective-permute-done | bytes 131104 | tf_op jit(solution)/shard_map/ppermute | solution.py:21
  51.1 1.8 collective-permute-start.21
  52.9 1.5 collective-permute-start.22
  55.2 1.6 collective-permute-start.20
  61.0 2.3 collective-permute-start.26
  66.0 2.7 slice_bitcast_fusion.5.refs_4_.factor_ref
  72.5 1.6 collective-permute-start.29
  78.8 1.8 collective-permute-start.35
  82.5 1.5 shard_map.55.refs_4_.refs_0_
  84.2 1.5 shard_map.56.refs_5_.refs_0_
  85.7 2.1 collective-permute-done.35.refs_0_.refs_3_
  90.9 1.6 collective-permute-start.38
  97.1 1.4 shard_map.62.refs_4_.refs_0_
  98.5 1.4 shard_map.63.refs_5_.refs_0_
  99.9 2.3 collective-permute-start.44
  104.4 3.8 %slice_bitcast_fusion.3 = (bf16[2,256,4096]{2,1,0:T(8,128)(2,1)S(1)}, bf16[2,256,4096]{2,1,0:T(8,128)(2,1)S(1)}) fusion(bf16[6,2,256,4096]{3,2,1,0:T(8,128)(2,1)} %param.5), kind=kLoop, calls=%fused_computation.3 | loop fusion | bytes 16777216 | tf_op jit(solution)/shard_map/squeeze | solution.py:244
  111.7 1.6 collective-permute-start.47
  122.1 5.0 %collective-permute-done.53.refs_0_.refs_2_ = bf16[256,256]{1,0:T(8,128)(2,1)S(1)} collective-permute-done((bf16[256,256]{1,0:T(8,128)(2,1)S(1)}, bf16[256,256]{1,0:T(8,128)(2,1)S(1)}, u32[]{:S(2)}, u32[]{:S(2)}) %collective-permute-start.53) | collective-permute-done | bytes 131104 | tf_op jit(solution)/shard_map/ppermute | solution.py:21
  129.7 1.6 collective-permute-start.56
  132.1 1.4 collective-permute-done.57.refs_5_
  139.4 1.5 collective-permute-done.60.refs_0_
  141.0 2.5 slice_bitcast_fusion.2.refs_4_.factor_ref
  147.3 1.6 collective-permute-start.65
  158.7 1.5 shard_map.79.refs_4_.refs_0_
  160.2 2.5 collective-permute-done.71.refs_0_.refs_3_
  165.3 1.6 collective-permute-start.74
  167.6 2.3 collective-permute-done.75.refs_6_
  171.7 1.7 shard_map.85.refs_4_.refs_0_
  173.4 2.3 collective-permute-start.80
  177.7 2.5 slice_bitcast_fusion.1.refs_5_.factor_ref
  184.3 1.6 collective-permute-start.83
  189.5 1.4 collective-permute-start.87
  194.6 5.5 %collective-permute-done.89.refs_0_.refs_2_ = bf16[256,256]{1,0:T(8,128)(2,1)S(1)} collective-permute-done((bf16[256,256]{1,0:T(8,128)(2,1)S(1)}, bf16[256,256]{1,0:T(8,128)(2,1)S(1)}, u32[]{:S(2)}, u32[]{:S(2)}) %collective-permute-start.89) | collective-permute-done | bytes 131104 | tf_op jit(solution)/shard_map/ppermute | solution.py:21
  202.9 1.6 collective-permute-start.92
  209.2 1.5 collective-permute-start.98
  212.5 1.4 collective-permute-done.96.refs_0_
  214.1 2.5 slice_bitcast_fusion.refs_4_.factor_ref
  219.6 1.6 collective-permute-start.101
  222.0 2.0 collective-permute-done.102.refs_6_
  226.4 1.7 collective-permute-start.107
  230.4 5.3 %collective-permute-done.107.refs_0_.refs_3_ = bf16[256,256]{1,0:T(8,128)(2,1)S(1)} collective-permute-done((bf16[256,256]{1,0:T(8,128)(2,1)S(1)}, bf16[256,256]{1,0:T(8,128)(2,1)S(1)}, u32[]{:S(2)}, u32[]{:S(2)}) %collective-permute-start.107) | collective-permute-done | bytes 131104 | tf_op jit(solution)/shard_map/ppermute | solution.py:21
  238.6 1.6 collective-permute-start.110
  244.9 1.6 collective-permute-start.116
  248.9 5.2 %collective-permute-done.116.refs_0_.refs_2_ = bf16[256,256]{1,0:T(8,128)(2,1)S(1)} collective-permute-done((bf16[256,256]{1,0:T(8,128)(2,1)S(1)}, bf16[256,256]{1,0:T(8,128)(2,1)S(1)}, u32[]{:S(2)}, u32[]{:S(2)}) %collective-permute-start.116) | collective-permute-done | bytes 131104 | tf_op jit(solution)/shard_map/ppermute | solution.py:21
  257.1 1.6 collective-permute-start.119
  263.7 4.1 %collective-permute-done.123.refs_0_ = bf16[256,256]{1,0:T(8,128)(2,1)S(1)} collective-permute-done((bf16[256,256]{1,0:T(8,128)(2,1)S(1)}, bf16[256,256]{1,0:T(8,128)(2,1)S(1)}, u32[]{:S(2)}, u32[]{:S(2)}) %collective-permute-start.123) | collective-permute-done | bytes 131104 | tf_op jit(solution)/shard_map/ppermute | solution.py:21
  270.1 1.6 collective-permute-start.125
  272.5 3.2 %collective-permute-done.125.refs_0_ = bf16[256,256]{1,0:T(8,128)(2,1)S(1)} collective-permute-done((bf16[256,256]{1,0:T(8,128)(2,1)S(1)}, bf16[256,256]{1,0:T(8,128)(2,1)S(1)}, u32[]{:S(2)}, u32[]{:S(2)}) %collective-permute-start.125) | collective-permute-done | bytes 131104 | tf_op jit(solution)/shard_map/ppermute | solution.py:267
  276.5 1.5 maximum_bitcast_fusion
  (283 shorter events, 129.4 us)
Async XLA Ops:
  1.8 10.5 %collective-permute-start = (bf16[256,256]{1,0:T(8,128)(2,1)S(1)}, bf16[256,256]{1,0:T(8,128)(2,1)S(1)}, u32[]{:S(2)}, u32[]{:S(2)}) collective-permute-start(bf16[256,256]{1,0:T(8,128)(2,1)S(1)} %get-tuple-element.233.refs_0_), channel_id=1, source_target_pairs={{0,16},{2,18},{4,20},{6,22},{8,24},{10,26},{12,28},{14,30},{16,0},... | collective-permute-start | bytes 393224 | tf_op jit(solution)/shard_map/ppermute | solution.py:21
  5.9 6.6 %collective-permute-start.1 = (bf16[256,256]{1,0:T(8,128)(2,1)S(1)}, bf16[256,256]{1,0:T(8,128)(2,1)S(1)}, u32[]{:S(2)}, u32[]{:S(2)}) collective-permute-start(bf16[256,256]{1,0:T(8,128)(2,1)S(1)} %get-tuple-element.233.refs_0_), channel_id=1, source_target_pairs={{0,8},{2,10},{4,12},{6,14},{8,0},{10,2},{12,4},{14,6},{16,24},{18,... | collective-permute-start | bytes 393224 | tf_op jit(solution)/shard_map/ppermute | solution.py:21
  15.5 14.3 %collective-permute-start.8 = (bf16[256,256]{1,0:T(8,128)(2,1)S(1)}, bf16[256,256]{1,0:T(8,128)(2,1)S(1)}, u32[]{:S(2)}, u32[]{:S(2)}) collective-permute-start(bf16[256,256]{1,0:T(8,128)(2,1)S(1)} %get-tuple-element.232.refs_1_), channel_id=1, source_target_pairs={{0,16},{2,18},{4,20},{6,22},{8,24},{10,26},{12,28},{14,30},{16,0},... | collective-permute-start | bytes 393224 | tf_op jit(solution)/shard_map/ppermute | solution.py:21
  17.9 11.9 %collective-permute-start.9 = (bf16[256,256]{1,0:T(8,128)(2,1)S(1)}, bf16[256,256]{1,0:T(8,128)(2,1)S(1)}, u32[]{:S(2)}, u32[]{:S(2)}) collective-permute-start(bf16[256,256]{1,0:T(8,128)(2,1)S(1)} %get-tuple-element.232.refs_1_), channel_id=1, source_target_pairs={{0,8},{2,10},{4,12},{6,14},{8,0},{10,2},{12,4},{14,6},{16,24},{18,... | collective-permute-start | bytes 393224 | tf_op jit(solution)/shard_map/ppermute | solution.py:21
  17.9 11.9 %collective-permute-start.10 = (bf16[256,256]{1,0:T(8,128)(2,1)S(1)}, bf16[256,256]{1,0:T(8,128)(2,1)S(1)}, u32[]{:S(2)}, u32[]{:S(2)}) collective-permute-start(bf16[256,256]{1,0:T(8,128)(2,1)S(1)} %get-tuple-element.232.refs_1_), channel_id=1, source_target_pairs={{0,4},{2,6},{4,0},{6,2},{8,12},{10,14},{12,8},{14,10},{16,20},{18,... | collective-permute-start | bytes 393224 | tf_op jit(solution)/shard_map/ppermute | solution.py:21
  19.7 9.5 %collective-permute-start.6 = (bf16[256,256]{1,0:T(8,128)(2,1)S(1)}, bf16[256,256]{1,0:T(8,128)(2,1)S(1)}, u32[]{:S(2)}, u32[]{:S(2)}) collective-permute-start(bf16[256,256]{1,0:T(8,128)(2,1)S(1)} %slice_select_fusion), channel_id=1, source_target_pairs={{0,4},{2,10},{4,0},{6,14},{8,12},{10,2},{12,8},{14,6},{16,20},{18,... | collective-permute-start | bytes 393224 | tf_op jit(solution)/shard_map/ppermute | solution.py:21
  29.8 6.9 %collective-permute-start.12 = (bf16[384,256]{1,0:T(8,128)(2,1)S(1)}, bf16[384,256]{1,0:T(8,128)(2,1)S(1)}, u32[]{:S(2)}, u32[]{:S(2)}) collective-permute-start(bf16[384,256]{1,0:T(8,128)(2,1)S(1)} %get-tuple-element.116.refs_4_), channel_id=1, source_target_pairs={{0,8},{2,10},{4,12},{6,14},{8,0},{10,2},{12,4},{14,6},{16,24},{18,... | collective-permute-start | bytes 589832 | tf_op jit(solution)/shard_map/ppermute | solution.py:21
  29.9 6.9 %collective-permute-start.13 = (bf16[384,256]{1,0:T(8,128)(2,1)S(1)}, bf16[384,256]{1,0:T(8,128)(2,1)S(1)}, u32[]{:S(2)}, u32[]{:S(2)}) collective-permute-start(bf16[384,256]{1,0:T(8,128)(2,1)S(1)} %get-tuple-element.119), channel_id=1, source_target_pairs={{0,4},{2,6},{4,0},{6,2},{8,12},{10,14},{12,8},{14,10},{16,20},{18,... | collective-permute-start | bytes 589832 | tf_op jit(solution)/shard_map/ppermute | solution.py:21
  39.0 15.3 %collective-permute-start.14 = (bf16[1792,256]{1,0:T(8,128)(2,1)S(1)}, bf16[1792,256]{1,0:T(8,128)(2,1)S(1)}, u32[]{:S(2)}, u32[]{:S(2)}) collective-permute-start(bf16[1792,256]{1,0:T(8,128)(2,1)S(1)} %get-tuple-element.121.refs_0_), channel_id=1, source_target_pairs={{0,2},{2,0},{4,6},{6,4},{8,10},{10,8},{12,14},{14,12},{16,18},{18,... | collective-permute-start | bytes 2752520 | tf_op jit(solution)/shard_map/ppermute | solution.py:21
  39.1 7.3 %collective-permute-start.15 = (bf16[256,256]{1,0:T(8,128)(2,1)S(1)}, bf16[256,256]{1,0:T(8,128)(2,1)S(1)}, u32[]{:S(2)}, u32[]{:S(2)}) collective-permute-start(bf16[256,256]{1,0:T(8,128)(2,1)S(1)} %get-tuple-element.122), channel_id=1, source_target_pairs={{0,4},{2,10},{4,0},{6,14},{8,12},{10,2},{12,8},{14,6},{16,20},{18,... | collective-permute-start | bytes 393224 | tf_op jit(solution)/shard_map/ppermute | solution.py:21
  40.9 9.6 %collective-permute-start.17 = (bf16[256,256]{1,0:T(8,128)(2,1)S(1)}, bf16[256,256]{1,0:T(8,128)(2,1)S(1)}, u32[]{:S(2)}, u32[]{:S(2)}) collective-permute-start(bf16[256,256]{1,0:T(8,128)(2,1)S(1)} %get-tuple-element.123.refs_1_), channel_id=1, source_target_pairs={{0,16},{2,18},{4,20},{6,22},{8,24},{10,26},{12,28},{14,30},{16,0},... | collective-permute-start | bytes 393224 | tf_op jit(solution)/shard_map/ppermute | solution.py:21
  46.3 8.0 %collective-permute-start.16 = (bf16[256,256]{1,0:T(8,128)(2,1)S(1)}, bf16[256,256]{1,0:T(8,128)(2,1)S(1)}, u32[]{:S(2)}, u32[]{:S(2)}) collective-permute-start(bf16[256,256]{1,0:T(8,128)(2,1)S(1)} %shard_map.44.refs_3_.refs_2_), channel_id=1, source_target_pairs={{0,2},{2,0},{4,6},{6,4},{8,10},{10,8},{12,14},{14,12},{16,18},{18,... | collective-permute-start | bytes 393224 | tf_op jit(solution)/shard_map/ppermute | solution.py:21
  51.1 6.5 %collective-permute-start.21 = (bf16[384,256]{1,0:T(8,128)(2,1)S(1)}, bf16[384,256]{1,0:T(8,128)(2,1)S(1)}, u32[]{:S(2)}, u32[]{:S(2)}) collective-permute-start(bf16[384,256]{1,0:T(8,128)(2,1)S(1)} %get-tuple-element.124.refs_4_), channel_id=1, source_target_pairs={{0,8},{2,10},{4,12},{6,14},{8,0},{10,2},{12,4},{14,6},{16,24},{18,... | collective-permute-start | bytes 589832 | tf_op jit(solution)/shard_map/ppermute | solution.py:21
  61.0 7.9 %collective-permute-start.26 = (bf16[256,256]{1,0:T(8,128)(2,1)S(1)}, bf16[256,256]{1,0:T(8,128)(2,1)S(1)}, u32[]{:S(2)}, u32[]{:S(2)}) collective-permute-start(bf16[256,256]{1,0:T(8,128)(2,1)S(1)} %get-tuple-element.129.refs_2_), channel_id=1, source_target_pairs={{0,16},{2,18},{4,20},{6,22},{8,24},{10,26},{12,28},{14,30},{16,0},... | collective-permute-start | bytes 393224 | tf_op jit(solution)/shard_map/ppermute | solution.py:21
  64.9 6.7 %collective-permute-start.23 = (bf16[1792,256]{1,0:T(8,128)(2,1)S(1)}, bf16[1792,256]{1,0:T(8,128)(2,1)S(1)}, u32[]{:S(2)}, u32[]{:S(2)}) collective-permute-start(bf16[1792,256]{1,0:T(8,128)(2,1)S(1)} %get-tuple-element.131.refs_0_), channel_id=1, source_target_pairs={{0,2},{2,0},{4,6},{6,4},{8,10},{10,8},{12,14},{14,12},{16,18},{18,... | collective-permute-start | bytes 2752520 | tf_op jit(solution)/shard_map/ppermute | solution.py:21
  69.5 6.7 %collective-permute-start.30 = (bf16[384,256]{1,0:T(8,128)(2,1)S(1)}, bf16[384,256]{1,0:T(8,128)(2,1)S(1)}, u32[]{:S(2)}, u32[]{:S(2)}) collective-permute-start(bf16[384,256]{1,0:T(8,128)(2,1)S(1)} %get-tuple-element.133.refs_4_), channel_id=1, source_target_pairs={{0,8},{2,10},{4,12},{6,14},{8,0},{10,2},{12,4},{14,6},{16,24},{18,... | collective-permute-start | bytes 589832 | tf_op jit(solution)/shard_map/ppermute | solution.py:21
  77.6 12.4 %collective-permute-start.32 = (bf16[1792,256]{1,0:T(8,128)(2,1)S(1)}, bf16[1792,256]{1,0:T(8,128)(2,1)S(1)}, u32[]{:S(2)}, u32[]{:S(2)}) collective-permute-start(bf16[1792,256]{1,0:T(8,128)(2,1)S(1)} %get-tuple-element.137.refs_0_), channel_id=1, source_target_pairs={{0,2},{2,0},{4,6},{6,4},{8,10},{10,8},{12,14},{14,12},{16,18},{18,... | collective-permute-start | bytes 2752520 | tf_op jit(solution)/shard_map/ppermute | solution.py:21
  78.8 8.9 %collective-permute-start.35 = (bf16[256,256]{1,0:T(8,128)(2,1)S(1)}, bf16[256,256]{1,0:T(8,128)(2,1)S(1)}, u32[]{:S(2)}, u32[]{:S(2)}) collective-permute-start(bf16[256,256]{1,0:T(8,128)(2,1)S(1)} %get-tuple-element.139.refs_2_), channel_id=1, source_target_pairs={{0,16},{2,18},{4,20},{6,22},{8,24},{10,26},{12,28},{14,30},{16,0},... | collective-permute-start | bytes 393224 | tf_op jit(solution)/shard_map/ppermute | solution.py:21
  80.6 7.2 %collective-permute-start.36 = (bf16[256,256]{1,0:T(8,128)(2,1)S(1)}, bf16[256,256]{1,0:T(8,128)(2,1)S(1)}, u32[]{:S(2)}, u32[]{:S(2)}) collective-permute-start(bf16[256,256]{1,0:T(8,128)(2,1)S(1)} %get-tuple-element.139.refs_2_), channel_id=1, source_target_pairs={{0,8},{2,10},{4,12},{6,14},{8,0},{10,2},{12,4},{14,6},{16,24},{18,... | collective-permute-start | bytes 393224 | tf_op jit(solution)/shard_map/ppermute | solution.py:21
  96.0 7.8 %collective-permute-start.42 = (bf16[256,256]{1,0:T(8,128)(2,1)S(1)}, bf16[256,256]{1,0:T(8,128)(2,1)S(1)}, u32[]{:S(2)}, u32[]{:S(2)}) collective-permute-start(bf16[256,256]{1,0:T(8,128)(2,1)S(1)} %get-tuple-element.145), channel_id=1, source_target_pairs={{0,4},{2,10},{4,0},{6,14},{8,12},{10,2},{12,8},{14,6},{16,20},{18,... | collective-permute-start | bytes 393224 | tf_op jit(solution)/shard_map/ppermute | solution.py:21
  99.9 8.3 %collective-permute-start.44 = (bf16[256,256]{1,0:T(8,128)(2,1)S(1)}, bf16[256,256]{1,0:T(8,128)(2,1)S(1)}, u32[]{:S(2)}, u32[]{:S(2)}) collective-permute-start(bf16[256,256]{1,0:T(8,128)(2,1)S(1)} %get-tuple-element.146.refs_1_), channel_id=1, source_target_pairs={{0,16},{2,18},{4,20},{6,22},{8,24},{10,26},{12,28},{14,30},{16,0},... | collective-permute-start | bytes 393224 | tf_op jit(solution)/shard_map/ppermute | solution.py:21
  103.8 7.0 %collective-permute-start.41 = (bf16[1792,256]{1,0:T(8,128)(2,1)S(1)}, bf16[1792,256]{1,0:T(8,128)(2,1)S(1)}, u32[]{:S(2)}, u32[]{:S(2)}) collective-permute-start(bf16[1792,256]{1,0:T(8,128)(2,1)S(1)} %get-tuple-element.144.refs_0_), channel_id=1, source_target_pairs={{0,2},{2,0},{4,6},{6,4},{8,10},{10,8},{12,14},{14,12},{16,18},{18,... | collective-permute-start | bytes 2752520 | tf_op jit(solution)/shard_map/ppermute | solution.py:21
  103.8 7.0 %collective-permute-start.43 = (bf16[256,256]{1,0:T(8,128)(2,1)S(1)}, bf16[256,256]{1,0:T(8,128)(2,1)S(1)}, u32[]{:S(2)}, u32[]{:S(2)}) collective-permute-start(bf16[256,256]{1,0:T(8,128)(2,1)S(1)} %shard_map.61.refs_3_.refs_2_), channel_id=1, source_target_pairs={{0,2},{2,0},{4,6},{6,4},{8,10},{10,8},{12,14},{14,12},{16,18},{18,... | collective-permute-start | bytes 393224 | tf_op jit(solution)/shard_map/ppermute | solution.py:21
  108.2 7.1 %collective-permute-start.48 = (bf16[384,256]{1,0:T(8,128)(2,1)S(1)}, bf16[384,256]{1,0:T(8,128)(2,1)S(1)}, u32[]{:S(2)}, u32[]{:S(2)}) collective-permute-start(bf16[384,256]{1,0:T(8,128)(2,1)S(1)} %get-tuple-element.148.refs_4_), channel_id=1, source_target_pairs={{0,8},{2,10},{4,12},{6,14},{8,0},{10,2},{12,4},{14,6},{16,24},{18,... | collective-permute-start | bytes 589832 | tf_op jit(solution)/shard_map/ppermute | solution.py:21
  109.5 6.7 %collective-permute-start.49 = (bf16[384,256]{1,0:T(8,128)(2,1)S(1)}, bf16[384,256]{1,0:T(8,128)(2,1)S(1)}, u32[]{:S(2)}, u32[]{:S(2)}) collective-permute-start(bf16[384,256]{1,0:T(8,128)(2,1)S(1)} %get-tuple-element.151), channel_id=1, source_target_pairs={{0,4},{2,6},{4,0},{6,2},{8,12},{10,14},{12,8},{14,10},{16,20},{18,... | collective-permute-start | bytes 589832 | tf_op jit(solution)/shard_map/ppermute | solution.py:21
  116.9 11.9 %collective-permute-start.50 = (bf16[1792,256]{1,0:T(8,128)(2,1)S(1)}, bf16[1792,256]{1,0:T(8,128)(2,1)S(1)}, u32[]{:S(2)}, u32[]{:S(2)}) collective-permute-start(bf16[1792,256]{1,0:T(8,128)(2,1)S(1)} %get-tuple-element.153.refs_0_), channel_id=1, source_target_pairs={{0,2},{2,0},{4,6},{6,4},{8,10},{10,8},{12,14},{14,12},{16,18},{18,... | collective-permute-start | bytes 2752520 | tf_op jit(solution)/shard_map/ppermute | solution.py:21
  117.8 9.4 %collective-permute-start.53 = (bf16[256,256]{1,0:T(8,128)(2,1)S(1)}, bf16[256,256]{1,0:T(8,128)(2,1)S(1)}, u32[]{:S(2)}, u32[]{:S(2)}) collective-permute-start(bf16[256,256]{1,0:T(8,128)(2,1)S(1)} %get-tuple-element.155.refs_1_), channel_id=1, source_target_pairs={{0,16},{2,18},{4,20},{6,22},{8,24},{10,26},{12,28},{14,30},{16,0},... | collective-permute-start | bytes 393224 | tf_op jit(solution)/shard_map/ppermute | solution.py:21
  118.8 8.4 %collective-permute-start.54 = (bf16[256,256]{1,0:T(8,128)(2,1)S(1)}, bf16[256,256]{1,0:T(8,128)(2,1)S(1)}, u32[]{:S(2)}, u32[]{:S(2)}) collective-permute-start(bf16[256,256]{1,0:T(8,128)(2,1)S(1)} %get-tuple-element.155.refs_1_), channel_id=1, source_target_pairs={{0,8},{2,10},{4,12},{6,14},{8,0},{10,2},{12,4},{14,6},{16,24},{18,... | collective-permute-start | bytes 393224 | tf_op jit(solution)/shard_map/ppermute | solution.py:21
  119.9 7.2 %collective-permute-start.55 = (bf16[256,256]{1,0:T(8,128)(2,1)S(1)}, bf16[256,256]{1,0:T(8,128)(2,1)S(1)}, u32[]{:S(2)}, u32[]{:S(2)}) collective-permute-start(bf16[256,256]{1,0:T(8,128)(2,1)S(1)} %get-tuple-element.155.refs_1_), channel_id=1, source_target_pairs={{0,4},{2,6},{4,0},{6,2},{8,12},{10,14},{12,8},{14,10},{16,20},{18,... | collective-permute-start | bytes 393224 | tf_op jit(solution)/shard_map/ppermute | solution.py:21
  122.0 6.8 %collective-permute-start.52 = (bf16[256,256]{1,0:T(8,128)(2,1)S(1)}, bf16[256,256]{1,0:T(8,128)(2,1)S(1)}, u32[]{:S(2)}, u32[]{:S(2)}) collective-permute-start(bf16[256,256]{1,0:T(8,128)(2,1)S(1)} %shard_map.68.refs_3_.refs_2_), channel_id=1, source_target_pairs={{0,2},{2,0},{4,6},{6,4},{8,10},{10,8},{12,14},{14,12},{16,18},{18,... | collective-permute-start | bytes 393224 | tf_op jit(solution)/shard_map/ppermute | solution.py:21
  128.1 6.5 %collective-permute-start.58 = (bf16[384,256]{1,0:T(8,128)(2,1)S(1)}, bf16[384,256]{1,0:T(8,128)(2,1)S(1)}, u32[]{:S(2)}, u32[]{:S(2)}) collective-permute-start(bf16[384,256]{1,0:T(8,128)(2,1)S(1)} %get-tuple-element.159), channel_id=1, source_target_pairs={{0,4},{2,6},{4,0},{6,2},{8,12},{10,14},{12,8},{14,10},{16,20},{18,... | collective-permute-start | bytes 589832 | tf_op jit(solution)/shard_map/ppermute | solution.py:21
  136.2 7.3 %collective-permute-start.62 = (bf16[256,256]{1,0:T(8,128)(2,1)S(1)}, bf16[256,256]{1,0:T(8,128)(2,1)S(1)}, u32[]{:S(2)}, u32[]{:S(2)}) collective-permute-start(bf16[256,256]{1,0:T(8,128)(2,1)S(1)} %get-tuple-element.161.refs_2_), channel_id=1, source_target_pairs={{0,16},{2,18},{4,20},{6,22},{8,24},{10,26},{12,28},{14,30},{16,0},... | collective-permute-start | bytes 393224 | tf_op jit(solution)/shard_map/ppermute | solution.py:21
  139.4 7.0 %collective-permute-start.59 = (bf16[1792,256]{1,0:T(8,128)(2,1)S(1)}, bf16[1792,256]{1,0:T(8,128)(2,1)S(1)}, u32[]{:S(2)}, u32[]{:S(2)}) collective-permute-start(bf16[1792,256]{1,0:T(8,128)(2,1)S(1)} %get-tuple-element.163.refs_0_), channel_id=1, source_target_pairs={{0,2},{2,0},{4,6},{6,4},{8,10},{10,8},{12,14},{14,12},{16,18},{18,... | collective-permute-start | bytes 2752520 | tf_op jit(solution)/shard_map/ppermute | solution.py:21
  143.7 7.2 %collective-permute-start.66 = (bf16[384,256]{1,0:T(8,128)(2,1)S(1)}, bf16[384,256]{1,0:T(8,128)(2,1)S(1)}, u32[]{:S(2)}, u32[]{:S(2)}) collective-permute-start(bf16[384,256]{1,0:T(8,128)(2,1)S(1)} %get-tuple-element.165.refs_5_), channel_id=1, source_target_pairs={{0,8},{2,10},{4,12},{6,14},{8,0},{10,2},{12,4},{14,6},{16,24},{18,... | collective-permute-start | bytes 589832 | tf_op jit(solution)/shard_map/ppermute | solution.py:21
  145.0 7.0 %collective-permute-start.67 = (bf16[384,256]{1,0:T(8,128)(2,1)S(1)}, bf16[384,256]{1,0:T(8,128)(2,1)S(1)}, u32[]{:S(2)}, u32[]{:S(2)}) collective-permute-start(bf16[384,256]{1,0:T(8,128)(2,1)S(1)} %get-tuple-element.168), channel_id=1, source_target_pairs={{0,4},{2,6},{4,0},{6,2},{8,12},{10,14},{12,8},{14,10},{16,20},{18,... | collective-permute-start | bytes 589832 | tf_op jit(solution)/shard_map/ppermute | solution.py:21
  152.8 11.6 %collective-permute-start.68 = (bf16[1792,256]{1,0:T(8,128)(2,1)S(1)}, bf16[1792,256]{1,0:T(8,128)(2,1)S(1)}, u32[]{:S(2)}, u32[]{:S(2)}) collective-permute-start(bf16[1792,256]{1,0:T(8,128)(2,1)S(1)} %get-tuple-element.169.refs_0_), channel_id=1, source_target_pairs={{0,2},{2,0},{4,6},{6,4},{8,10},{10,8},{12,14},{14,12},{16,18},{18,... | collective-permute-start | bytes 2752520 | tf_op jit(solution)/shard_map/ppermute | solution.py:21
  153.6 9.1 %collective-permute-start.71 = (bf16[256,256]{1,0:T(8,128)(2,1)S(1)}, bf16[256,256]{1,0:T(8,128)(2,1)S(1)}, u32[]{:S(2)}, u32[]{:S(2)}) collective-permute-start(bf16[256,256]{1,0:T(8,128)(2,1)S(1)} %get-tuple-element.171.refs_2_), channel_id=1, source_target_pairs={{0,16},{2,18},{4,20},{6,22},{8,24},{10,26},{12,28},{14,30},{16,0},... | collective-permute-start | bytes 393224 | tf_op jit(solution)/shard_map/ppermute | solution.py:21
  155.0 8.0 %collective-permute-start.72 = (bf16[256,256]{1,0:T(8,128)(2,1)S(1)}, bf16[256,256]{1,0:T(8,128)(2,1)S(1)}, u32[]{:S(2)}, u32[]{:S(2)}) collective-permute-start(bf16[256,256]{1,0:T(8,128)(2,1)S(1)} %get-tuple-element.171.refs_2_), channel_id=1, source_target_pairs={{0,8},{2,10},{4,12},{6,14},{8,0},{10,2},{12,4},{14,6},{16,24},{18,... | collective-permute-start | bytes 393224 | tf_op jit(solution)/shard_map/ppermute | solution.py:21
  155.6 7.3 %collective-permute-start.73 = (bf16[256,256]{1,0:T(8,128)(2,1)S(1)}, bf16[256,256]{1,0:T(8,128)(2,1)S(1)}, u32[]{:S(2)}, u32[]{:S(2)}) collective-permute-start(bf16[256,256]{1,0:T(8,128)(2,1)S(1)} %get-tuple-element.171.refs_2_), channel_id=1, source_target_pairs={{0,4},{2,6},{4,0},{6,2},{8,12},{10,14},{12,8},{14,10},{16,20},{18,... | collective-permute-start | bytes 393224 | tf_op jit(solution)/shard_map/ppermute | solution.py:21
  157.9 6.5 %collective-permute-start.70 = (bf16[256,256]{1,0:T(8,128)(2,1)S(1)}, bf16[256,256]{1,0:T(8,128)(2,1)S(1)}, u32[]{:S(2)}, u32[]{:S(2)}) collective-permute-start(bf16[256,256]{1,0:T(8,128)(2,1)S(1)} %shard_map.78.refs_3_.refs_2_), channel_id=1, source_target_pairs={{0,2},{2,0},{4,6},{6,4},{8,10},{10,8},{12,14},{14,12},{16,18},{18,... | collective-permute-start | bytes 393224 | tf_op jit(solution)/shard_map/ppermute | solution.py:21
  163.0 6.9 %collective-permute-start.75 = (bf16[384,256]{1,0:T(8,128)(2,1)S(1)}, bf16[384,256]{1,0:T(8,128)(2,1)S(1)}, u32[]{:S(2)}, u32[]{:S(2)}) collective-permute-start(bf16[384,256]{1,0:T(8,128)(2,1)S(1)} %get-tuple-element.172.refs_5_), channel_id=1, source_target_pairs={{0,8},{2,10},{4,12},{6,14},{8,0},{10,2},{12,4},{14,6},{16,24},{18,... | collective-permute-start | bytes 589832 | tf_op jit(solution)/shard_map/ppermute | solution.py:21
  163.5 6.5 %collective-permute-start.76 = (bf16[384,256]{1,0:T(8,128)(2,1)S(1)}, bf16[384,256]{1,0:T(8,128)(2,1)S(1)}, u32[]{:S(2)}, u32[]{:S(2)}) collective-permute-start(bf16[384,256]{1,0:T(8,128)(2,1)S(1)} %get-tuple-element.175), channel_id=1, source_target_pairs={{0,4},{2,6},{4,0},{6,2},{8,12},{10,14},{12,8},{14,10},{16,20},{18,... | collective-permute-start | bytes 589832 | tf_op jit(solution)/shard_map/ppermute | solution.py:21
  170.5 6.7 %collective-permute-start.78 = (bf16[256,256]{1,0:T(8,128)(2,1)S(1)}, bf16[256,256]{1,0:T(8,128)(2,1)S(1)}, u32[]{:S(2)}, u32[]{:S(2)}) collective-permute-start(bf16[256,256]{1,0:T(8,128)(2,1)S(1)} %get-tuple-element.177), channel_id=1, source_target_pairs={{0,4},{2,10},{4,0},{6,14},{8,12},{10,2},{12,8},{14,6},{16,20},{18,... | collective-permute-start | bytes 393224 | tf_op jit(solution)/shard_map/ppermute | solution.py:21
  173.4 8.0 %collective-permute-start.80 = (bf16[256,256]{1,0:T(8,128)(2,1)S(1)}, bf16[256,256]{1,0:T(8,128)(2,1)S(1)}, u32[]{:S(2)}, u32[]{:S(2)}) collective-permute-start(bf16[256,256]{1,0:T(8,128)(2,1)S(1)} %get-tuple-element.178.refs_1_), channel_id=1, source_target_pairs={{0,16},{2,18},{4,20},{6,22},{8,24},{10,26},{12,28},{14,30},{16,0},... | collective-permute-start | bytes 393224 | tf_op jit(solution)/shard_map/ppermute | solution.py:21
  189.4 12.6 %collective-permute-start.86 = (bf16[1792,256]{1,0:T(8,128)(2,1)S(1)}, bf16[1792,256]{1,0:T(8,128)(2,1)S(1)}, u32[]{:S(2)}, u32[]{:S(2)}) collective-permute-start(bf16[1792,256]{1,0:T(8,128)(2,1)S(1)} %get-tuple-element.185.refs_0_), channel_id=1, source_target_pairs={{0,2},{2,0},{4,6},{6,4},{8,10},{10,8},{12,14},{14,12},{16,18},{18,... | collective-permute-start | bytes 2752520 | tf_op jit(solution)/shard_map/ppermute | solution.py:21
  190.9 9.2 %collective-permute-start.89 = (bf16[256,256]{1,0:T(8,128)(2,1)S(1)}, bf16[256,256]{1,0:T(8,128)(2,1)S(1)}, u32[]{:S(2)}, u32[]{:S(2)}) collective-permute-start(bf16[256,256]{1,0:T(8,128)(2,1)S(1)} %get-tuple-element.187.refs_1_), channel_id=1, source_target_pairs={{0,16},{2,18},{4,20},{6,22},{8,24},{10,26},{12,28},{14,30},{16,0},... | collective-permute-start | bytes 393224 | tf_op jit(solution)/shard_map/ppermute | solution.py:21
  191.9 8.2 %collective-permute-start.90 = (bf16[256,256]{1,0:T(8,128)(2,1)S(1)}, bf16[256,256]{1,0:T(8,128)(2,1)S(1)}, u32[]{:S(2)}, u32[]{:S(2)}) collective-permute-start(bf16[256,256]{1,0:T(8,128)(2,1)S(1)} %get-tuple-element.187.refs_1_), channel_id=1, source_target_pairs={{0,8},{2,10},{4,12},{6,14},{8,0},{10,2},{12,4},{14,6},{16,24},{18,... | collective-permute-start | bytes 393224 | tf_op jit(solution)/shard_map/ppermute | solution.py:21
  193.3 6.9 %collective-permute-start.91 = (bf16[256,256]{1,0:T(8,128)(2,1)S(1)}, bf16[256,256]{1,0:T(8,128)(2,1)S(1)}, u32[]{:S(2)}, u32[]{:S(2)}) collective-permute-start(bf16[256,256]{1,0:T(8,128)(2,1)S(1)} %get-tuple-element.187.refs_1_), channel_id=1, source_target_pairs={{0,4},{2,6},{4,0},{6,2},{8,12},{10,14},{12,8},{14,10},{16,20},{18,... | collective-permute-start | bytes 393224 | tf_op jit(solution)/shard_map/ppermute | solution.py:21
  194.6 7.5 %collective-permute-start.88 = (bf16[256,256]{1,0:T(8,128)(2,1)S(1)}, bf16[256,256]{1,0:T(8,128)(2,1)S(1)}, u32[]{:S(2)}, u32[]{:S(2)}) collective-permute-start(bf16[256,256]{1,0:T(8,128)(2,1)S(1)} %shard_map.90.refs_3_.refs_2_), channel_id=1, source_target_pairs={{0,2},{2,0},{4,6},{6,4},{8,10},{10,8},{12,14},{14,12},{16,18},{18,... | collective-permute-start | bytes 393224 | tf_op jit(solution)/shard_map/ppermute | solution.py:21
  200.2 6.4 %collective-permute-start.93 = (bf16[384,256]{1,0:T(8,128)(2,1)S(1)}, bf16[384,256]{1,0:T(8,128)(2,1)S(1)}, u32[]{:S(2)}, u32[]{:S(2)}) collective-permute-start(bf16[384,256]{1,0:T(8,128)(2,1)S(1)} %get-tuple-element.188.refs_4_), channel_id=1, source_target_pairs={{0,8},{2,10},{4,12},{6,14},{8,0},{10,2},{12,4},{14,6},{16,24},{18,... | collective-permute-start | bytes 589832 | tf_op jit(solution)/shard_map/ppermute | solution.py:21
  209.2 7.3 %collective-permute-start.98 = (bf16[256,256]{1,0:T(8,128)(2,1)S(1)}, bf16[256,256]{1,0:T(8,128)(2,1)S(1)}, u32[]{:S(2)}, u32[]{:S(2)}) collective-permute-start(bf16[256,256]{1,0:T(8,128)(2,1)S(1)} %get-tuple-element.193.refs_2_), channel_id=1, source_target_pairs={{0,16},{2,18},{4,20},{6,22},{8,24},{10,26},{12,28},{14,30},{16,0},... | collective-permute-start | bytes 393224 | tf_op jit(solution)/shard_map/ppermute | solution.py:21
  216.6 7.4 %collective-permute-start.102 = (bf16[384,256]{1,0:T(8,128)(2,1)S(1)}, bf16[384,256]{1,0:T(8,128)(2,1)S(1)}, u32[]{:S(2)}, u32[]{:S(2)}) collective-permute-start(bf16[384,256]{1,0:T(8,128)(2,1)S(1)} %get-tuple-element.197.refs_5_), channel_id=1, source_target_pairs={{0,8},{2,10},{4,12},{6,14},{8,0},{10,2},{12,4},{14,6},{16,24},{18,... | collective-permute-start | bytes 589832 | tf_op jit(solution)/shard_map/ppermute | solution.py:21
  217.8 7.0 %collective-permute-start.103 = (bf16[384,256]{1,0:T(8,128)(2,1)S(1)}, bf16[384,256]{1,0:T(8,128)(2,1)S(1)}, u32[]{:S(2)}, u32[]{:S(2)}) collective-permute-start(bf16[384,256]{1,0:T(8,128)(2,1)S(1)} %get-tuple-element.200), channel_id=1, source_target_pairs={{0,4},{2,6},{4,0},{6,2},{8,12},{10,14},{12,8},{14,10},{16,20},{18,... | collective-permute-start | bytes 589832 | tf_op jit(solution)/shard_map/ppermute | solution.py:21
  225.2 12.5 %collective-permute-start.104 = (bf16[1792,256]{1,0:T(8,128)(2,1)S(1)}, bf16[1792,256]{1,0:T(8,128)(2,1)S(1)}, u32[]{:S(2)}, u32[]{:S(2)}) collective-permute-start(bf16[1792,256]{1,0:T(8,128)(2,1)S(1)} %get-tuple-element.201.refs_0_), channel_id=1, source_target_pairs={{0,2},{2,0},{4,6},{6,4},{8,10},{10,8},{12,14},{14,12},{16,18},{18,... | collective-permute-start | bytes 2752520 | tf_op jit(solution)/shard_map/ppermute | solution.py:21
  226.4 9.3 %collective-permute-start.107 = (bf16[256,256]{1,0:T(8,128)(2,1)S(1)}, bf16[256,256]{1,0:T(8,128)(2,1)S(1)}, u32[]{:S(2)}, u32[]{:S(2)}) collective-permute-start(bf16[256,256]{1,0:T(8,128)(2,1)S(1)} %get-tuple-element.203.refs_2_), channel_id=1, source_target_pairs={{0,16},{2,18},{4,20},{6,22},{8,24},{10,26},{12,28},{14,30},{16,0},... | collective-permute-start | bytes 393224 | tf_op jit(solution)/shard_map/ppermute | solution.py:21
  228.1 7.6 %collective-permute-start.108 = (bf16[256,256]{1,0:T(8,128)(2,1)S(1)}, bf16[256,256]{1,0:T(8,128)(2,1)S(1)}, u32[]{:S(2)}, u32[]{:S(2)}) collective-permute-start(bf16[256,256]{1,0:T(8,128)(2,1)S(1)} %get-tuple-element.203.refs_2_), channel_id=1, source_target_pairs={{0,8},{2,10},{4,12},{6,14},{8,0},{10,2},{12,4},{14,6},{16,24},{18,... | collective-permute-start | bytes 393224 | tf_op jit(solution)/shard_map/ppermute | solution.py:21
  229.2 6.5 %collective-permute-start.109 = (bf16[256,256]{1,0:T(8,128)(2,1)S(1)}, bf16[256,256]{1,0:T(8,128)(2,1)S(1)}, u32[]{:S(2)}, u32[]{:S(2)}) collective-permute-start(bf16[256,256]{1,0:T(8,128)(2,1)S(1)} %get-tuple-element.203.refs_2_), channel_id=1, source_target_pairs={{0,4},{2,6},{4,0},{6,2},{8,12},{10,14},{12,8},{14,10},{16,20},{18,... | collective-permute-start | bytes 393224 | tf_op jit(solution)/shard_map/ppermute | solution.py:21
  230.3 7.4 %collective-permute-start.106 = (bf16[256,256]{1,0:T(8,128)(2,1)S(1)}, bf16[256,256]{1,0:T(8,128)(2,1)S(1)}, u32[]{:S(2)}, u32[]{:S(2)}) collective-permute-start(bf16[256,256]{1,0:T(8,128)(2,1)S(1)} %shard_map.100.refs_3_.refs_2_), channel_id=1, source_target_pairs={{0,2},{2,0},{4,6},{6,4},{8,10},{10,8},{12,14},{14,12},{16,18},{18,... | collective-permute-start | bytes 393224 | tf_op jit(solution)/shard_map/ppermute | solution.py:21
  243.7 12.5 %collective-permute-start.113 = (bf16[1792,256]{1,0:T(8,128)(2,1)S(1)}, bf16[1792,256]{1,0:T(8,128)(2,1)S(1)}, u32[]{:S(2)}, u32[]{:S(2)}) collective-permute-start(bf16[1792,256]{1,0:T(8,128)(2,1)S(1)} %get-tuple-element.208.refs_0_), channel_id=1, source_target_pairs={{0,2},{2,0},{4,6},{6,4},{8,10},{10,8},{12,14},{14,12},{16,18},{18,... | collective-permute-start | bytes 2752520 | tf_op jit(solution)/shard_map/ppermute | solution.py:21
  244.9 9.2 %collective-permute-start.116 = (bf16[256,256]{1,0:T(8,128)(2,1)S(1)}, bf16[256,256]{1,0:T(8,128)(2,1)S(1)}, u32[]{:S(2)}, u32[]{:S(2)}) collective-permute-start(bf16[256,256]{1,0:T(8,128)(2,1)S(1)} %get-tuple-element.210.refs_1_), channel_id=1, source_target_pairs={{0,16},{2,18},{4,20},{6,22},{8,24},{10,26},{12,28},{14,30},{16,0},... | collective-permute-start | bytes 393224 | tf_op jit(solution)/shard_map/ppermute | solution.py:21
  246.6 7.5 %collective-permute-start.117 = (bf16[256,256]{1,0:T(8,128)(2,1)S(1)}, bf16[256,256]{1,0:T(8,128)(2,1)S(1)}, u32[]{:S(2)}, u32[]{:S(2)}) collective-permute-start(bf16[256,256]{1,0:T(8,128)(2,1)S(1)} %get-tuple-element.210.refs_1_), channel_id=1, source_target_pairs={{0,8},{2,10},{4,12},{6,14},{8,0},{10,2},{12,4},{14,6},{16,24},{18,... | collective-permute-start | bytes 393224 | tf_op jit(solution)/shard_map/ppermute | solution.py:21
  247.4 6.7 %collective-permute-start.118 = (bf16[256,256]{1,0:T(8,128)(2,1)S(1)}, bf16[256,256]{1,0:T(8,128)(2,1)S(1)}, u32[]{:S(2)}, u32[]{:S(2)}) collective-permute-start(bf16[256,256]{1,0:T(8,128)(2,1)S(1)} %get-tuple-element.210.refs_1_), channel_id=1, source_target_pairs={{0,4},{2,6},{4,0},{6,2},{8,12},{10,14},{12,8},{14,10},{16,20},{18,... | collective-permute-start | bytes 393224 | tf_op jit(solution)/shard_map/ppermute | solution.py:21
  248.9 7.3 %collective-permute-start.115 = (bf16[256,256]{1,0:T(8,128)(2,1)S(1)}, bf16[256,256]{1,0:T(8,128)(2,1)S(1)}, u32[]{:S(2)}, u32[]{:S(2)}) collective-permute-start(bf16[256,256]{1,0:T(8,128)(2,1)S(1)} %shard_map.105.refs_3_.refs_2_), channel_id=1, source_target_pairs={{0,2},{2,0},{4,6},{6,4},{8,10},{10,8},{12,14},{14,12},{16,18},{18,... | collective-permute-start | bytes 393224 | tf_op jit(solution)/shard_map/ppermute | solution.py:21
  262.8 6.4 %collective-permute-start.122 = (bf16[1792,256]{1,0:T(8,128)(2,1)S(1)}, bf16[1792,256]{1,0:T(8,128)(2,1)S(1)}, u32[]{:S(2)}, u32[]{:S(2)}) collective-permute-start(bf16[1792,256]{1,0:T(8,128)(2,1)S(1)} %get-tuple-element.216.refs_0_), channel_id=1, source_target_pairs={{0,2},{2,0},{4,6},{6,4},{8,10},{10,8},{12,14},{14,12},{16,18},{18,... | collective-permute-start | bytes 2752520 | tf_op jit(solution)/shard_map/ppermute | solution.py:21
  (63 other events, 340.4 us)
